TPU v7x, 256 devices: a whole 4x4x8 slice. The times are simulated.
256 devices in a mesh: pipe: 16 (over y, x_lo, core), fsdp: 8 (over z), tp: 2 (over x_hi).
Axes of the slice: x: 4 (x_hi: 2, x_lo: 2; x = x_hi * 2 + x_lo), y: 4, z: 8, core: 2. Of those that a mesh axis runs over, the one named last changes fastest.
Arguments:
- act_in: bfloat16 [16, 2, 8, 128, 4096], P('pipe', None, 'fsdp', None, 'tp'), may hold values from -6 to 6
- gate_q: bfloat16 [16, 2, 8, 128, 4096], P('pipe', None, 'fsdp', None, 'tp'), may hold values from -6 to 6
- gate_k: bfloat16 [16, 2, 8, 128, 4096], P('pipe', None, 'fsdp', None, 'tp'), may hold values from -6 to 6
- grad_in: bfloat16 [16, 8, 128, 4096], P('pipe', 'fsdp', None, 'tp'), may hold values from -6 to 6
- weight: bfloat16 [16, 4096, 4096], P('pipe', 'tp', 'fsdp'), may hold values from -0.09375 to 0.09375
- filters: bfloat16 [16, 128, 256], P('pipe', None, 'tp'), may hold values from -0.5 to 0.5
Outputs:
- grad_out: bfloat16 [16, 2, 8, 128, 4096], P('pipe', None, 'fsdp', None, 'tp')
- filter_grad: float32 [16, 128, 256], P('pipe', 'fsdp', 'tp')
All inputs are finite; a program needn't handle non-finite values.
Results may differ from a plain program's by a relative error of at most 0.0056.
Values may be sent and summed in bfloat16 or wider, within the bound.
No kernel may reach another device: no remote copies, remote signals or barrier semaphores. Data moves between devices by JAX's collectives and lax.ppermute only.
A program may use at most 128 MiB of HBM per device.

v0:
```python
import math

import jax
import jax.numpy as jnp
from jax import lax
from jax.sharding import PartitionSpec as P


def passed_along(value, axis, by):
    peers = lax.axis_size(axis)
    pairs = [(i, i + by) for i in range(peers) if 0 <= i + by < peers]
    return lax.ppermute(value, axis, pairs)


def toeplitz(taps_table, seqlen):
    rows = taps_table.T
    padded = jnp.pad(rows, ((0, 0), (0, 2 * seqlen - rows.shape[1])))
    tiled = jnp.tile(padded, (1, seqlen))
    cut = tiled[:, : seqlen * (2 * seqlen - 1)].reshape(rows.shape[0], seqlen, 2 * seqlen - 1)
    return cut[:, :, :seqlen]


def filter_terms(adjoint, shaped, taps):
    seqlen = adjoint.shape[0]
    groups_loc = adjoint.shape[1]
    flipped = jnp.pad(shaped[::-1], ((0, taps), (0, 0), (0, 0)))
    span = seqlen + taps
    block = math.gcd(groups_loc, 16)
    pieces = []
    for first in range(0, groups_loc, block):
        corr = jnp.einsum(
            "tgc,ugc->gtu",
            adjoint[:, first : first + block],
            flipped[:, first : first + block],
            preferred_element_type=jnp.float32,
        )
        flat = corr.reshape(block, seqlen * span)[:, : seqlen * (span - 1)]
        skewed = flat.reshape(block, seqlen, span - 1)[:, :, seqlen - 1 : seqlen - 1 + taps]
        pieces.append(jnp.sum(skewed, axis=1))
    return jnp.concatenate(pieces, axis=0).T


def body(act_in, gate_q, gate_k, grad_in, weight, filters):
    ticks = act_in.shape[1]
    seqlen = act_in.shape[3]
    width_loc = act_in.shape[4]
    taps = filters.shape[1]
    groups_loc = filters.shape[2]
    per_group = width_loc // groups_loc
    scale = 1.0 / math.sqrt(ticks * lax.axis_size("fsdp") * seqlen * per_group)
    kernel = toeplitz(filters[0], seqlen)
    contract = (((1,), (1,)), ((), ()))
    incoming = grad_in[0, 0]
    outputs = []
    pending = jnp.zeros((taps, groups_loc), jnp.float32)
    for tick in range(ticks):
        if tick > 0:
            incoming = passed_along(outputs[-1], "pipe", -1)
        whole = lax.all_gather(incoming, "tp", axis=1, tiled=True)

        def add_panel(total, piece, start, whole=whole):
            return lax.dot_general(whole, piece, contract, preferred_element_type=jnp.float32)

        deriv = add_panel(
            jnp.zeros((seqlen, width_loc), jnp.float32),
            lax.all_gather(weight[0], "fsdp", axis=1, tiled=True),
            jnp.int32(0),
        )
        adjoint = (
            (gate_q[0, tick, 0] * deriv).astype(jnp.bfloat16).reshape(seqlen, groups_loc, per_group)
        )
        back = jnp.einsum(
            "gtu,ugc->tgc", kernel, adjoint, preferred_element_type=jnp.float32
        ).reshape(seqlen, width_loc)
        result = (incoming + gate_k[0, tick, 0] * back).astype(jnp.bfloat16)
        outputs.append(result)
        shaped = (
            gate_k[0, tick, 0].astype(jnp.float32) * act_in[0, tick, 0].astype(jnp.float32)
        ).astype(jnp.bfloat16)
        term = filter_terms(adjoint, shaped.reshape(seqlen, groups_loc, per_group), taps) * scale
        pending = pending + term
    summed = lax.psum_scatter(pending, "fsdp", scatter_dimension=0, tiled=True)
    grads = jnp.stack(outputs, axis=0)[None, :, None]
    return (grads, summed[None])


def solution(mesh):
    placed = (
        P("pipe", None, "fsdp", None, "tp"),
        P("pipe", None, "fsdp", None, "tp"),
        P("pipe", None, "fsdp", None, "tp"),
        P("pipe", "fsdp", None, "tp"),
        P("pipe", "tp", "fsdp"),
        P("pipe", None, "tp"),
    )
    return jax.shard_map(
        body,
        mesh=mesh,
        in_specs=placed,
        out_specs=(P("pipe", None, "fsdp", None, "tp"), P("pipe", "fsdp", "tp")),
        check_vma=False,
    )
```

profile of v0, /device:TPU:16, one launch (start us, length us, event | category | flops | bytes accessed | tf_op | source)
XLA Modules:
  0.0 514.2 jit_solution(2104143820232488051)
XLA Ops:
  8.9 3.8 tile.4
  12.7 12.3 %copy.61 = bf16[16,8,128,256]{3,1,2,0:T(8,128)(2,1)} copy(bf16[16,8,128,256]{3,2,1,0:T(8,128)(2,1)} %bitcast.136) | data formatting | bytes 16777216
  25.0 7.3 %slice.290 = bf16[128,32640]{1,0:T(8,128)(2,1)} slice(bf16[128,32768]{1,0:T(8,128)(2,1)} %bitcast.137), slice={[0:128], [0:32640]} | slice | bytes 16711680 | tf_op jit(solution)/shard_map/slice | solution.py:19
  32.4 29.8 %reshape.184 = bf16[128,128,255]{2,1,0:T(8,128)(2,1)} reshape(bf16[128,32640]{1,0:T(8,128)(2,1)} %slice.290) | data formatting | bytes 16711680 | tf_op jit(solution)/shard_map/reshape | solution.py:19
  64.0 150.6 %all-gather.10.cloned.1.call-done = bf16[1,2048,4096]{2,1,0:T(8,128)(2,1)} async-done(((bf16[1,2048,512]{2,1,0:T(8,128)(2,1)}), bf16[1,2048,4096]{2,1,0:T(8,128)(2,1)}) %all-gather.10.cloned.1.call-update) | async-done | bytes 16777232 | tf_op jit(solution)/shard_map/all_gather | solution.py:66
  214.6 11.8 %fusion.17 = bf16[128,2048]{1,0:T(8,128)(2,1)S(1)} fusion(bf16[1,2048,4096]{2,1,0:T(8,128)(2,1)} %all-gather.10.cloned.1.call-done, bf16[1,1,128,4096]{3,2,1,0:T(8,128)(2,1)} %all-gather.8.cloned.1.call-done, bf16[1,2,1,128,2048]{4,3,2,1,0:T(8,128)(2,1)S(1)} %copy-done.9), kind=kOutput, calls=%fused_computation.11 | convolution fusion | flops 2148270080 | bytes 18874368 | tf_op jit(solution)/shard_map/dot_general | solution.py:62
  242.9 3.0 collective-permute-start
  248.6 6.2 %reshape.190 = f32[16,128,255]{2,1,0:T(8,128)} reshape(f32[16,32640]{1,0:T(8,128)} %slice.292) | data formatting | bytes 4177920 | tf_op jit(solution)/shard_map/reshape | solution.py:38
  256.8 2.8 copy.63
  261.1 6.1 %reshape.192 = f32[16,128,255]{2,1,0:T(8,128)} reshape(f32[16,32640]{1,0:T(8,128)} %slice.294) | data formatting | bytes 4177920 | tf_op jit(solution)/shard_map/reshape | solution.py:38
  269.2 2.8 copy.64
  273.4 6.1 %reshape.194 = f32[16,128,255]{2,1,0:T(8,128)} reshape(f32[16,32640]{1,0:T(8,128)} %slice.296) | data formatting | bytes 4177920 | tf_op jit(solution)/shard_map/reshape | solution.py:38
  281.5 3.2 copy.65
  286.2 6.1 %reshape.196 = f32[16,128,255]{2,1,0:T(8,128)} reshape(f32[16,32640]{1,0:T(8,128)} %slice.298) | data formatting | bytes 4177920 | tf_op jit(solution)/shard_map/reshape | solution.py:38
  298.5 6.3 %reshape.198 = f32[16,128,255]{2,1,0:T(8,128)} reshape(f32[16,32640]{1,0:T(8,128)} %slice.300) | data formatting | bytes 4177920 | tf_op jit(solution)/shard_map/reshape | solution.py:38
  311.0 6.1 %reshape.200 = f32[16,128,255]{2,1,0:T(8,128)} reshape(f32[16,32640]{1,0:T(8,128)} %slice.302) | data formatting | bytes 4177920 | tf_op jit(solution)/shard_map/reshape | solution.py:38
  327.1 6.2 %reshape.202 = f32[16,128,255]{2,1,0:T(8,128)} reshape(f32[16,32640]{1,0:T(8,128)} %slice.304) | data formatting | bytes 4177920 | tf_op jit(solution)/shard_map/reshape | solution.py:38
  333.3 2.9 copy.69
  337.6 6.1 %reshape.204 = f32[16,128,255]{2,1,0:T(8,128)} reshape(f32[16,32640]{1,0:T(8,128)} %slice.306) | data formatting | bytes 4177920 | tf_op jit(solution)/shard_map/reshape | solution.py:38
  350.1 12.0 %fusion.14 = bf16[128,2048]{1,0:T(8,128)(2,1)S(1)} fusion(bf16[128,4096]{1,0:T(8,128)(2,1)} %all-gather.6.cloned.1.call-done, bf16[1,2048,4096]{2,1,0:T(8,128)(2,1)} %all-gather.10.cloned.1.call-done, bf16[1,2,1,128,2048]{4,3,2,1,0:T(8,128)(2,1)} %param.7), kind=kOutput, calls=%fused_computation.10 | convolution fusion | flops 2148270080 | bytes 18874368 | tf_op jit(solution)/shard_map/dot_general | solution.py:62
  373.2 3.3 fusion.4
  379.3 6.2 %reshape.206 = f32[16,128,255]{2,1,0:T(8,128)} reshape(f32[16,32640]{1,0:T(8,128)} %slice.308) | data formatting | bytes 4177920 | tf_op jit(solution)/shard_map/reshape | solution.py:38
  391.7 6.1 %reshape.208 = f32[16,128,255]{2,1,0:T(8,128)} reshape(f32[16,32640]{1,0:T(8,128)} %slice.310) | data formatting | bytes 4177920 | tf_op jit(solution)/shard_map/reshape | solution.py:38
  399.8 3.2 copy.72
  404.5 6.2 %reshape.210 = f32[16,128,255]{2,1,0:T(8,128)} reshape(f32[16,32640]{1,0:T(8,128)} %slice.312) | data formatting | bytes 4177920 | tf_op jit(solution)/shard_map/reshape | solution.py:38
  416.8 6.2 %reshape.212 = f32[16,128,255]{2,1,0:T(8,128)} reshape(f32[16,32640]{1,0:T(8,128)} %slice.314) | data formatting | bytes 4177920 | tf_op jit(solution)/shard_map/reshape | solution.py:38
  429.2 6.2 %reshape.214 = f32[16,128,255]{2,1,0:T(8,128)} reshape(f32[16,32640]{1,0:T(8,128)} %slice.316) | data formatting | bytes 4177920 | tf_op jit(solution)/shard_map/reshape | solution.py:38
  437.3 3.0 copy.75
  441.8 6.2 %reshape.216 = f32[16,128,255]{2,1,0:T(8,128)} reshape(f32[16,32640]{1,0:T(8,128)} %slice.318) | data formatting | bytes 4177920 | tf_op jit(solution)/shard_map/reshape | solution.py:38
  454.1 6.2 %reshape.218 = f32[16,128,255]{2,1,0:T(8,128)} reshape(f32[16,32640]{1,0:T(8,128)} %slice.320) | data formatting | bytes 4177920 | tf_op jit(solution)/shard_map/reshape | solution.py:38
  463.7 4.6 reshape.220
  473.9 32.1 %reduce-scatter.4.cloned.1.call-done = f32[16,128]{1,0:T(8,128)} async-done(((f32[128,128]{1,0:T(8,128)}), f32[16,128]{1,0:T(8,128)}) %reduce-scatter.4.cloned.1.call-update) | async-done | bytes 8208
  (137 shorter events, 118.6 us)
Async XLA Ops:
  7.2 1.5 copy-start.10
  7.2 56.8 %all-gather.8.cloned.1.call-start = ((), (), s32[]{:S(2)}) async-start(), calls=%async_computation.2 | async-start | bytes 1572864 | tf_op jit(solution)/shard_map/all_gather | solution.py:59
  7.9 206.7 %all-gather.10.cloned.1.call-start = ((), (), s32[]{:S(2)}) async-start(), calls=%async_computation.3 | async-start | bytes 18874368 | tf_op jit(solution)/shard_map/all_gather | solution.py:66
  8.7 341.4 %all-gather.6.cloned.1.call-start = ((), (), s32[]{:S(2)}) async-start(), calls=%async_computation.1 | async-start | bytes 1572864 | tf_op jit(solution)/shard_map/all_gather | solution.py:59
  32.3 29.8 %copy-start.1 = (bf16[1,2,1,128,2048]{4,3,2,1,0:T(8,128)(2,1)S(1)}, bf16[1,2,1,128,2048]{4,3,2,1,0:T(8,128)(2,1)}, u32[]{:S(2)}) copy-start(bf16[1,2,1,128,2048]{4,3,2,1,0:T(8,128)(2,1)} %param.8) | copy-start | bytes 3145732
  32.4 29.8 %copy-start.8 = (bf16[1,2,1,128,2048]{4,3,2,1,0:T(8,128)(2,1)S(1)}, bf16[1,2,1,128,2048]{4,3,2,1,0:T(8,128)(2,1)}, u32[]{:S(2)}) copy-start(bf16[1,2,1,128,2048]{4,3,2,1,0:T(8,128)(2,1)} %param.6) | copy-start | bytes 3145732
  62.6 152.0 %copy-start.9 = (bf16[1,2,1,128,2048]{4,3,2,1,0:T(8,128)(2,1)S(1)}, bf16[1,2,1,128,2048]{4,3,2,1,0:T(8,128)(2,1)}, u32[]{:S(2)}) copy-start(bf16[1,2,1,128,2048]{4,3,2,1,0:T(8,128)(2,1)} %param.7) | copy-start | bytes 3145732
  226.6 10.2 %slice-start = ((s8[8388608]{0:T(1024)(128)(4,1)}), s8[4194304]{0:T(1024)(128)(4,1)S(1)}, s32[]{:S(2)}) async-start(s8[8388608]{0:T(1024)(128)(4,1)} %bitcast.132), calls=%async_computation.5 | async-start | bytes 8388608
  231.7 5.1 slice-start.1
  239.0 1.3 copy-start.4
  240.4 5.6 %copy-start = (f32[16,128,256]{2,1,0:T(8,128)S(1)}, f32[16,128,256]{2,1,0:T(8,128)}, u32[]{:S(2)}) copy-start(f32[16,128,256]{2,1,0:T(8,128)} %fusion.33) | copy-start | bytes 6291460
  242.9 79.6 %collective-permute-start = (bf16[128,2048]{1,0:T(8,128)(2,1)}, bf16[128,2048]{1,0:T(8,128)(2,1)}, u32[]{:S(2)}, u32[]{:S(2)}) collective-permute-start(bf16[128,2048]{1,0:T(8,128)(2,1)} %fusion.23), channel_id=1, source_target_pairs={{16,0},{32,16},{48,32},{64,48},{80,64},{96,80},{112,96},{128,112},... | collective-permute-start | bytes 1572872 | tf_op jit(solution)/shard_map/ppermute | solution.py:12
  322.6 183.4 %reduce-scatter.4.cloned.1.call-start = ((), (), s32[]{:S(2)}) async-start(), calls=%async_computation.4 | async-start | bytes 73728
  343.7 5.3 %copy-start.2 = (bf16[1,2,1,128,2048]{4,3,2,1,0:T(8,128)(2,1)S(1)}, bf16[1,2,1,128,2048]{4,3,2,1,0:T(8,128)(2,1)}, u32[]{:S(2)}) copy-start(bf16[1,2,1,128,2048]{4,3,2,1,0:T(8,128)(2,1)} %param.8) | copy-start | bytes 3145732
  345.0 4.0 copy-start.5
  364.4 8.8 %slice-start.2 = ((s8[8388608]{0:T(1024)(128)(4,1)}), s8[4194304]{0:T(1024)(128)(4,1)S(1)}, s32[]{:S(2)}) async-start(s8[8388608]{0:T(1024)(128)(4,1)} %bitcast.134), calls=%async_computation.7 | async-start | bytes 8388608
  369.4 3.8 slice-start.3
  463.6 7.5 %copy-start.6 = (f32[128,16,128]{2,1,0:T(8,128)S(1)}, f32[128,16,128]{2,1,0:T(8,128)}, u32[]{:S(2)}) copy-start(f32[128,16,128]{2,1,0:T(8,128)} %fusion.4) | copy-start | bytes 3145732
  468.2 3.2 copy-start.3
  471.5 1.3 copy-start.7
Sparse Core Ops, SparseCore 0:
  9.8 30.6 all-gather.7
  42.3 172.2 all-gather.9
  322.7 26.2 all-gather.5
  471.2 34.7 reduce-scatter.3
where the time goes:
time: 522 us; the launch traced here: 514 us
  local copies, waits for them, and re-layouts  221 us (42%)
  waiting for transfers between devices  184 us (35%)
  matrix products  53.6 us (10%)
  other arithmetic  37.5 us (7%)
  between operations  14.5 us (3%)
    all_gather x1, waiting for transfers between devices, body(): lax.all_gather(weight[0], 'fsdp', axis=1, tiled=True)  151 us
    reshape x16, local copies, waits for them, and re-layouts, filter_terms(): flat.reshape(block, seqlen, span - 1)[:, :, seqlen - 1:seqlen - 1 + taps]  97.1 us
    unnamed x65, local copies, waits for them, and re-layouts  55.9 us
    unnamed x5, waiting for transfers between devices  33.5 us
    reduce_sum x16, other arithmetic, filter_terms(): pieces.append(jnp.sum(skewed, axis=1))  31.1 us
    reshape x1, local copies, waits for them, and re-layouts, toeplitz(): tiled[:, :seqlen * (2 * seqlen - 1)]  29.8 us
    dot_general x16, matrix products, filter_terms(): jnp.einsum('tgc,ugc->gtu', adjoint[:, first:first + block], flipped[:, fi...  24.3 us
    dot_general x2, matrix products, add_panel(): lax.dot_general(whole, piece, contract, preferred_element_type=jnp.float32)  23.7 us
  transfers between devices with their start and end apart: 5, of which 2 were waited for; matrix products, arithmetic and copies ran while one was open for 31% of the time, Pallas kernels for 0%

commit v1 on v0

v1 whole, which is shorter than its diff:
```python
import functools
import math

import jax
import jax.numpy as jnp
from jax import lax
from jax.experimental import pallas as pl
from jax.experimental.pallas import tpu as pltpu
from jax.sharding import PartitionSpec as P

BLOCK = 512
VMEM = 40 * 1024 * 1024


def toeplitz_kernel(rows_ref, out_ref):
    groups, seqlen, _ = out_ref.shape
    u = lax.broadcasted_iota(jnp.int32, (seqlen, seqlen), 0)
    t = lax.broadcasted_iota(jnp.int32, (seqlen, seqlen), 1)
    for p in range(groups):
        wide = jnp.broadcast_to(rows_ref[p : p + 1, :], (seqlen, seqlen))
        rolled = pltpu.roll(wide, 1, 1, stride=1, stride_axis=0)
        out_ref[p] = jnp.where(u >= t, rolled, 0.0).astype(jnp.bfloat16)


def toeplitz(rows, step=16):
    groups, seqlen = rows.shape
    return pl.pallas_call(
        toeplitz_kernel,
        grid=(groups // step,),
        in_specs=[pl.BlockSpec((step, seqlen), lambda i: (i, 0))],
        out_specs=pl.BlockSpec((step, seqlen, seqlen), lambda i: (i, 0, 0)),
        out_shape=jax.ShapeDtypeStruct((groups, seqlen, seqlen), jnp.bfloat16),
        name="toeplitz",
    )(rows)


def prepare_kernel(per, act_ref, q_ref, k_ref, qt_ref, kt_ref, late_ref):
    _, seqlen, width = act_ref.shape
    row = lax.broadcasted_iota(jnp.int32, (seqlen, seqlen), 0)
    column = lax.broadcasted_iota(jnp.int32, (seqlen, seqlen), 1)
    flip = jnp.where(row + column == seqlen - 1, 1.0, 0.0).astype(jnp.bfloat16)
    for at in range(0, width, seqlen):
        here = slice(at, at + seqlen)
        qt_ref[here, :] = q_ref[0, :, here].T
        kt_ref[here, :] = k_ref[0, :, here].T
        shaped = (k_ref[0, :, here].astype(jnp.float32) * act_ref[0, :, here].astype(jnp.float32)).astype(jnp.bfloat16)
        late = jnp.dot(flip, shaped, preferred_element_type=jnp.float32).astype(jnp.bfloat16)
        for i in range(seqlen // per):
            late_ref[at // per + i] = late[:, i * per : (i + 1) * per]


def prepare(act, q, k, tick, per):
    _, seqlen, width = act.shape
    groups = width // per
    block = pl.BlockSpec((1, seqlen, width), lambda i: (tick, 0, 0))
    return pl.pallas_call(
        functools.partial(prepare_kernel, per),
        grid=(1,),
        in_specs=[block] * 3,
        out_specs=[whole_spec((width, seqlen))] * 2 + [whole_spec((groups, seqlen, per))],
        out_shape=[jax.ShapeDtypeStruct((width, seqlen), jnp.bfloat16)] * 2
        + [jax.ShapeDtypeStruct((groups, seqlen, per), jnp.bfloat16)],
        compiler_params=pltpu.CompilerParams(vmem_limit_bytes=VMEM),
        name="prepare",
    )(act, q, k)


def correlate(adj, late):
    corr = jnp.dot(late, adj, preferred_element_type=jnp.float32)
    rolled = pltpu.roll(corr, 1, 1, stride=1, stride_axis=0)
    r = lax.broadcasted_iota(jnp.int32, corr.shape, 0)
    lag = lax.broadcasted_iota(jnp.int32, corr.shape, 1)
    return jnp.sum(jnp.where(lag <= r, rolled, 0.0), axis=0, keepdims=True)


def project(offsets, place_ref, g_ref, w_refs, total=None):
    parts, depth, _ = g_ref.shape
    for (offset, first), w_ref in zip(offsets, w_refs):
        g = g_ref[lax.rem(place_ref[0] + (offset + parts), parts), first : first + w_ref.shape[1], :]
        part = jnp.dot(w_ref[...], g, preferred_element_type=jnp.float32)
        total = part if total is None else total + part
    return total


def shape_back(adj, own, k, toe_ref, out_ref, per):
    for p in range(toe_ref.shape[0]):
        at = slice(p * per, (p + 1) * per)
        back = jnp.dot(adj[at], toe_ref[p], preferred_element_type=jnp.float32)
        out_ref[at, :] = (own[at].astype(jnp.float32) + k[at].astype(jnp.float32) * back).astype(jnp.bfloat16)


def partial_kernel(offsets, place_ref, g_ref, *refs):
    count = len(offsets)
    w_refs, out_ref = refs[:count], refs[-1]
    total = refs[count][...] if len(refs) > count + 1 else None
    out_ref[...] = project(offsets, place_ref, g_ref, w_refs, total)


def first_kernel(offsets, per, place_ref, g_ref, *refs):
    count = len(offsets)
    w_refs = refs[:count]
    acc_ref, own_ref, q_ref, k_ref, toe_ref, out_ref, adj_ref = refs[count:]
    deriv = project(offsets, place_ref, g_ref, w_refs, acc_ref[...])
    adj = (q_ref[...].astype(jnp.float32) * deriv).astype(jnp.bfloat16)
    adj_ref[...] = adj
    shape_back(adj, own_ref[...], k_ref[...], toe_ref, out_ref, per)


def last_kernel(offsets, per, place_ref, own_ref, other_ref, *refs):
    count = len(offsets)
    w_refs = refs[:count]
    q_ref, late_ref, term_ref, _, adj_ref, sum_ref, g_ref, lag_ref = refs[count:]
    step = pl.program_id(0)
    parts = own_ref.shape[0]

    @pl.when(step == 0)
    def _():
        g_ref[pl.ds(place_ref[1] * parts, parts)] = own_ref[...]
        g_ref[pl.ds((1 - place_ref[1]) * parts, parts)] = other_ref[...]

    deriv = project(offsets, place_ref, g_ref, w_refs)
    adj = (q_ref[...].astype(jnp.float32) * deriv).astype(jnp.bfloat16)
    adj_ref[...] = adj
    groups = late_ref.shape[0]
    rows = [correlate(adj[p * per : (p + 1) * per], late_ref[p]) for p in range(groups)]
    for p in range(0, groups, 8):
        at = pl.ds(pl.multiple_of(step * groups + p, 8), 8)
        lag_ref[at, :] = term_ref[p : p + 8, :] + jnp.concatenate(rows[p : p + 8], axis=0)

    @pl.when(step == pl.num_programs(0) - 1)
    def _():
        sum_ref[...] = lag_ref[...].T


def lags_kernel(per, adj_ref, late_ref, out_ref):
    for p in range(out_ref.shape[0]):
        out_ref[p : p + 1, :] = correlate(adj_ref[p * per : (p + 1) * per, :], late_ref[p])


def turn_kernel(in_ref, out_ref):
    out_ref[0] = in_ref[...].T


def finish_kernel(per, adj_ref, own_ref, k_ref, toe_ref, held_ref, out_ref, back_ref):
    shape_back(adj_ref[...], own_ref[...], k_ref[...], toe_ref, back_ref, per)
    out_ref[0] = back_ref[...].T


def chan(seqlen):
    return pl.BlockSpec((BLOCK, seqlen), lambda i, *_: (i, 0))


def grouped(tail, per):
    return pl.BlockSpec((BLOCK // per, *tail), lambda i, *_: (i, *([0] * len(tail))))


def whole_spec(shape):
    return pl.BlockSpec(shape, lambda i, *_: (0,) * len(shape))


def call(kernel, place, gs, panels, rest, rest_specs, out_specs, out_shape, name, scratch=()):
    width = panels[0].shape[0]
    size = sum(p.size for p in panels)
    seqlen = gs[0].shape[2]
    return pl.pallas_call(
        kernel,
        grid_spec=pltpu.PrefetchScalarGridSpec(
            num_scalar_prefetch=1,
            grid=(width // BLOCK,),
            in_specs=[whole_spec(g.shape) for g in gs]
            + [pl.BlockSpec((BLOCK, p.shape[1]), lambda i, *_: (i, 0)) for p in panels]
            + rest_specs,
            out_specs=out_specs,
            scratch_shapes=list(scratch),
        ),
        out_shape=out_shape,
        compiler_params=pltpu.CompilerParams(vmem_limit_bytes=VMEM),
        cost_estimate=pl.CostEstimate(flops=2 * size * seqlen, bytes_accessed=2 * size, transcendentals=0),
        name=name,
    )(place, *gs, *panels, *rest)


def partial(place, g, offsets, panels, acc=None):
    seqlen = g.shape[2]
    rest = [] if acc is None else [acc]
    return call(
        functools.partial(partial_kernel, offsets), place, [g], panels, rest, [chan(seqlen)] * len(rest), chan(seqlen),
        jax.ShapeDtypeStruct((panels[0].shape[0], seqlen), jnp.float32), "partial_sums",
    )


def first_part(place, g, offsets, panels, acc, own, q, k, toe, per):
    seqlen = g.shape[2]
    at = chan(seqlen)
    return call(
        functools.partial(first_kernel, offsets, per), place, [g], panels, [acc, own, q, k, toe],
        [at, at, at, at, grouped(toe.shape[1:], per)], [at] * 2,
        [jax.ShapeDtypeStruct(own.shape, jnp.bfloat16)] * 2, "first_tick",
    )


def last_part(place, own, other, offsets, panels, q, late, term, ready, per):
    parts, depth, seqlen = own.shape
    at = chan(seqlen)
    groups = late.shape[0]
    return call(
        functools.partial(last_kernel, offsets, per), place, [own, other], panels, [q, late, term, ready],
        [at, grouped(late.shape[1:], per), grouped((seqlen,), per), pl.BlockSpec(memory_space=pl.ANY)], [at, whole_spec((seqlen, groups))],
        [jax.ShapeDtypeStruct(q.shape, jnp.bfloat16), jax.ShapeDtypeStruct((seqlen, groups), jnp.float32)],
        "last_tick",
        [pltpu.VMEM((2 * parts, depth, seqlen), jnp.bfloat16), pltpu.VMEM((groups, seqlen), jnp.float32)],
    )


def small_cost(width, seqlen):
    return pl.CostEstimate(flops=width * seqlen * seqlen * 8, bytes_accessed=8 * width * seqlen, transcendentals=0)


def lags(adj, late, per):
    width, seqlen = adj.shape
    return pl.pallas_call(
        functools.partial(lags_kernel, per),
        grid=(width // BLOCK,),
        in_specs=[chan(seqlen), grouped(late.shape[1:], per)],
        out_specs=grouped((seqlen,), per),
        out_shape=jax.ShapeDtypeStruct((width // per, seqlen), jnp.float32),
        compiler_params=pltpu.CompilerParams(vmem_limit_bytes=VMEM),
        cost_estimate=small_cost(width, seqlen),
        name="lags",
    )(adj, late)


def turn(value, ticks):
    width, seqlen = value.shape
    return pl.pallas_call(
        turn_kernel,
        grid=(width // BLOCK,),
        in_specs=[chan(seqlen)],
        out_specs=pl.BlockSpec((1, seqlen, BLOCK), lambda i: (0, 0, i)),
        out_shape=jax.ShapeDtypeStruct((ticks, seqlen, width), jnp.bfloat16),
        name="turn",
    )(value)


def finish(adj, own, k, toe, held, tick, per):
    width, seqlen = adj.shape
    return pl.pallas_call(
        functools.partial(finish_kernel, per),
        grid=(width // BLOCK,),
        in_specs=[chan(seqlen)] * 3 + [grouped(toe.shape[1:], per), pl.BlockSpec(memory_space=pl.ANY)],
        out_specs=pl.BlockSpec((1, seqlen, BLOCK), lambda i: (tick, 0, i)),
        out_shape=jax.ShapeDtypeStruct(held.shape, jnp.bfloat16),
        scratch_shapes=[pltpu.VMEM((BLOCK, seqlen), jnp.bfloat16)],
        input_output_aliases={4: 0},
        compiler_params=pltpu.CompilerParams(vmem_limit_bytes=VMEM),
        cost_estimate=small_cost(width, seqlen),
        name="finish",
    )(adj, own, k, toe, held)


def after_kernel(*refs):
    pass


def after(value, *others):
    anywhere = pl.BlockSpec(memory_space=pl.ANY)
    return pl.pallas_call(
        after_kernel,
        in_specs=[anywhere] * (1 + len(others)),
        out_specs=anywhere,
        out_shape=jax.ShapeDtypeStruct(value.shape, value.dtype),
        input_output_aliases={0: 0},
        name="after",
    )(value, *others)


def both_halves(own, other, rank):
    return jnp.concatenate([jnp.where(rank == 0, own, other), jnp.where(rank == 0, other, own)], axis=0)


def round_ring(value, by):
    peers = lax.axis_size("fsdp")
    return lax.ppermute(value, "fsdp", [(i, (i + by) % peers) for i in range(peers)])


def body(act_in, gate_q, gate_k, grad_in, weight, filters):
    ticks, _, seqlen, width = act_in.shape[1:]
    taps, groups = filters.shape[1:]
    per = width // groups
    depth = weight.shape[2]
    sections = lax.axis_size("pipe")
    scale = 1.0 / math.sqrt(ticks * lax.axis_size("fsdp") * seqlen * per)
    rank = lax.axis_index("tp")
    place = jnp.stack([lax.axis_index("fsdp"), rank])
    half = depth // 2
    panels = {(0, first): weight[0, :, first : first + half] for first in (0, half)}

    def circulate(step, first):
        if step < 4 or first == 0:
            panels[-step, first] = round_ring(panels[1 - step, first], 1)
        if step < 4 or first == half:
            panels[step, first] = round_ring(panels[step - 1, first], -1)

    circulate(1, 0)
    circulate(1, half)
    own = grad_in[0, 0].T
    other = lax.ppermute(own, "tp", [(0, 1), (1, 0)])
    acts, qs, ks = act_in[0, :, 0], gate_q[0, :, 0], gate_k[0, :, 0]
    ready = [prepare(acts, qs, ks, i, per) for i in range(ticks)]
    q, k, late = zip(*ready)
    toe = toeplitz(filters[0, ::-1].T.astype(jnp.float32))
    whole = both_halves(own, other, rank).reshape(-1, depth, seqlen)
    circulate(2, 0)
    circulate(2, half)
    panels[2, half] = after(panels[2, half], *ready[0], *ready[1], toe)
    for step in range(3, 5):
        for first in (0, half):
            circulate(step, first)

    def held(*steps):
        return [at for at in sorted(panels) if abs(at[0]) in steps]

    straight = [(s + 1, s) for s in range(sections - 1)]
    crossed = [((s + 1) * 2 + h, s * 2 + 1 - h) for s in range(sections - 1) for h in range(2)]
    acc = None
    for steps in ((0, 1), (2,), (3,)):
        near = held(*steps)
        acc = partial(place, whole, near, [panels[at] for at in near], acc)
    far = held(4)
    out, adj = first_part(place, whole, far, [panels[at] for at in far], acc, own, q[0], k[0], toe, per)
    own = lax.ppermute(out, "pipe", straight)
    other = lax.ppermute(out, ("pipe", "tp"), crossed)
    term = lags(adj, late[0], per)
    grads = turn(out, ticks)
    every = held(0, 1, 2, 3, 4)
    adj, total = last_part(
        place, own.reshape(-1, depth, seqlen), other.reshape(-1, depth, seqlen), every, [panels[at] for at in every],
        q[1], late[1], term, grads, per,
    )
    spread = lax.all_to_all(total.reshape(lax.axis_size("fsdp"), -1, groups), "fsdp", 0, 0, tiled=True)
    grads = finish(adj, own, k[1], toe, grads, 1, per)
    summed = jnp.sum(spread, axis=0) * scale
    return (grads[None, :, None], summed[None])


def solution(mesh):
    placed = (
        P("pipe", None, "fsdp", None, "tp"),
        P("pipe", None, "fsdp", None, "tp"),
        P("pipe", None, "fsdp", None, "tp"),
        P("pipe", "fsdp", None, "tp"),
        P("pipe", "tp", "fsdp"),
        P("pipe", None, "tp"),
    )
    return jax.shard_map(
        body,
        mesh=mesh,
        in_specs=placed,
        out_specs=(P("pipe", None, "fsdp", None, "tp"), P("pipe", "fsdp", "tp")),
        check_vma=False,
    )
```

time: 522 us -> 221 us (0.42); the launches traced: 514 us -> 219 us
  local copies, waits for them, and re-layouts: 221 us -> 21.5 us
  waiting for transfers between devices: 184 us -> 103 us
  matrix products: 53.6 us -> 0 us
  Pallas kernels: 0 us -> 49.1 us
  starting transfers between devices: 3.33 us -> 41.9 us
  other arithmetic: 37.5 us -> 2.5 us
  between operations: 14.5 us -> 0.95 us
    all_gather x3 -> x0, waiting for transfers between devices: 151 us -> none  [the longest x1 151 us: body(): lax.all_gather(weight[0], 'fsdp', axis=1, tiled=True)]
    reshape x20 -> x0, local copies, waits for them, and re-layouts: 130 us -> none  [the longest x16 97.1 us: filter_terms(): flat.reshape(block, seqlen, span - 1)[:, :, seqlen - 1:seqlen - 1 + taps]]
    ppermute x1 -> x17, waiting for transfers between devices: 0.01 us -> 100 us  [the longest x14 99.8 us: round_ring(): lax.ppermute(value, 'fsdp', [(i, (i + by) % peers) for i in range(peers)])]
    dot_general x20 -> x0, matrix products: 53.6 us -> none  [the longest x16 24.3 us: filter_terms(): jnp.einsum('tgc,ugc->gtu', adjoint[:, first:first + block], flipped[:, fi...]
    pallas_call x0 -> x12, Pallas kernels: none -> 49.1 us  [the longest x5 30 us: call(): pl.pallas_call(kernel, grid_spec=pltpu.PrefetchScalarGridSpec(num_scalar_...]
    unnamed x65 -> x68, local copies, waits for them, and re-layouts: 55.9 us -> 19.6 us
    unnamed x5 -> x0, waiting for transfers between devices: 33.5 us -> none
    ppermute x1 -> x17, starting transfers between devices: 3 us -> 36.1 us  [the longest x14 25.9 us: round_ring(): lax.ppermute(value, 'fsdp', [(i, (i + by) % peers) for i in range(peers)])]
  transfers between devices with their start and end apart: 5 -> 18, of which waited for: 2 -> 9; matrix products, arithmetic and copies ran while one was open for 31% -> 2% of each run, Pallas kernels for 0% -> 15%
where the time goes in v1:
time: 221 us; the launch traced here: 219 us
  waiting for transfers between devices  103 us (47%)
  Pallas kernels  49.1 us (22%)
  starting transfers between devices  41.9 us (19%)
  local copies, waits for them, and re-layouts  21.5 us (10%)
  other arithmetic  2.5 us (1%)
    ppermute x14, waiting for transfers between devices, round_ring(): lax.ppermute(value, 'fsdp', [(i, (i + by) % peers) for i in range(peers)])  99.8 us
    pallas_call x5, Pallas kernels, call(): pl.pallas_call(kernel, grid_spec=pltpu.PrefetchScalarGridSpec(num_scalar_...  30 us
    ppermute x14, starting transfers between devices, round_ring(): lax.ppermute(value, 'fsdp', [(i, (i + by) % peers) for i in range(peers)])  25.9 us
    unnamed x68, local copies, waits for them, and re-layouts  19.6 us
    all_to_all x1, starting transfers between devices, body(): lax.all_to_all(total.reshape(lax.axis_size('fsdp'), -1, groups), 'fsdp',...  5.85 us
    pallas_call x1, Pallas kernels, toeplitz(): pl.pallas_call(toeplitz_kernel, grid=(groups // step,), in_specs=[pl.Bloc...  5.44 us
    pallas_call x2, Pallas kernels, prepare(): pl.pallas_call(functools.partial(prepare_kernel, per), grid=(1,), in_spec...  4.57 us
  transfers between devices with their start and end apart: 18, of which 9 were waited for; matrix products, arithmetic and copies ran while one was open for 2% of the time, Pallas kernels for 15%

profile of v1, /device:TPU:16, one launch (start us, length us, event | category | flops | bytes accessed | tf_op | source)
XLA Modules:
  0.0 218.6 jit_solution(7927347092733228473)
XLA Ops:
  4.5 4.0 %collective-permute-start.5 = (bf16[2048,256]{1,0:T(8,128)(2,1)S(1)}, bf16[2048,256]{1,0:T(8,128)(2,1)}, u32[]{:S(2)}, u32[]{:S(2)}) collective-permute-start(bf16[2048,256]{1,0:T(8,128)(2,1)S(1)} %get-tuple-element.24.refs_3_.refs_8_), channel_id=1, source_target_pairs={{0,14},{2,0},{4,2},{6,4},{8,6},{10,8},{12,10},{14,12},{1,15},{3,1}... | collective-permute-start | bytes 3145736 | tf_op jit(solution)/shard_map/ppermute | solution.py:283
  8.5 3.2 %collective-permute-start.12 = (bf16[2048,256]{1,0:T(8,128)(2,1)S(1)}, bf16[2048,256]{1,0:T(8,128)(2,1)}, u32[]{:S(2)}, u32[]{:S(2)}) collective-permute-start(bf16[2048,256]{1,0:T(8,128)(2,1)S(1)} %get-tuple-element.25.refs_2_.refs_7_), channel_id=1, source_target_pairs={{0,14},{2,0},{4,2},{6,4},{8,6},{10,8},{12,10},{14,12},{1,15},{3,1}... | collective-permute-start | bytes 3145736 | tf_op jit(solution)/shard_map/ppermute | solution.py:283
  11.8 20.8 %collective-permute-done.1.refs_0_.refs_5_ = bf16[2048,256]{1,0:T(8,128)(2,1)} collective-permute-done((bf16[2048,256]{1,0:T(8,128)(2,1)S(1)}, bf16[2048,256]{1,0:T(8,128)(2,1)}, u32[]{:S(2)}, u32[]{:S(2)}) %collective-permute-start.1) | collective-permute-done | bytes 1048608 | tf_op jit(solution)/shard_map/ppermute | solution.py:283
  32.5 3.4 %collective-permute-start.6 = (bf16[2048,256]{1,0:T(8,128)(2,1)}, bf16[2048,256]{1,0:T(8,128)(2,1)S(1)}, u32[]{:S(2)}, u32[]{:S(2)}) collective-permute-start(bf16[2048,256]{1,0:T(8,128)(2,1)} %collective-permute-done.5.refs_5_.refs_10_), channel_id=1, source_target_pairs={{0,14},{2,0},{4,2},{6,4},{8,6},{10,8},{12,10},{14,12},{1,15},{3,1}... | collective-permute-start | bytes 3145736 | tf_op jit(solution)/shard_map/ppermute | solution.py:283
  35.9 2.3 %prepare.3 = (bf16[2048,128]{1,0:T(8,128)(2,1)S(1)}, bf16[2048,128]{1,0:T(8,128)(2,1)S(1)}, bf16[128,128,16]{2,1,0:T(8,128)(2,1)S(1)}) custom-call(bf16[2,128,2048]{2,1,0:T(8,128)(2,1)S(1)} %bitcast.34, bf16[2,128,2048]{2,1,0:T(8,128)(2,1)S(1)} %bitcast.36, bf16[2,128,2048]{2,1,0:T(8,128)(2,1)S(1)} %bitcast.38), custom_call_target="tpu_custom_call" | custom-call | tf_op jit(solution)/shard_map/prepare/pallas_call | solution.py:56
  41.8 2.3 %prepare.2 = (bf16[2048,128]{1,0:T(8,128)(2,1)S(1)}, bf16[2048,128]{1,0:T(8,128)(2,1)S(1)}, bf16[128,128,16]{2,1,0:T(8,128)(2,1)S(1)}) custom-call(bf16[2,128,2048]{2,1,0:T(8,128)(2,1)S(1)} %bitcast.35, bf16[2,128,2048]{2,1,0:T(8,128)(2,1)S(1)} %bitcast.37, bf16[2,128,2048]{2,1,0:T(8,128)(2,1)S(1)} %bitcast.39), custom_call_target="tpu_custom_call" | custom-call | tf_op jit(solution)/shard_map/prepare/pallas_call | solution.py:56
  44.1 2.1 copy-done.3
  48.6 5.4 %toeplitz.1.refs_7_.refs_6_.toe_ref = bf16[128,128,128]{2,1,0:T(8,128)(2,1)} custom-call(f32[128,128]{1,0:T(8,128)} %convert_bitcast_fusion.rows_ref), custom_call_target="tpu_custom_call" | custom-call | tf_op jit(solution)/shard_map/toeplitz/pallas_call | solution.py:27
  55.0 3.4 %collective-permute-start.13 = (bf16[2048,256]{1,0:T(8,128)(2,1)}, bf16[2048,256]{1,0:T(8,128)(2,1)}, u32[]{:S(2)}, u32[]{:S(2)}) collective-permute-start(bf16[2048,256]{1,0:T(8,128)(2,1)} %collective-permute-done.12.refs_4_.refs_9_), channel_id=1, source_target_pairs={{0,14},{2,0},{4,2},{6,4},{8,6},{10,8},{12,10},{14,12},{1,15},{3,1}... | collective-permute-start | bytes 3145736 | tf_op jit(solution)/shard_map/ppermute | solution.py:283
  58.3 19.1 %collective-permute-done.2.refs_0_.refs_3_ = bf16[2048,256]{1,0:T(8,128)(2,1)} collective-permute-done((bf16[2048,256]{1,0:T(8,128)(2,1)}, bf16[2048,256]{1,0:T(8,128)(2,1)}, u32[]{:S(2)}, u32[]{:S(2)}) %collective-permute-start.2) | collective-permute-done | bytes 1048608 | tf_op jit(solution)/shard_map/ppermute | solution.py:283
  78.4 3.2 %collective-permute-start.7 = (bf16[2048,256]{1,0:T(8,128)(2,1)}, bf16[2048,256]{1,0:T(8,128)(2,1)}, u32[]{:S(2)}, u32[]{:S(2)}) collective-permute-start(bf16[2048,256]{1,0:T(8,128)(2,1)} %after.1.refs_3_.refs_12_), channel_id=1, source_target_pairs={{0,14},{2,0},{4,2},{6,4},{8,6},{10,8},{12,10},{14,12},{1,15},{3,1}... | collective-permute-start | bytes 3145736 | tf_op jit(solution)/shard_map/ppermute | solution.py:283
  83.0 3.1 %collective-permute-start = (bf16[2048,128]{1,0:T(8,128)(2,1)S(1)}, bf16[2048,128]{1,0:T(8,128)(2,1)}, u32[]{:S(2)}, u32[]{:S(2)}) collective-permute-start(bf16[2048,128]{1,0:T(8,128)(2,1)S(1)} %bitcast.32), channel_id=1, source_target_pairs={{0,1},{1,0},{2,3},{3,2},{4,5},{5,4},{6,7},{7,6},{8,9},{9,8},{10,11... | collective-permute-start | bytes 1572872 | tf_op jit(solution)/shard_map/ppermute | solution.py:307
  86.2 13.7 %collective-permute-done.10.refs_1_.refs_4_ = bf16[2048,256]{1,0:T(8,128)(2,1)} collective-permute-done((bf16[2048,256]{1,0:T(8,128)(2,1)}, bf16[2048,256]{1,0:T(8,128)(2,1)}, u32[]{:S(2)}, u32[]{:S(2)}) %collective-permute-start.10) | collective-permute-done | bytes 1048608 | tf_op jit(solution)/shard_map/ppermute | solution.py:283
  99.9 3.4 %collective-permute-start.14 = (bf16[2048,256]{1,0:T(8,128)(2,1)}, bf16[2048,256]{1,0:T(8,128)(2,1)S(1)}, u32[]{:S(2)}, u32[]{:S(2)}) collective-permute-start(bf16[2048,256]{1,0:T(8,128)(2,1)} %collective-permute-done.13.refs_2_.refs_11_), channel_id=1, source_target_pairs={{0,14},{2,0},{4,2},{6,4},{8,6},{10,8},{12,10},{14,12},{1,15},{3,1}... | collective-permute-start | bytes 3145736 | tf_op jit(solution)/shard_map/ppermute | solution.py:283
  103.3 19.1 %collective-permute-done.3.refs_0_.refs_1_ = bf16[2048,256]{1,0:T(8,128)(2,1)} collective-permute-done((bf16[2048,256]{1,0:T(8,128)(2,1)}, bf16[2048,256]{1,0:T(8,128)(2,1)}, u32[]{:S(2)}, u32[]{:S(2)}) %collective-permute-start.3) | collective-permute-done | bytes 1048608 | tf_op jit(solution)/shard_map/ppermute | solution.py:283
  122.4 3.4 %collective-permute-start.8 = (bf16[2048,256]{1,0:T(8,128)(2,1)}, bf16[2048,256]{1,0:T(8,128)(2,1)S(1)}, u32[]{:S(2)}, u32[]{:S(2)}) collective-permute-start(bf16[2048,256]{1,0:T(8,128)(2,1)} %collective-permute-done.7.refs_3_.refs_14_), channel_id=1, source_target_pairs={{0,14},{2,0},{4,2},{6,4},{8,6},{10,8},{12,10},{14,12},{1,15},{3,1}... | collective-permute-start | bytes 3145736 | tf_op jit(solution)/shard_map/ppermute | solution.py:283
  127.0 4.8 %partial_sums.3.refs_4_ = f32[2048,128]{1,0:T(8,128)S(1)} custom-call(s32[2]{0:T(128)S(1)} %pad_add_fusion.place_ref, bf16[8,512,128]{2,1,0:T(8,128)(2,1)S(1)} %bitcast.28, bf16[2048,256]{1,0:T(8,128)(2,1)} %collective-permute-done.1.refs_0_.refs_5_, bf16[2048,256]{1,0:T(8,128)(2,1)} %collective-permute-done.9.refs_1_.refs_6_, ...), custom_call_target="tpu_custom_call" | custom-call | flops 805306368 | bytes 6291456 | tf_op jit(solution)/shard_map/partial_sums/pallas_call | solution.py:165
  131.8 4.2 %partial_sums.4.refs_4_ = f32[2048,128]{1,0:T(8,128)S(1)} custom-call(s32[2]{0:T(128)S(1)} %pad_add_fusion.place_ref, bf16[8,512,128]{2,1,0:T(8,128)(2,1)S(1)} %bitcast.29, bf16[2048,256]{1,0:T(8,128)(2,1)} %collective-permute-done.2.refs_0_.refs_3_, bf16[2048,256]{1,0:T(8,128)(2,1)} %collective-permute-done.10.refs_1_.refs_4_, ...), custom_call_target="tpu_custom_call" | custom-call | flops 536870912 | bytes 4194304 | tf_op jit(solution)/shard_map/partial_sums/pallas_call | solution.py:165
  136.1 8.7 %collective-permute-done.11.refs_1_.refs_2_ = bf16[2048,256]{1,0:T(8,128)(2,1)S(1)} collective-permute-done((bf16[2048,256]{1,0:T(8,128)(2,1)}, bf16[2048,256]{1,0:T(8,128)(2,1)S(1)}, u32[]{:S(2)}, u32[]{:S(2)}) %collective-permute-start.11) | collective-permute-done | bytes 1048608 | tf_op jit(solution)/shard_map/ppermute | solution.py:283
  144.8 4.2 %partial_sums.5.refs_2_ = f32[2048,128]{1,0:T(8,128)S(1)} custom-call(s32[2]{0:T(128)S(1)} %pad_add_fusion.place_ref, bf16[8,512,128]{2,1,0:T(8,128)(2,1)S(1)} %bitcast.30, bf16[2048,256]{1,0:T(8,128)(2,1)} %collective-permute-done.3.refs_0_.refs_1_, bf16[2048,256]{1,0:T(8,128)(2,1)S(1)} %collective-permute-done.11.refs_1_.refs_2_, ...), custom_call_target="tpu_custom_call" | custom-call | flops 536870912 | bytes 4194304 | tf_op jit(solution)/shard_map/partial_sums/pallas_call | solution.py:165
  149.0 17.4 %collective-permute-done.4.refs_0_ = bf16[2048,256]{1,0:T(8,128)(2,1)S(1)} collective-permute-done((bf16[2048,256]{1,0:T(8,128)(2,1)}, bf16[2048,256]{1,0:T(8,128)(2,1)S(1)}, u32[]{:S(2)}, u32[]{:S(2)}) %collective-permute-start.4) | collective-permute-done | bytes 1048608 | tf_op jit(solution)/shard_map/ppermute | solution.py:283
  166.5 4.4 %first_tick.1 = (bf16[2048,128]{1,0:T(8,128)(2,1)}, bf16[2048,128]{1,0:T(8,128)(2,1)S(1)}) custom-call(s32[2]{0:T(128)S(1)} %pad_add_fusion.place_ref, bf16[8,512,128]{2,1,0:T(8,128)(2,1)S(1)} %bitcast.31, bf16[2048,256]{1,0:T(8,128)(2,1)S(1)} %collective-permute-done.4.refs_0_, bf16[2048,256]{1,0:T(8,128)(2,1)S(1)} %collective-permute-done.8.refs_1_.refs_15_, ...), custom_call_target="tpu_custom_call" | custom-call | flops 268435456 | bytes 2097152 | tf_op jit(solution)/shard_map/first_tick/pallas_call | solution.py:165
  171.7 3.4 %collective-permute-start.16 = (bf16[2048,128]{1,0:T(8,128)(2,1)}, bf16[2048,128]{1,0:T(8,128)(2,1)S(1)}, u32[]{:S(2)}, u32[]{:S(2)}) collective-permute-start(bf16[2048,128]{1,0:T(8,128)(2,1)} %get-tuple-element.18.in_ref), channel_id=1, source_target_pairs={{16,1},{17,0},{32,17},{33,16},{48,33},{49,32},{64,49},{65,48},{80,... | collective-permute-start | bytes 1572872 | tf_op jit(solution)/shard_map/ppermute | solution.py:332
  175.2 3.6 %collective-permute-start.15 = (bf16[2048,128]{1,0:T(8,128)(2,1)}, bf16[2048,128]{1,0:T(8,128)(2,1)S(1)}, u32[]{:S(2)}, u32[]{:S(2)}) collective-permute-start(bf16[2048,128]{1,0:T(8,128)(2,1)} %get-tuple-element.18.in_ref), channel_id=1, source_target_pairs={{16,0},{32,16},{48,32},{64,48},{80,64},{96,80},{112,96},{128,112},... | collective-permute-start | bytes 1572872 | tf_op jit(solution)/shard_map/ppermute | solution.py:331
  178.8 3.3 %turn.1.refs_19_.held_ref = bf16[2,128,2048]{2,1,0:T(8,128)(2,1)} custom-call(bf16[2048,128]{1,0:T(8,128)(2,1)} %get-tuple-element.18.in_ref), custom_call_target="tpu_custom_call" | custom-call | tf_op jit(solution)/shard_map/turn/pallas_call | solution.py:235
  182.1 2.2 copy-done.4
  185.3 3.1 %lags.1.refs_18_ = f32[128,128]{1,0:T(8,128)S(1)} custom-call(bf16[2048,128]{1,0:T(8,128)(2,1)S(1)} %copy-done.29, bf16[128,128,16]{2,1,0:T(8,128)(2,1)S(1)} %copy-done.4), custom_call_target="tpu_custom_call" | custom-call | flops 268435456 | bytes 2097152 | tf_op jit(solution)/shard_map/lags/pallas_call | solution.py:221
  190.7 12.3 %last_tick.1 = (bf16[2048,128]{1,0:T(8,128)(2,1)S(1)}, f32[128,128]{1,0:T(8,128)}) custom-call(s32[2]{0:T(128)S(1)} %pad_add_fusion.place_ref, bf16[4,512,128]{2,1,0:T(8,128)(2,1)S(1)} %bitcast.40, bf16[4,512,128]{2,1,0:T(8,128)(2,1)S(1)} %bitcast.41, bf16[2048,256]{1,0:T(8,128)(2,1)S(1)} %copy-done.13, ...), custom_call_target="tpu_custom_call" | custom-call | flops 2147483648 | bytes 16777216 | tf_op jit(solution)/shard_map/last_tick/pallas_call | solution.py:165
  203.8 5.9 %all-to-all-start = ((f32[8,16,128]{2,1,0:T(8,128)}), f32[8,16,128]{2,1,0:T(8,128)S(1)}, u32[]{:S(2)}, u32[]{:S(2)}) async-start(f32[8,16,128]{2,1,0:T(8,128)} %bitcast.17), calls=%async_computation | async-start | bytes 131072 | tf_op jit(solution)/shard_map/all_to_all | solution.py:340
  209.6 2.2 copy-done.1
  212.9 2.7 %finish.1 = bf16[2,128,2048]{2,1,0:T(8,128)(2,1)} custom-call(bf16[2048,128]{1,0:T(8,128)(2,1)S(1)} %copy-done.31, bf16[2048,128]{1,0:T(8,128)(2,1)S(1)} %collective-permute-done.15.own_ref, bf16[2048,128]{1,0:T(8,128)(2,1)S(1)} %copy-done.25, bf16[128,128,128]{2,1,0:T(8,128)(2,1)S(1)} %copy-done.1, ...), custom_call_target="tpu_custom_call", output_to_operand_aliasing={{}: (4, {})} | custom-call | flops 268435456 | bytes 2097152 | tf_op jit(solution)/shard_map/finish/pallas_call | solution.py:247
  215.6 2.4 %all-to-all-done = f32[8,16,128]{2,1,0:T(8,128)S(1)} async-done(((f32[8,16,128]{2,1,0:T(8,128)}), f32[8,16,128]{2,1,0:T(8,128)S(1)}, u32[]{:S(2)}, u32[]{:S(2)}) %all-to-all-start) | async-done | bytes 65568 | tf_op jit(solution)/shard_map/all_to_all | solution.py:340
  (92 shorter events, 21.0 us)
Async XLA Ops:
  0.6 35.2 %copy-start.11 = (bf16[1,2,1,128,2048]{4,3,2,1,0:T(8,128)(2,1)S(1)}, bf16[1,2,1,128,2048]{4,3,2,1,0:T(8,128)(2,1)}, u32[]{:S(2)}) copy-start(bf16[1,2,1,128,2048]{4,3,2,1,0:T(8,128)(2,1)} %param.8) | copy-start | bytes 3145732
  0.6 35.2 %copy-start.10 = (bf16[1,2,1,128,2048]{4,3,2,1,0:T(8,128)(2,1)S(1)}, bf16[1,2,1,128,2048]{4,3,2,1,0:T(8,128)(2,1)}, u32[]{:S(2)}) copy-start(bf16[1,2,1,128,2048]{4,3,2,1,0:T(8,128)(2,1)} %param.7) | copy-start | bytes 3145732
  0.7 35.2 %copy-start.9 = (bf16[1,2,1,128,2048]{4,3,2,1,0:T(8,128)(2,1)S(1)}, bf16[1,2,1,128,2048]{4,3,2,1,0:T(8,128)(2,1)}, u32[]{:S(2)}) copy-start(bf16[1,2,1,128,2048]{4,3,2,1,0:T(8,128)(2,1)} %param.6) | copy-start | bytes 3145732
  2.5 30.0 %collective-permute-start.1 = (bf16[2048,256]{1,0:T(8,128)(2,1)S(1)}, bf16[2048,256]{1,0:T(8,128)(2,1)}, u32[]{:S(2)}, u32[]{:S(2)}) collective-permute-start(bf16[2048,256]{1,0:T(8,128)(2,1)S(1)} %get-tuple-element.25.refs_2_.refs_7_), channel_id=1, source_target_pairs={{0,2},{2,4},{4,6},{6,8},{8,10},{10,12},{12,14},{14,0},{1,3},{3,5},... | collective-permute-start | bytes 3145736 | tf_op jit(solution)/shard_map/ppermute | solution.py:283
  4.5 28.0 %collective-permute-start.5 = (bf16[2048,256]{1,0:T(8,128)(2,1)S(1)}, bf16[2048,256]{1,0:T(8,128)(2,1)}, u32[]{:S(2)}, u32[]{:S(2)}) collective-permute-start(bf16[2048,256]{1,0:T(8,128)(2,1)S(1)} %get-tuple-element.24.refs_3_.refs_8_), channel_id=1, source_target_pairs={{0,14},{2,0},{4,2},{6,4},{8,6},{10,8},{12,10},{14,12},{1,15},{3,1}... | collective-permute-start | bytes 3145736 | tf_op jit(solution)/shard_map/ppermute | solution.py:283
  8.5 46.5 %collective-permute-start.9 = (bf16[2048,256]{1,0:T(8,128)(2,1)S(1)}, bf16[2048,256]{1,0:T(8,128)(2,1)}, u32[]{:S(2)}, u32[]{:S(2)}) collective-permute-start(bf16[2048,256]{1,0:T(8,128)(2,1)S(1)} %get-tuple-element.24.refs_3_.refs_8_), channel_id=1, source_target_pairs={{0,2},{2,4},{4,6},{6,8},{8,10},{10,12},{12,14},{14,0},{1,3},{3,5},... | collective-permute-start | bytes 3145736 | tf_op jit(solution)/shard_map/ppermute | solution.py:283
  8.5 46.5 %collective-permute-start.12 = (bf16[2048,256]{1,0:T(8,128)(2,1)S(1)}, bf16[2048,256]{1,0:T(8,128)(2,1)}, u32[]{:S(2)}, u32[]{:S(2)}) collective-permute-start(bf16[2048,256]{1,0:T(8,128)(2,1)S(1)} %get-tuple-element.25.refs_2_.refs_7_), channel_id=1, source_target_pairs={{0,14},{2,0},{4,2},{6,4},{8,6},{10,8},{12,10},{14,12},{1,15},{3,1}... | collective-permute-start | bytes 3145736 | tf_op jit(solution)/shard_map/ppermute | solution.py:283
  32.5 44.9 %collective-permute-start.2 = (bf16[2048,256]{1,0:T(8,128)(2,1)}, bf16[2048,256]{1,0:T(8,128)(2,1)}, u32[]{:S(2)}, u32[]{:S(2)}) collective-permute-start(bf16[2048,256]{1,0:T(8,128)(2,1)} %collective-permute-done.1.refs_0_.refs_5_), channel_id=1, source_target_pairs={{0,2},{2,4},{4,6},{6,8},{8,10},{10,12},{12,14},{14,0},{1,3},{3,5},... | collective-permute-start | bytes 3145736 | tf_op jit(solution)/shard_map/ppermute | solution.py:283
  32.5 44.9 %collective-permute-start.6 = (bf16[2048,256]{1,0:T(8,128)(2,1)}, bf16[2048,256]{1,0:T(8,128)(2,1)S(1)}, u32[]{:S(2)}, u32[]{:S(2)}) collective-permute-start(bf16[2048,256]{1,0:T(8,128)(2,1)} %collective-permute-done.5.refs_5_.refs_10_), channel_id=1, source_target_pairs={{0,14},{2,0},{4,2},{6,4},{8,6},{10,8},{12,10},{14,12},{1,15},{3,1}... | collective-permute-start | bytes 3145736 | tf_op jit(solution)/shard_map/ppermute | solution.py:283
  41.8 6.0 %copy-start.32 = (bf16[1,128,128]{2,1,0:T(8,128)(2,1)S(1)}, bf16[1,128,128]{2,1,0:T(8,128)(2,1)}, u32[]{:S(2)}) copy-start(bf16[1,128,128]{2,1,0:T(8,128)(2,1)} %param.11) | copy-start | bytes 98308
  55.0 44.9 %collective-permute-start.10 = (bf16[2048,256]{1,0:T(8,128)(2,1)}, bf16[2048,256]{1,0:T(8,128)(2,1)}, u32[]{:S(2)}, u32[]{:S(2)}) collective-permute-start(bf16[2048,256]{1,0:T(8,128)(2,1)} %collective-permute-done.9.refs_1_.refs_6_), channel_id=1, source_target_pairs={{0,2},{2,4},{4,6},{6,8},{8,10},{10,12},{12,14},{14,0},{1,3},{3,5},... | collective-permute-start | bytes 3145736 | tf_op jit(solution)/shard_map/ppermute | solution.py:283
  55.0 44.9 %collective-permute-start.13 = (bf16[2048,256]{1,0:T(8,128)(2,1)}, bf16[2048,256]{1,0:T(8,128)(2,1)}, u32[]{:S(2)}, u32[]{:S(2)}) collective-permute-start(bf16[2048,256]{1,0:T(8,128)(2,1)} %collective-permute-done.12.refs_4_.refs_9_), channel_id=1, source_target_pairs={{0,14},{2,0},{4,2},{6,4},{8,6},{10,8},{12,10},{14,12},{1,15},{3,1}... | collective-permute-start | bytes 3145736 | tf_op jit(solution)/shard_map/ppermute | solution.py:283
  77.5 44.9 %collective-permute-start.3 = (bf16[2048,256]{1,0:T(8,128)(2,1)}, bf16[2048,256]{1,0:T(8,128)(2,1)}, u32[]{:S(2)}, u32[]{:S(2)}) collective-permute-start(bf16[2048,256]{1,0:T(8,128)(2,1)} %collective-permute-done.2.refs_0_.refs_3_), channel_id=1, source_target_pairs={{0,2},{2,4},{4,6},{6,8},{8,10},{10,12},{12,14},{14,0},{1,3},{3,5},... | collective-permute-start | bytes 3145736 | tf_op jit(solution)/shard_map/ppermute | solution.py:283
  78.4 44.0 %collective-permute-start.7 = (bf16[2048,256]{1,0:T(8,128)(2,1)}, bf16[2048,256]{1,0:T(8,128)(2,1)}, u32[]{:S(2)}, u32[]{:S(2)}) collective-permute-start(bf16[2048,256]{1,0:T(8,128)(2,1)} %after.1.refs_3_.refs_12_), channel_id=1, source_target_pairs={{0,14},{2,0},{4,2},{6,4},{8,6},{10,8},{12,10},{14,12},{1,15},{3,1}... | collective-permute-start | bytes 3145736 | tf_op jit(solution)/shard_map/ppermute | solution.py:283
  83.0 44.0 %copy-start.7 = (bf16[1,1,128,2048]{2,3,1,0:T(8,128)(2,1)}, bf16[1,1,128,2048]{2,3,1,0:T(8,128)(2,1)S(1)}, u32[]{:S(2)}) copy-start(bf16[1,1,128,2048]{2,3,1,0:T(8,128)(2,1)S(1)} %copy.10) | copy-start | bytes 1572868
  83.0 42.7 %collective-permute-start = (bf16[2048,128]{1,0:T(8,128)(2,1)S(1)}, bf16[2048,128]{1,0:T(8,128)(2,1)}, u32[]{:S(2)}, u32[]{:S(2)}) collective-permute-start(bf16[2048,128]{1,0:T(8,128)(2,1)S(1)} %bitcast.32), channel_id=1, source_target_pairs={{0,1},{1,0},{2,3},{3,2},{4,5},{5,4},{6,7},{7,6},{8,9},{9,8},{10,11... | collective-permute-start | bytes 1572872 | tf_op jit(solution)/shard_map/ppermute | solution.py:307
  99.9 44.8 %collective-permute-start.11 = (bf16[2048,256]{1,0:T(8,128)(2,1)}, bf16[2048,256]{1,0:T(8,128)(2,1)S(1)}, u32[]{:S(2)}, u32[]{:S(2)}) collective-permute-start(bf16[2048,256]{1,0:T(8,128)(2,1)} %collective-permute-done.10.refs_1_.refs_4_), channel_id=1, source_target_pairs={{0,2},{2,4},{4,6},{6,8},{8,10},{10,12},{12,14},{14,0},{1,3},{3,5},... | collective-permute-start | bytes 3145736 | tf_op jit(solution)/shard_map/ppermute | solution.py:283
  99.9 44.8 %collective-permute-start.14 = (bf16[2048,256]{1,0:T(8,128)(2,1)}, bf16[2048,256]{1,0:T(8,128)(2,1)S(1)}, u32[]{:S(2)}, u32[]{:S(2)}) collective-permute-start(bf16[2048,256]{1,0:T(8,128)(2,1)} %collective-permute-done.13.refs_2_.refs_11_), channel_id=1, source_target_pairs={{0,14},{2,0},{4,2},{6,4},{8,6},{10,8},{12,10},{14,12},{1,15},{3,1}... | collective-permute-start | bytes 3145736 | tf_op jit(solution)/shard_map/ppermute | solution.py:283
  122.4 44.0 %collective-permute-start.4 = (bf16[2048,256]{1,0:T(8,128)(2,1)}, bf16[2048,256]{1,0:T(8,128)(2,1)S(1)}, u32[]{:S(2)}, u32[]{:S(2)}) collective-permute-start(bf16[2048,256]{1,0:T(8,128)(2,1)} %collective-permute-done.3.refs_0_.refs_1_), channel_id=1, source_target_pairs={{0,2},{2,4},{4,6},{6,8},{8,10},{10,12},{12,14},{14,0},{1,3},{3,5},... | collective-permute-start | bytes 3145736 | tf_op jit(solution)/shard_map/ppermute | solution.py:283
  122.4 44.0 %collective-permute-start.8 = (bf16[2048,256]{1,0:T(8,128)(2,1)}, bf16[2048,256]{1,0:T(8,128)(2,1)S(1)}, u32[]{:S(2)}, u32[]{:S(2)}) collective-permute-start(bf16[2048,256]{1,0:T(8,128)(2,1)} %collective-permute-done.7.refs_3_.refs_14_), channel_id=1, source_target_pairs={{0,14},{2,0},{4,2},{6,4},{8,6},{10,8},{12,10},{14,12},{1,15},{3,1}... | collective-permute-start | bytes 3145736 | tf_op jit(solution)/shard_map/ppermute | solution.py:283
  127.0 4.8 %copy-start.6 = (bf16[2048,256]{1,0:T(8,128)(2,1)S(1)}, bf16[2048,256]{1,0:T(8,128)(2,1)}, u32[]{:S(2)}) copy-start(bf16[2048,256]{1,0:T(8,128)(2,1)} %after.1.refs_3_.refs_12_) | copy-start | bytes 3145732
  136.0 30.4 %copy-start = (bf16[128,128,128]{2,1,0:T(8,128)(2,1)S(1)}, bf16[128,128,128]{2,1,0:T(8,128)(2,1)}, u32[]{:S(2)}) copy-start(bf16[128,128,128]{2,1,0:T(8,128)(2,1)} %toeplitz.1.refs_7_.refs_6_.toe_ref) | copy-start | bytes 12582916
  136.0 30.4 %copy-start.8 = (bf16[1,1,128,2048]{2,3,1,0:T(8,128)(2,1)S(1)}, bf16[1,1,128,2048]{2,3,1,0:T(8,128)(2,1)}, u32[]{:S(2)}) copy-start(bf16[1,1,128,2048]{2,3,1,0:T(8,128)(2,1)} %copy-done.7) | copy-start | bytes 1572868
  136.0 30.4 %copy-start.21 = (bf16[2048,128]{1,0:T(8,128)(2,1)S(1)}, bf16[2048,128]{1,0:T(8,128)(2,1)}, u32[]{:S(2)}) copy-start(bf16[2048,128]{1,0:T(8,128)(2,1)} %copy-done.20) | copy-start | bytes 1572868
  136.1 30.4 %copy-start.23 = (bf16[2048,128]{1,0:T(8,128)(2,1)S(1)}, bf16[2048,128]{1,0:T(8,128)(2,1)}, u32[]{:S(2)}) copy-start(bf16[2048,128]{1,0:T(8,128)(2,1)} %copy-done.22) | copy-start | bytes 1572868
  166.4 4.5 %copy-start.12 = (bf16[2048,256]{1,0:T(8,128)(2,1)}, bf16[2048,256]{1,0:T(8,128)(2,1)S(1)}, u32[]{:S(2)}) copy-start(bf16[2048,256]{1,0:T(8,128)(2,1)S(1)} %collective-permute-done.4.refs_0_) | copy-start | bytes 3145732
  166.4 4.4 %copy-start.14 = (bf16[2048,256]{1,0:T(8,128)(2,1)}, bf16[2048,256]{1,0:T(8,128)(2,1)S(1)}, u32[]{:S(2)}) copy-start(bf16[2048,256]{1,0:T(8,128)(2,1)S(1)} %collective-permute-done.8.refs_1_.refs_15_) | copy-start | bytes 3145732
  171.7 17.1 %collective-permute-start.16 = (bf16[2048,128]{1,0:T(8,128)(2,1)}, bf16[2048,128]{1,0:T(8,128)(2,1)S(1)}, u32[]{:S(2)}, u32[]{:S(2)}) collective-permute-start(bf16[2048,128]{1,0:T(8,128)(2,1)} %get-tuple-element.18.in_ref), channel_id=1, source_target_pairs={{16,1},{17,0},{32,17},{33,16},{48,33},{49,32},{64,49},{65,48},{80,... | collective-permute-start | bytes 1572872 | tf_op jit(solution)/shard_map/ppermute | solution.py:332
  175.2 14.4 %collective-permute-start.15 = (bf16[2048,128]{1,0:T(8,128)(2,1)}, bf16[2048,128]{1,0:T(8,128)(2,1)S(1)}, u32[]{:S(2)}, u32[]{:S(2)}) collective-permute-start(bf16[2048,128]{1,0:T(8,128)(2,1)} %get-tuple-element.18.in_ref), channel_id=1, source_target_pairs={{16,0},{32,16},{48,32},{64,48},{80,64},{96,80},{112,96},{128,112},... | collective-permute-start | bytes 1572872 | tf_op jit(solution)/shard_map/ppermute | solution.py:331
  185.3 4.3 %copy-start.19 = (bf16[2048,128]{1,0:T(8,128)(2,1)S(1)}, bf16[2048,128]{1,0:T(8,128)(2,1)}, u32[]{:S(2)}) copy-start(bf16[2048,128]{1,0:T(8,128)(2,1)} %copy-done.18) | copy-start | bytes 1572868
  190.7 19.0 %copy-start.25 = (bf16[2048,128]{1,0:T(8,128)(2,1)S(1)}, bf16[2048,128]{1,0:T(8,128)(2,1)}, u32[]{:S(2)}) copy-start(bf16[2048,128]{1,0:T(8,128)(2,1)} %copy-done.24) | copy-start | bytes 1572868
  203.8 14.2 %all-to-all-start = ((f32[8,16,128]{2,1,0:T(8,128)}), f32[8,16,128]{2,1,0:T(8,128)S(1)}, u32[]{:S(2)}, u32[]{:S(2)}) async-start(f32[8,16,128]{2,1,0:T(8,128)} %bitcast.17), calls=%async_computation | async-start | bytes 131072 | tf_op jit(solution)/shard_map/all_to_all | solution.py:340
  (19 other events, 35.1 us)

commit v2 on v1

--- a/solution.py
+++ b/solution.py
@@ -34,7 +34,7 @@
     )(rows)
 
 
-def prepare_kernel(per, act_ref, q_ref, k_ref, qt_ref, kt_ref, late_ref):
+def prepare_kernel(act_ref, q_ref, k_ref, qt_ref, kt_ref, late_ref):
     _, seqlen, width = act_ref.shape
     row = lax.broadcasted_iota(jnp.int32, (seqlen, seqlen), 0)
     column = lax.broadcasted_iota(jnp.int32, (seqlen, seqlen), 1)
@@ -44,33 +44,38 @@
         qt_ref[here, :] = q_ref[0, :, here].T
         kt_ref[here, :] = k_ref[0, :, here].T
         shaped = (k_ref[0, :, here].astype(jnp.float32) * act_ref[0, :, here].astype(jnp.float32)).astype(jnp.bfloat16)
-        late = jnp.dot(flip, shaped, preferred_element_type=jnp.float32).astype(jnp.bfloat16)
-        for i in range(seqlen // per):
-            late_ref[at // per + i] = late[:, i * per : (i + 1) * per]
-
-
-def prepare(act, q, k, tick, per):
+        late_ref[:, here] = jnp.dot(flip, shaped, preferred_element_type=jnp.float32).astype(jnp.bfloat16)
+
+
+def prepare(act, q, k, tick):
     _, seqlen, width = act.shape
-    groups = width // per
     block = pl.BlockSpec((1, seqlen, width), lambda i: (tick, 0, 0))
     return pl.pallas_call(
-        functools.partial(prepare_kernel, per),
+        prepare_kernel,
         grid=(1,),
         in_specs=[block] * 3,
-        out_specs=[whole_spec((width, seqlen))] * 2 + [whole_spec((groups, seqlen, per))],
+        out_specs=[whole_spec((width, seqlen))] * 2 + [whole_spec((seqlen, width))],
         out_shape=[jax.ShapeDtypeStruct((width, seqlen), jnp.bfloat16)] * 2
-        + [jax.ShapeDtypeStruct((groups, seqlen, per), jnp.bfloat16)],
+        + [jax.ShapeDtypeStruct((seqlen, width), jnp.bfloat16)],
         compiler_params=pltpu.CompilerParams(vmem_limit_bytes=VMEM),
         name="prepare",
     )(act, q, k)
 
 
-def correlate(adj, late):
-    corr = jnp.dot(late, adj, preferred_element_type=jnp.float32)
-    rolled = pltpu.roll(corr, 1, 1, stride=1, stride_axis=0)
-    r = lax.broadcasted_iota(jnp.int32, corr.shape, 0)
-    lag = lax.broadcasted_iota(jnp.int32, corr.shape, 1)
-    return jnp.sum(jnp.where(lag <= r, rolled, 0.0), axis=0, keepdims=True)
+def correlate(adj, late, per):
+    width, seqlen = adj.shape
+    spread = []
+    for at in range(0, width, per):
+        above, below = jnp.zeros((at, seqlen), adj.dtype), jnp.zeros((width - at - per, seqlen), adj.dtype)
+        spread.append(jnp.concatenate([x for x in (above, adj[at : at + per], below) if x.shape[0]], axis=0))
+    corr = jnp.dot(late, jnp.concatenate(spread, axis=1), preferred_element_type=jnp.float32)
+    r = lax.broadcasted_iota(jnp.int32, (seqlen, seqlen), 0)
+    lag = lax.broadcasted_iota(jnp.int32, (seqlen, seqlen), 1)
+    rows = []
+    for at in range(0, corr.shape[1], seqlen):
+        rolled = pltpu.roll(corr[:, at : at + seqlen], 1, 1, stride=1, stride_axis=0)
+        rows.append(jnp.sum(jnp.where(lag <= r, rolled, 0.0), axis=0, keepdims=True))
+    return jnp.concatenate(rows, axis=0)
 
 
 def project(offsets, place_ref, g_ref, w_refs, total=None):
@@ -108,42 +113,49 @@
 
 def last_kernel(offsets, per, place_ref, own_ref, other_ref, *refs):
     count = len(offsets)
-    w_refs = refs[:count]
-    q_ref, late_ref, term_ref, _, adj_ref, sum_ref, g_ref, lag_ref = refs[count:]
-    step = pl.program_id(0)
+    q_ref, late_ref, term_ref, adj_ref, sum_ref, g_ref, acc_ref, lag_ref, held_ref, sems = refs[count:]
+    copies = [pltpu.make_async_copy(refs[i], held_ref.at[i], sems.at[i]) for i in range(count)]
+    for copy in copies:
+        copy.start()
     parts = own_ref.shape[0]
-
-    @pl.when(step == 0)
-    def _():
-        g_ref[pl.ds(place_ref[1] * parts, parts)] = own_ref[...]
-        g_ref[pl.ds((1 - place_ref[1]) * parts, parts)] = other_ref[...]
-
-    deriv = project(offsets, place_ref, g_ref, w_refs)
-    adj = (q_ref[...].astype(jnp.float32) * deriv).astype(jnp.bfloat16)
-    adj_ref[...] = adj
-    groups = late_ref.shape[0]
-    rows = [correlate(adj[p * per : (p + 1) * per], late_ref[p]) for p in range(groups)]
-    for p in range(0, groups, 8):
-        at = pl.ds(pl.multiple_of(step * groups + p, 8), 8)
-        lag_ref[at, :] = term_ref[p : p + 8, :] + jnp.concatenate(rows[p : p + 8], axis=0)
-
-    @pl.when(step == pl.num_programs(0) - 1)
-    def _():
-        sum_ref[...] = lag_ref[...].T
+    g_ref[pl.ds(place_ref[1] * parts, parts)] = own_ref[...]
+    g_ref[pl.ds((1 - place_ref[1]) * parts, parts)] = other_ref[...]
+    width, seqlen = acc_ref.shape
+    peers, depth = g_ref.shape[0], held_ref.shape[2]
+    for i, (offset, first) in enumerate(offsets):
+        g = g_ref[lax.rem(place_ref[0] + (offset + peers), peers), first : first + depth, :]
+        copies[i].wait()
+        for row in range(0, width, width // 2):
+            at = slice(row, row + width // 2)
+            part = jnp.dot(held_ref[i, at, :], g, preferred_element_type=jnp.float32)
+            acc_ref[at, :] = part if i == 0 else acc_ref[at, :] + part
+    for row in range(0, width, seqlen):
+        at = slice(row, row + seqlen)
+        adj = (q_ref[at, :].astype(jnp.float32) * acc_ref[at, :]).astype(jnp.bfloat16)
+        adj_ref[at, :] = adj
+        to = slice(row // per, (row + seqlen) // per)
+        lag_ref[to, :] = term_ref[to, :] + correlate(adj, late_ref[:, at], per)
+    sum_ref[...] = lag_ref[...].T
 
 
 def lags_kernel(per, adj_ref, late_ref, out_ref):
-    for p in range(out_ref.shape[0]):
-        out_ref[p : p + 1, :] = correlate(adj_ref[p * per : (p + 1) * per, :], late_ref[p])
+    width, seqlen = adj_ref.shape
+    for row in range(0, width, seqlen):
+        at = slice(row, row + seqlen)
+        out_ref[row // per : (row + seqlen) // per, :] = correlate(adj_ref[at, :], late_ref[:, at], per)
 
 
 def turn_kernel(in_ref, out_ref):
-    out_ref[0] = in_ref[...].T
+    width, seqlen = in_ref.shape
+    for row in range(0, width, seqlen):
+        out_ref[0, :, row : row + seqlen] = in_ref[row : row + seqlen, :].T
 
 
 def finish_kernel(per, adj_ref, own_ref, k_ref, toe_ref, held_ref, out_ref, back_ref):
     shape_back(adj_ref[...], own_ref[...], k_ref[...], toe_ref, back_ref, per)
-    out_ref[0] = back_ref[...].T
+    width, seqlen = back_ref.shape
+    for row in range(0, width, seqlen):
+        out_ref[0, :, row : row + seqlen] = back_ref[row : row + seqlen, :].T
 
 
 def chan(seqlen):
@@ -199,17 +211,34 @@
     )
 
 
-def last_part(place, own, other, offsets, panels, q, late, term, ready, per):
+def last_part(place, own, other, offsets, panels, q, late, term, per):
     parts, depth, seqlen = own.shape
-    at = chan(seqlen)
-    groups = late.shape[0]
-    return call(
-        functools.partial(last_kernel, offsets, per), place, [own, other], panels, [q, late, term, ready],
-        [at, grouped(late.shape[1:], per), grouped((seqlen,), per), pl.BlockSpec(memory_space=pl.ANY)], [at, whole_spec((seqlen, groups))],
-        [jax.ShapeDtypeStruct(q.shape, jnp.bfloat16), jax.ShapeDtypeStruct((seqlen, groups), jnp.float32)],
-        "last_tick",
-        [pltpu.VMEM((2 * parts, depth, seqlen), jnp.bfloat16), pltpu.VMEM((groups, seqlen), jnp.float32)],
-    )
+    width, across = panels[0].shape
+    groups = width // per
+    size = sum(p.size for p in panels)
+    anywhere = pl.BlockSpec(memory_space=pl.ANY)
+    return pl.pallas_call(
+        functools.partial(last_kernel, offsets, per),
+        grid_spec=pltpu.PrefetchScalarGridSpec(
+            num_scalar_prefetch=1,
+            grid=(1,),
+            in_specs=[whole_spec(own.shape)] * 2
+            + [anywhere] * len(panels)
+            + [whole_spec(q.shape), whole_spec(late.shape), whole_spec(term.shape)],
+            out_specs=[whole_spec(q.shape), whole_spec((seqlen, groups))],
+            scratch_shapes=[
+                pltpu.VMEM((2 * parts, depth, seqlen), jnp.bfloat16),
+                pltpu.VMEM((width, seqlen), jnp.float32),
+                pltpu.VMEM((groups, seqlen), jnp.float32),
+                pltpu.VMEM((len(panels), width, across), jnp.bfloat16),
+                pltpu.SemaphoreType.DMA((len(panels),)),
+            ],
+        ),
+        out_shape=[jax.ShapeDtypeStruct(q.shape, jnp.bfloat16), jax.ShapeDtypeStruct((seqlen, groups), jnp.float32)],
+        compiler_params=pltpu.CompilerParams(vmem_limit_bytes=VMEM),
+        cost_estimate=pl.CostEstimate(flops=2 * size * seqlen, bytes_accessed=2 * size, transcendentals=0),
+        name="last_tick",
+    )(place, own, other, *panels, q, late, term)
 
 
 def small_cost(width, seqlen):
@@ -221,7 +250,7 @@
     return pl.pallas_call(
         functools.partial(lags_kernel, per),
         grid=(width // BLOCK,),
-        in_specs=[chan(seqlen), grouped(late.shape[1:], per)],
+        in_specs=[chan(seqlen), pl.BlockSpec((seqlen, BLOCK), lambda i: (0, i))],
         out_specs=grouped((seqlen,), per),
         out_shape=jax.ShapeDtypeStruct((width // per, seqlen), jnp.float32),
         compiler_params=pltpu.CompilerParams(vmem_limit_bytes=VMEM),
@@ -234,10 +263,11 @@
     width, seqlen = value.shape
     return pl.pallas_call(
         turn_kernel,
-        grid=(width // BLOCK,),
-        in_specs=[chan(seqlen)],
-        out_specs=pl.BlockSpec((1, seqlen, BLOCK), lambda i: (0, 0, i)),
+        grid=(1,),
+        in_specs=[whole_spec(value.shape)],
+        out_specs=pl.BlockSpec((1, seqlen, width), lambda i: (0, 0, 0)),
         out_shape=jax.ShapeDtypeStruct((ticks, seqlen, width), jnp.bfloat16),
+        compiler_params=pltpu.CompilerParams(vmem_limit_bytes=VMEM),
         name="turn",
     )(value)
 
@@ -306,7 +336,7 @@
     own = grad_in[0, 0].T
     other = lax.ppermute(own, "tp", [(0, 1), (1, 0)])
     acts, qs, ks = act_in[0, :, 0], gate_q[0, :, 0], gate_k[0, :, 0]
-    ready = [prepare(acts, qs, ks, i, per) for i in range(ticks)]
+    ready = [prepare(acts, qs, ks, i) for i in range(ticks)]
     q, k, late = zip(*ready)
     toe = toeplitz(filters[0, ::-1].T.astype(jnp.float32))
     whole = both_halves(own, other, rank).reshape(-1, depth, seqlen)
@@ -335,7 +365,7 @@
     every = held(0, 1, 2, 3, 4)
     adj, total = last_part(
         place, own.reshape(-1, depth, seqlen), other.reshape(-1, depth, seqlen), every, [panels[at] for at in every],
-        q[1], late[1], term, grads, per,
+        q[1], late[1], term, per,
     )
     spread = lax.all_to_all(total.reshape(lax.axis_size("fsdp"), -1, groups), "fsdp", 0, 0, tiled=True)
     grads = finish(adj, own, k[1], toe, grads, 1, per)

time: 221 us -> 216 us (0.977)
  waiting for transfers between devices: 103 us -> 115 us
  Pallas kernels: 49.1 us -> 39.9 us
  local copies, waits for them, and re-layouts: 21.5 us -> 14.3 us
    pallas_call x5 -> x4, Pallas kernels: 30 us -> 16.8 us  [call(): pl.pallas_call(kernel, grid_spec=pltpu.PrefetchScalarGridSpec(num_scalar_...]
    unnamed x68 -> x54, local copies, waits for them, and re-layouts: 19.6 us -> 12.4 us
    ppermute x14, waiting for transfers between devices: 99.8 us -> 107 us  [round_ring(): lax.ppermute(value, 'fsdp', [(i, (i + by) % peers) for i in range(peers)])]
    ppermute x1, waiting for transfers between devices: 0.41 us -> 6.52 us  [body(): other = lax.ppermute(out, ('pipe', 'tp'), crossed)]
    pallas_call x3 -> x4, Pallas kernels: 7.89 us -> 11.7 us  [the longest x1 9.9 us: last_part(): pl.pallas_call(functools.partial(last_kernel, offsets, per), grid_spec=pl...]
  transfers between devices with their start and end apart: 18 -> 18, of which waited for: 9 -> 10; matrix products, arithmetic and copies ran while one was open for 2% -> 1% of each run, Pallas kernels for 15% -> 12%
where the time goes in v2:
time: 216 us; the launch traced here: 213 us
  waiting for transfers between devices  115 us (53%)
  starting transfers between devices  41.9 us (19%)
  Pallas kernels  39.9 us (18%)
  local copies, waits for them, and re-layouts  14.3 us (7%)
    ppermute x14, waiting for transfers between devices, round_ring(): lax.ppermute(value, 'fsdp', [(i, (i + by) % peers) for i in range(peers)])  107 us
    ppermute x14, starting transfers between devices, round_ring(): lax.ppermute(value, 'fsdp', [(i, (i + by) % peers) for i in range(peers)])  25.9 us
    pallas_call x4, Pallas kernels, call(): pl.pallas_call(kernel, grid_spec=pltpu.PrefetchScalarGridSpec(num_scalar_...  16.8 us
    unnamed x54, local copies, waits for them, and re-layouts  12.4 us
    pallas_call x1, Pallas kernels, last_part(): pl.pallas_call(functools.partial(last_kernel, offsets, per), grid_spec=pl...  9.9 us
    ppermute x1, waiting for transfers between devices, body(): other = lax.ppermute(out, ('pipe', 'tp'), crossed)  6.52 us
    all_to_all x1, starting transfers between devices, body(): lax.all_to_all(total.reshape(lax.axis_size('fsdp'), -1, groups), 'fsdp',...  5.83 us
    pallas_call x1, Pallas kernels, toeplitz(): pl.pallas_call(toeplitz_kernel, grid=(groups // step,), in_specs=[pl.Bloc...  5.49 us
  transfers between devices with their start and end apart: 18, of which 10 were waited for; matrix products, arithmetic and copies ran while one was open for 1% of the time, Pallas kernels for 12%

profile of v2, /device:TPU:16, one launch (start us, length us, event | category | flops | bytes accessed | tf_op | source)
XLA Modules:
  0.0 213.4 jit_solution(7126890134628945752)
XLA Ops:
  0.7 1.8 slice_bitcast_fusion
  2.5 2.0 collective-permute-start.1
  4.5 4.0 %collective-permute-start.5 = (bf16[2048,256]{1,0:T(8,128)(2,1)S(1)}, bf16[2048,256]{1,0:T(8,128)(2,1)}, u32[]{:S(2)}, u32[]{:S(2)}) collective-permute-start(bf16[2048,256]{1,0:T(8,128)(2,1)S(1)} %get-tuple-element.24.refs_3_.refs_8_), channel_id=1, source_target_pairs={{0,14},{2,0},{4,2},{6,4},{8,6},{10,8},{12,10},{14,12},{1,15},{3,1}... | collective-permute-start | bytes 3145736 | tf_op jit(solution)/shard_map/ppermute | solution.py:313
  8.5 3.2 %collective-permute-start.12 = (bf16[2048,256]{1,0:T(8,128)(2,1)S(1)}, bf16[2048,256]{1,0:T(8,128)(2,1)}, u32[]{:S(2)}, u32[]{:S(2)}) collective-permute-start(bf16[2048,256]{1,0:T(8,128)(2,1)S(1)} %get-tuple-element.25.refs_2_.refs_7_), channel_id=1, source_target_pairs={{0,14},{2,0},{4,2},{6,4},{8,6},{10,8},{12,10},{14,12},{1,15},{3,1}... | collective-permute-start | bytes 3145736 | tf_op jit(solution)/shard_map/ppermute | solution.py:313
  11.8 20.8 %collective-permute-done.1.refs_0_.refs_5_ = bf16[2048,256]{1,0:T(8,128)(2,1)} collective-permute-done((bf16[2048,256]{1,0:T(8,128)(2,1)S(1)}, bf16[2048,256]{1,0:T(8,128)(2,1)}, u32[]{:S(2)}, u32[]{:S(2)}) %collective-permute-start.1) | collective-permute-done | bytes 1048608 | tf_op jit(solution)/shard_map/ppermute | solution.py:313
  32.5 3.4 %collective-permute-start.6 = (bf16[2048,256]{1,0:T(8,128)(2,1)}, bf16[2048,256]{1,0:T(8,128)(2,1)S(1)}, u32[]{:S(2)}, u32[]{:S(2)}) collective-permute-start(bf16[2048,256]{1,0:T(8,128)(2,1)} %collective-permute-done.5.refs_5_.refs_10_), channel_id=1, source_target_pairs={{0,14},{2,0},{4,2},{6,4},{8,6},{10,8},{12,10},{14,12},{1,15},{3,1}... | collective-permute-start | bytes 3145736 | tf_op jit(solution)/shard_map/ppermute | solution.py:313
  42.5 5.5 %toeplitz.1.refs_7_.refs_6_.toe_ref = bf16[128,128,128]{2,1,0:T(8,128)(2,1)} custom-call(f32[128,128]{1,0:T(8,128)} %convert_bitcast_fusion.rows_ref), custom_call_target="tpu_custom_call" | custom-call | tf_op jit(solution)/shard_map/toeplitz/pallas_call | solution.py:27
  48.0 7.0 %collective-permute-done.9.refs_1_.refs_6_ = bf16[2048,256]{1,0:T(8,128)(2,1)} collective-permute-done((bf16[2048,256]{1,0:T(8,128)(2,1)S(1)}, bf16[2048,256]{1,0:T(8,128)(2,1)}, u32[]{:S(2)}, u32[]{:S(2)}) %collective-permute-start.9) | collective-permute-done | bytes 1048608 | tf_op jit(solution)/shard_map/ppermute | solution.py:313
  55.0 3.4 %collective-permute-start.13 = (bf16[2048,256]{1,0:T(8,128)(2,1)}, bf16[2048,256]{1,0:T(8,128)(2,1)}, u32[]{:S(2)}, u32[]{:S(2)}) collective-permute-start(bf16[2048,256]{1,0:T(8,128)(2,1)} %collective-permute-done.12.refs_4_.refs_9_), channel_id=1, source_target_pairs={{0,14},{2,0},{4,2},{6,4},{8,6},{10,8},{12,10},{14,12},{1,15},{3,1}... | collective-permute-start | bytes 3145736 | tf_op jit(solution)/shard_map/ppermute | solution.py:313
  58.3 19.1 %collective-permute-done.2.refs_0_.refs_3_ = bf16[2048,256]{1,0:T(8,128)(2,1)} collective-permute-done((bf16[2048,256]{1,0:T(8,128)(2,1)}, bf16[2048,256]{1,0:T(8,128)(2,1)}, u32[]{:S(2)}, u32[]{:S(2)}) %collective-permute-start.2) | collective-permute-done | bytes 1048608 | tf_op jit(solution)/shard_map/ppermute | solution.py:313
  78.4 3.2 %collective-permute-start.7 = (bf16[2048,256]{1,0:T(8,128)(2,1)}, bf16[2048,256]{1,0:T(8,128)(2,1)}, u32[]{:S(2)}, u32[]{:S(2)}) collective-permute-start(bf16[2048,256]{1,0:T(8,128)(2,1)} %after.1.refs_3_.refs_12_), channel_id=1, source_target_pairs={{0,14},{2,0},{4,2},{6,4},{8,6},{10,8},{12,10},{14,12},{1,15},{3,1}... | collective-permute-start | bytes 3145736 | tf_op jit(solution)/shard_map/ppermute | solution.py:313
  81.7 1.3 copy.10
  83.0 3.1 %collective-permute-start = (bf16[2048,128]{1,0:T(8,128)(2,1)S(1)}, bf16[2048,128]{1,0:T(8,128)(2,1)S(1)}, u32[]{:S(2)}, u32[]{:S(2)}) collective-permute-start(bf16[2048,128]{1,0:T(8,128)(2,1)S(1)} %bitcast.32), channel_id=1, source_target_pairs={{0,1},{1,0},{2,3},{3,2},{4,5},{5,4},{6,7},{7,6},{8,9},{9,8},{10,11... | collective-permute-start | bytes 1572872 | tf_op jit(solution)/shard_map/ppermute | solution.py:337
  86.2 13.7 %collective-permute-done.10.refs_1_.refs_4_ = bf16[2048,256]{1,0:T(8,128)(2,1)} collective-permute-done((bf16[2048,256]{1,0:T(8,128)(2,1)}, bf16[2048,256]{1,0:T(8,128)(2,1)}, u32[]{:S(2)}, u32[]{:S(2)}) %collective-permute-start.10) | collective-permute-done | bytes 1048608 | tf_op jit(solution)/shard_map/ppermute | solution.py:313
  99.9 3.4 %collective-permute-start.14 = (bf16[2048,256]{1,0:T(8,128)(2,1)}, bf16[2048,256]{1,0:T(8,128)(2,1)S(1)}, u32[]{:S(2)}, u32[]{:S(2)}) collective-permute-start(bf16[2048,256]{1,0:T(8,128)(2,1)} %collective-permute-done.13.refs_2_.refs_11_), channel_id=1, source_target_pairs={{0,14},{2,0},{4,2},{6,4},{8,6},{10,8},{12,10},{14,12},{1,15},{3,1}... | collective-permute-start | bytes 3145736 | tf_op jit(solution)/shard_map/ppermute | solution.py:313
  103.3 19.1 %collective-permute-done.3.refs_0_.refs_1_ = bf16[2048,256]{1,0:T(8,128)(2,1)} collective-permute-done((bf16[2048,256]{1,0:T(8,128)(2,1)}, bf16[2048,256]{1,0:T(8,128)(2,1)}, u32[]{:S(2)}, u32[]{:S(2)}) %collective-permute-start.3) | collective-permute-done | bytes 1048608 | tf_op jit(solution)/shard_map/ppermute | solution.py:313
  122.4 3.4 %collective-permute-start.8 = (bf16[2048,256]{1,0:T(8,128)(2,1)}, bf16[2048,256]{1,0:T(8,128)(2,1)S(1)}, u32[]{:S(2)}, u32[]{:S(2)}) collective-permute-start(bf16[2048,256]{1,0:T(8,128)(2,1)} %collective-permute-done.7.refs_3_.refs_14_), channel_id=1, source_target_pairs={{0,14},{2,0},{4,2},{6,4},{8,6},{10,8},{12,10},{14,12},{1,15},{3,1}... | collective-permute-start | bytes 3145736 | tf_op jit(solution)/shard_map/ppermute | solution.py:313
  125.9 4.8 %partial_sums.3.refs_4_ = f32[2048,128]{1,0:T(8,128)S(1)} custom-call(s32[2]{0:T(128)S(1)} %pad_add_fusion.place_ref, bf16[8,512,128]{2,1,0:T(8,128)(2,1)S(1)} %bitcast.28, bf16[2048,256]{1,0:T(8,128)(2,1)} %collective-permute-done.1.refs_0_.refs_5_, bf16[2048,256]{1,0:T(8,128)(2,1)} %collective-permute-done.9.refs_1_.refs_6_, ...), custom_call_target="tpu_custom_call" | custom-call | flops 805306368 | bytes 6291456 | tf_op jit(solution)/shard_map/partial_sums/pallas_call | solution.py:177
  130.8 4.2 %partial_sums.4.refs_4_ = f32[2048,128]{1,0:T(8,128)S(1)} custom-call(s32[2]{0:T(128)S(1)} %pad_add_fusion.place_ref, bf16[8,512,128]{2,1,0:T(8,128)(2,1)S(1)} %bitcast.29, bf16[2048,256]{1,0:T(8,128)(2,1)} %collective-permute-done.2.refs_0_.refs_3_, bf16[2048,256]{1,0:T(8,128)(2,1)} %collective-permute-done.10.refs_1_.refs_4_, ...), custom_call_target="tpu_custom_call" | custom-call | flops 536870912 | bytes 4194304 | tf_op jit(solution)/shard_map/partial_sums/pallas_call | solution.py:177
  135.0 9.8 %collective-permute-done.11.refs_1_.refs_2_ = bf16[2048,256]{1,0:T(8,128)(2,1)S(1)} collective-permute-done((bf16[2048,256]{1,0:T(8,128)(2,1)}, bf16[2048,256]{1,0:T(8,128)(2,1)S(1)}, u32[]{:S(2)}, u32[]{:S(2)}) %collective-permute-start.11) | collective-permute-done | bytes 1048608 | tf_op jit(solution)/shard_map/ppermute | solution.py:313
  144.8 4.0 %partial_sums.5.refs_2_ = f32[2048,128]{1,0:T(8,128)S(1)} custom-call(s32[2]{0:T(128)S(1)} %pad_add_fusion.place_ref, bf16[8,512,128]{2,1,0:T(8,128)(2,1)S(1)} %bitcast.30, bf16[2048,256]{1,0:T(8,128)(2,1)} %collective-permute-done.3.refs_0_.refs_1_, bf16[2048,256]{1,0:T(8,128)(2,1)S(1)} %collective-permute-done.11.refs_1_.refs_2_, ...), custom_call_target="tpu_custom_call" | custom-call | flops 536870912 | bytes 4194304 | tf_op jit(solution)/shard_map/partial_sums/pallas_call | solution.py:177
  148.9 17.6 %collective-permute-done.4.refs_0_ = bf16[2048,256]{1,0:T(8,128)(2,1)S(1)} collective-permute-done((bf16[2048,256]{1,0:T(8,128)(2,1)}, bf16[2048,256]{1,0:T(8,128)(2,1)S(1)}, u32[]{:S(2)}, u32[]{:S(2)}) %collective-permute-start.4) | collective-permute-done | bytes 1048608 | tf_op jit(solution)/shard_map/ppermute | solution.py:313
  166.4 3.8 %first_tick.1 = (bf16[2048,128]{1,0:T(8,128)(2,1)S(1)}, bf16[2048,128]{1,0:T(8,128)(2,1)S(1)}) custom-call(s32[2]{0:T(128)S(1)} %pad_add_fusion.place_ref, bf16[8,512,128]{2,1,0:T(8,128)(2,1)S(1)} %bitcast.31, bf16[2048,256]{1,0:T(8,128)(2,1)S(1)} %collective-permute-done.4.refs_0_, bf16[2048,256]{1,0:T(8,128)(2,1)S(1)} %collective-permute-done.8.refs_1_.refs_15_, ...), custom_call_target="tpu_custom_call" | custom-call | flops 268435456 | bytes 2097152 | tf_op jit(solution)/shard_map/first_tick/pallas_call | solution.py:177
  170.2 3.4 %collective-permute-start.16 = (bf16[2048,128]{1,0:T(8,128)(2,1)S(1)}, bf16[2048,128]{1,0:T(8,128)(2,1)S(1)}, u32[]{:S(2)}, u32[]{:S(2)}) collective-permute-start(bf16[2048,128]{1,0:T(8,128)(2,1)S(1)} %get-tuple-element.18.in_ref), channel_id=1, source_target_pairs={{16,1},{17,0},{32,17},{33,16},{48,33},{49,32},{64,49},{65,48},{80,... | collective-permute-start | bytes 1572872 | tf_op jit(solution)/shard_map/ppermute | solution.py:362
  173.7 3.6 %collective-permute-start.15 = (bf16[2048,128]{1,0:T(8,128)(2,1)S(1)}, bf16[2048,128]{1,0:T(8,128)(2,1)S(1)}, u32[]{:S(2)}, u32[]{:S(2)}) collective-permute-start(bf16[2048,128]{1,0:T(8,128)(2,1)S(1)} %get-tuple-element.18.in_ref), channel_id=1, source_target_pairs={{16,0},{32,16},{48,32},{64,48},{80,64},{96,80},{112,96},{128,112},... | collective-permute-start | bytes 1572872 | tf_op jit(solution)/shard_map/ppermute | solution.py:361
  177.3 3.2 %lags.1.refs_18_ = f32[128,128]{1,0:T(8,128)S(1)} custom-call(bf16[2048,128]{1,0:T(8,128)(2,1)S(1)} %get-tuple-element.19.adj_ref, bf16[128,2048]{1,0:T(8,128)(2,1)S(1)} %copy-done.18), custom_call_target="tpu_custom_call" | custom-call | flops 268435456 | bytes 2097152 | tf_op jit(solution)/shard_map/lags/pallas_call | solution.py:250
  180.5 6.5 %collective-permute-done.16 = bf16[2048,128]{1,0:T(8,128)(2,1)S(1)} collective-permute-done((bf16[2048,128]{1,0:T(8,128)(2,1)S(1)}, bf16[2048,128]{1,0:T(8,128)(2,1)S(1)}, u32[]{:S(2)}, u32[]{:S(2)}) %collective-permute-start.16) | collective-permute-done | bytes 524320 | tf_op jit(solution)/shard_map/ppermute | solution.py:362
  187.8 9.9 %last_tick.1 = (bf16[2048,128]{1,0:T(8,128)(2,1)S(1)}, f32[128,128]{1,0:T(8,128)}) custom-call(s32[2]{0:T(128)S(1)} %pad_add_fusion.place_ref, bf16[4,512,128]{2,1,0:T(8,128)(2,1)S(1)} %bitcast.40, bf16[4,512,128]{2,1,0:T(8,128)(2,1)S(1)} %bitcast.41, bf16[2048,256]{1,0:T(8,128)(2,1)S(1)} %collective-permute-done.4.refs_0_, ...), custom_call_target="tpu_custom_call" | custom-call | flops 2147483648 | bytes 16777216 | tf_op jit(solution)/shard_map/last_tick/pallas_call | solution.py:220
  198.5 5.8 %all-to-all-start = ((f32[8,16,128]{2,1,0:T(8,128)}), f32[8,16,128]{2,1,0:T(8,128)S(1)}, u32[]{:S(2)}, u32[]{:S(2)}) async-start(f32[8,16,128]{2,1,0:T(8,128)} %bitcast.17), calls=%async_computation | async-start | bytes 131072 | tf_op jit(solution)/shard_map/all_to_all | solution.py:370
  206.4 2.2 %copy-done.1 = bf16[128,128,128]{2,1,0:T(8,128)(2,1)S(1)} copy-done((bf16[128,128,128]{2,1,0:T(8,128)(2,1)S(1)}, bf16[128,128,128]{2,1,0:T(8,128)(2,1)}, u32[]{:S(2)}) %copy-start.1) | copy-done | bytes 4194328
  208.6 1.0 copy-done.24
  209.6 2.7 %finish.1 = bf16[2,128,2048]{2,1,0:T(8,128)(2,1)} custom-call(bf16[2048,128]{1,0:T(8,128)(2,1)S(1)} %copy-done.24, bf16[2048,128]{1,0:T(8,128)(2,1)S(1)} %collective-permute-done.15.own_ref, bf16[2048,128]{1,0:T(8,128)(2,1)S(1)} %copy-done.20, bf16[128,128,128]{2,1,0:T(8,128)(2,1)S(1)} %copy-done.1, ...), custom_call_target="tpu_custom_call", output_to_operand_aliasing={{}: (4, {})} | custom-call | flops 268435456 | bytes 2097152 | tf_op jit(solution)/shard_map/finish/pallas_call | solution.py:277
  (78 shorter events, 12.5 us)
Async XLA Ops:
  0.6 35.2 %copy-start.6 = (bf16[1,2,1,128,2048]{4,3,2,1,0:T(8,128)(2,1)S(1)}, bf16[1,2,1,128,2048]{4,3,2,1,0:T(8,128)(2,1)}, u32[]{:S(2)}) copy-start(bf16[1,2,1,128,2048]{4,3,2,1,0:T(8,128)(2,1)} %param.8) | copy-start | bytes 3145732
  0.6 35.2 %copy-start.5 = (bf16[1,2,1,128,2048]{4,3,2,1,0:T(8,128)(2,1)S(1)}, bf16[1,2,1,128,2048]{4,3,2,1,0:T(8,128)(2,1)}, u32[]{:S(2)}) copy-start(bf16[1,2,1,128,2048]{4,3,2,1,0:T(8,128)(2,1)} %param.7) | copy-start | bytes 3145732
  0.7 35.2 %copy-start.4 = (bf16[1,2,1,128,2048]{4,3,2,1,0:T(8,128)(2,1)S(1)}, bf16[1,2,1,128,2048]{4,3,2,1,0:T(8,128)(2,1)}, u32[]{:S(2)}) copy-start(bf16[1,2,1,128,2048]{4,3,2,1,0:T(8,128)(2,1)} %param.6) | copy-start | bytes 3145732
  2.5 30.0 %collective-permute-start.1 = (bf16[2048,256]{1,0:T(8,128)(2,1)S(1)}, bf16[2048,256]{1,0:T(8,128)(2,1)}, u32[]{:S(2)}, u32[]{:S(2)}) collective-permute-start(bf16[2048,256]{1,0:T(8,128)(2,1)S(1)} %get-tuple-element.25.refs_2_.refs_7_), channel_id=1, source_target_pairs={{0,2},{2,4},{4,6},{6,8},{8,10},{10,12},{12,14},{14,0},{1,3},{3,5},... | collective-permute-start | bytes 3145736 | tf_op jit(solution)/shard_map/ppermute | solution.py:313
  4.5 28.0 %collective-permute-start.5 = (bf16[2048,256]{1,0:T(8,128)(2,1)S(1)}, bf16[2048,256]{1,0:T(8,128)(2,1)}, u32[]{:S(2)}, u32[]{:S(2)}) collective-permute-start(bf16[2048,256]{1,0:T(8,128)(2,1)S(1)} %get-tuple-element.24.refs_3_.refs_8_), channel_id=1, source_target_pairs={{0,14},{2,0},{4,2},{6,4},{8,6},{10,8},{12,10},{14,12},{1,15},{3,1}... | collective-permute-start | bytes 3145736 | tf_op jit(solution)/shard_map/ppermute | solution.py:313
  8.5 46.5 %collective-permute-start.9 = (bf16[2048,256]{1,0:T(8,128)(2,1)S(1)}, bf16[2048,256]{1,0:T(8,128)(2,1)}, u32[]{:S(2)}, u32[]{:S(2)}) collective-permute-start(bf16[2048,256]{1,0:T(8,128)(2,1)S(1)} %get-tuple-element.24.refs_3_.refs_8_), channel_id=1, source_target_pairs={{0,2},{2,4},{4,6},{6,8},{8,10},{10,12},{12,14},{14,0},{1,3},{3,5},... | collective-permute-start | bytes 3145736 | tf_op jit(solution)/shard_map/ppermute | solution.py:313
  8.5 46.5 %collective-permute-start.12 = (bf16[2048,256]{1,0:T(8,128)(2,1)S(1)}, bf16[2048,256]{1,0:T(8,128)(2,1)}, u32[]{:S(2)}, u32[]{:S(2)}) collective-permute-start(bf16[2048,256]{1,0:T(8,128)(2,1)S(1)} %get-tuple-element.25.refs_2_.refs_7_), channel_id=1, source_target_pairs={{0,14},{2,0},{4,2},{6,4},{8,6},{10,8},{12,10},{14,12},{1,15},{3,1}... | collective-permute-start | bytes 3145736 | tf_op jit(solution)/shard_map/ppermute | solution.py:313
  32.5 44.9 %collective-permute-start.2 = (bf16[2048,256]{1,0:T(8,128)(2,1)}, bf16[2048,256]{1,0:T(8,128)(2,1)}, u32[]{:S(2)}, u32[]{:S(2)}) collective-permute-start(bf16[2048,256]{1,0:T(8,128)(2,1)} %collective-permute-done.1.refs_0_.refs_5_), channel_id=1, source_target_pairs={{0,2},{2,4},{4,6},{6,8},{8,10},{10,12},{12,14},{14,0},{1,3},{3,5},... | collective-permute-start | bytes 3145736 | tf_op jit(solution)/shard_map/ppermute | solution.py:313
  32.5 44.9 %collective-permute-start.6 = (bf16[2048,256]{1,0:T(8,128)(2,1)}, bf16[2048,256]{1,0:T(8,128)(2,1)S(1)}, u32[]{:S(2)}, u32[]{:S(2)}) collective-permute-start(bf16[2048,256]{1,0:T(8,128)(2,1)} %collective-permute-done.5.refs_5_.refs_10_), channel_id=1, source_target_pairs={{0,14},{2,0},{4,2},{6,4},{8,6},{10,8},{12,10},{14,12},{1,15},{3,1}... | collective-permute-start | bytes 3145736 | tf_op jit(solution)/shard_map/ppermute | solution.py:313
  55.0 44.9 %collective-permute-start.10 = (bf16[2048,256]{1,0:T(8,128)(2,1)}, bf16[2048,256]{1,0:T(8,128)(2,1)}, u32[]{:S(2)}, u32[]{:S(2)}) collective-permute-start(bf16[2048,256]{1,0:T(8,128)(2,1)} %collective-permute-done.9.refs_1_.refs_6_), channel_id=1, source_target_pairs={{0,2},{2,4},{4,6},{6,8},{8,10},{10,12},{12,14},{14,0},{1,3},{3,5},... | collective-permute-start | bytes 3145736 | tf_op jit(solution)/shard_map/ppermute | solution.py:313
  55.0 44.9 %collective-permute-start.13 = (bf16[2048,256]{1,0:T(8,128)(2,1)}, bf16[2048,256]{1,0:T(8,128)(2,1)}, u32[]{:S(2)}, u32[]{:S(2)}) collective-permute-start(bf16[2048,256]{1,0:T(8,128)(2,1)} %collective-permute-done.12.refs_4_.refs_9_), channel_id=1, source_target_pairs={{0,14},{2,0},{4,2},{6,4},{8,6},{10,8},{12,10},{14,12},{1,15},{3,1}... | collective-permute-start | bytes 3145736 | tf_op jit(solution)/shard_map/ppermute | solution.py:313
  77.5 44.9 %collective-permute-start.3 = (bf16[2048,256]{1,0:T(8,128)(2,1)}, bf16[2048,256]{1,0:T(8,128)(2,1)}, u32[]{:S(2)}, u32[]{:S(2)}) collective-permute-start(bf16[2048,256]{1,0:T(8,128)(2,1)} %collective-permute-done.2.refs_0_.refs_3_), channel_id=1, source_target_pairs={{0,2},{2,4},{4,6},{6,8},{8,10},{10,12},{12,14},{14,0},{1,3},{3,5},... | collective-permute-start | bytes 3145736 | tf_op jit(solution)/shard_map/ppermute | solution.py:313
  78.4 44.0 %collective-permute-start.7 = (bf16[2048,256]{1,0:T(8,128)(2,1)}, bf16[2048,256]{1,0:T(8,128)(2,1)}, u32[]{:S(2)}, u32[]{:S(2)}) collective-permute-start(bf16[2048,256]{1,0:T(8,128)(2,1)} %after.1.refs_3_.refs_12_), channel_id=1, source_target_pairs={{0,14},{2,0},{4,2},{6,4},{8,6},{10,8},{12,10},{14,12},{1,15},{3,1}... | collective-permute-start | bytes 3145736 | tf_op jit(solution)/shard_map/ppermute | solution.py:313
  83.0 42.8 %collective-permute-start = (bf16[2048,128]{1,0:T(8,128)(2,1)S(1)}, bf16[2048,128]{1,0:T(8,128)(2,1)S(1)}, u32[]{:S(2)}, u32[]{:S(2)}) collective-permute-start(bf16[2048,128]{1,0:T(8,128)(2,1)S(1)} %bitcast.32), channel_id=1, source_target_pairs={{0,1},{1,0},{2,3},{3,2},{4,5},{5,4},{6,7},{7,6},{8,9},{9,8},{10,11... | collective-permute-start | bytes 1572872 | tf_op jit(solution)/shard_map/ppermute | solution.py:337
  99.9 44.8 %collective-permute-start.11 = (bf16[2048,256]{1,0:T(8,128)(2,1)}, bf16[2048,256]{1,0:T(8,128)(2,1)S(1)}, u32[]{:S(2)}, u32[]{:S(2)}) collective-permute-start(bf16[2048,256]{1,0:T(8,128)(2,1)} %collective-permute-done.10.refs_1_.refs_4_), channel_id=1, source_target_pairs={{0,2},{2,4},{4,6},{6,8},{8,10},{10,12},{12,14},{14,0},{1,3},{3,5},... | collective-permute-start | bytes 3145736 | tf_op jit(solution)/shard_map/ppermute | solution.py:313
  99.9 44.8 %collective-permute-start.14 = (bf16[2048,256]{1,0:T(8,128)(2,1)}, bf16[2048,256]{1,0:T(8,128)(2,1)S(1)}, u32[]{:S(2)}, u32[]{:S(2)}) collective-permute-start(bf16[2048,256]{1,0:T(8,128)(2,1)} %collective-permute-done.13.refs_2_.refs_11_), channel_id=1, source_target_pairs={{0,14},{2,0},{4,2},{6,4},{8,6},{10,8},{12,10},{14,12},{1,15},{3,1}... | collective-permute-start | bytes 3145736 | tf_op jit(solution)/shard_map/ppermute | solution.py:313
  122.4 44.0 %collective-permute-start.4 = (bf16[2048,256]{1,0:T(8,128)(2,1)}, bf16[2048,256]{1,0:T(8,128)(2,1)S(1)}, u32[]{:S(2)}, u32[]{:S(2)}) collective-permute-start(bf16[2048,256]{1,0:T(8,128)(2,1)} %collective-permute-done.3.refs_0_.refs_1_), channel_id=1, source_target_pairs={{0,2},{2,4},{4,6},{6,8},{8,10},{10,12},{12,14},{14,0},{1,3},{3,5},... | collective-permute-start | bytes 3145736 | tf_op jit(solution)/shard_map/ppermute | solution.py:313
  122.4 44.0 %collective-permute-start.8 = (bf16[2048,256]{1,0:T(8,128)(2,1)}, bf16[2048,256]{1,0:T(8,128)(2,1)S(1)}, u32[]{:S(2)}, u32[]{:S(2)}) collective-permute-start(bf16[2048,256]{1,0:T(8,128)(2,1)} %collective-permute-done.7.refs_3_.refs_14_), channel_id=1, source_target_pairs={{0,14},{2,0},{4,2},{6,4},{8,6},{10,8},{12,10},{14,12},{1,15},{3,1}... | collective-permute-start | bytes 3145736 | tf_op jit(solution)/shard_map/ppermute | solution.py:313
  125.9 4.8 %copy-start.3 = (bf16[2048,256]{1,0:T(8,128)(2,1)S(1)}, bf16[2048,256]{1,0:T(8,128)(2,1)}, u32[]{:S(2)}) copy-start(bf16[2048,256]{1,0:T(8,128)(2,1)} %after.1.refs_3_.refs_12_) | copy-start | bytes 3145732
  135.0 31.4 %copy-start = (bf16[128,128,128]{2,1,0:T(8,128)(2,1)S(1)}, bf16[128,128,128]{2,1,0:T(8,128)(2,1)}, u32[]{:S(2)}) copy-start(bf16[128,128,128]{2,1,0:T(8,128)(2,1)} %toeplitz.1.refs_7_.refs_6_.toe_ref) | copy-start | bytes 12582916
  135.0 31.4 %copy-start.14 = (bf16[2048,128]{1,0:T(8,128)(2,1)S(1)}, bf16[2048,128]{1,0:T(8,128)(2,1)}, u32[]{:S(2)}) copy-start(bf16[2048,128]{1,0:T(8,128)(2,1)} %copy-done.13) | copy-start | bytes 1572868
  135.0 31.4 %copy-start.16 = (bf16[2048,128]{1,0:T(8,128)(2,1)S(1)}, bf16[2048,128]{1,0:T(8,128)(2,1)}, u32[]{:S(2)}) copy-start(bf16[2048,128]{1,0:T(8,128)(2,1)} %copy-done.15) | copy-start | bytes 1572868
  144.8 4.0 %copy-start.8 = (bf16[2048,256]{1,0:T(8,128)(2,1)}, bf16[2048,256]{1,0:T(8,128)(2,1)S(1)}, u32[]{:S(2)}) copy-start(bf16[2048,256]{1,0:T(8,128)(2,1)S(1)} %collective-permute-done.14.refs_2_.refs_13_) | copy-start | bytes 3145732
  148.8 28.5 %copy-start.18 = (bf16[128,2048]{1,0:T(8,128)(2,1)S(1)}, bf16[128,2048]{1,0:T(8,128)(2,1)}, u32[]{:S(2)}) copy-start(bf16[128,2048]{1,0:T(8,128)(2,1)} %copy-done.17) | copy-start | bytes 1572868
  148.8 39.0 %copy-start.10 = (bf16[2048,128]{1,0:T(8,128)(2,1)S(1)}, bf16[2048,128]{1,0:T(8,128)(2,1)}, u32[]{:S(2)}) copy-start(bf16[2048,128]{1,0:T(8,128)(2,1)} %copy-done.9) | copy-start | bytes 1572868
  148.8 39.0 %copy-start.12 = (bf16[128,2048]{1,0:T(8,128)(2,1)S(1)}, bf16[128,2048]{1,0:T(8,128)(2,1)}, u32[]{:S(2)}) copy-start(bf16[128,2048]{1,0:T(8,128)(2,1)} %copy-done.11) | copy-start | bytes 1572868
  166.4 3.8 %copy-start.7 = (bf16[2048,256]{1,0:T(8,128)(2,1)}, bf16[2048,256]{1,0:T(8,128)(2,1)S(1)}, u32[]{:S(2)}) copy-start(bf16[2048,256]{1,0:T(8,128)(2,1)S(1)} %collective-permute-done.8.refs_1_.refs_15_) | copy-start | bytes 3145732
  170.2 27.5 %copy-start.21 = (bf16[2048,128]{1,0:T(8,128)(2,1)}, bf16[2048,128]{1,0:T(8,128)(2,1)S(1)}, u32[]{:S(2)}) copy-start(bf16[2048,128]{1,0:T(8,128)(2,1)S(1)} %get-tuple-element.18.in_ref) | copy-start | bytes 1572868
  170.2 16.8 %collective-permute-start.16 = (bf16[2048,128]{1,0:T(8,128)(2,1)S(1)}, bf16[2048,128]{1,0:T(8,128)(2,1)S(1)}, u32[]{:S(2)}, u32[]{:S(2)}) collective-permute-start(bf16[2048,128]{1,0:T(8,128)(2,1)S(1)} %get-tuple-element.18.in_ref), channel_id=1, source_target_pairs={{16,1},{17,0},{32,17},{33,16},{48,33},{49,32},{64,49},{65,48},{80,... | collective-permute-start | bytes 1572872 | tf_op jit(solution)/shard_map/ppermute | solution.py:362
  173.7 14.1 %collective-permute-start.15 = (bf16[2048,128]{1,0:T(8,128)(2,1)S(1)}, bf16[2048,128]{1,0:T(8,128)(2,1)S(1)}, u32[]{:S(2)}, u32[]{:S(2)}) collective-permute-start(bf16[2048,128]{1,0:T(8,128)(2,1)S(1)} %get-tuple-element.18.in_ref), channel_id=1, source_target_pairs={{16,0},{32,16},{48,32},{64,48},{80,64},{96,80},{112,96},{128,112},... | collective-permute-start | bytes 1572872 | tf_op jit(solution)/shard_map/ppermute | solution.py:361
  187.8 18.6 %copy-start.20 = (bf16[2048,128]{1,0:T(8,128)(2,1)S(1)}, bf16[2048,128]{1,0:T(8,128)(2,1)}, u32[]{:S(2)}) copy-start(bf16[2048,128]{1,0:T(8,128)(2,1)} %copy-done.19) | copy-start | bytes 1572868
  198.5 14.2 %all-to-all-start = ((f32[8,16,128]{2,1,0:T(8,128)}), f32[8,16,128]{2,1,0:T(8,128)S(1)}, u32[]{:S(2)}, u32[]{:S(2)}) async-start(f32[8,16,128]{2,1,0:T(8,128)} %bitcast.17), calls=%async_computation | async-start | bytes 131072 | tf_op jit(solution)/shard_map/all_to_all | solution.py:370
  (12 other events, 13.8 us)

commit v3 on v2

--- a/solution.py
+++ b/solution.py
@@ -113,7 +113,7 @@
 
 def last_kernel(offsets, per, place_ref, own_ref, other_ref, *refs):
     count = len(offsets)
-    q_ref, late_ref, term_ref, adj_ref, sum_ref, g_ref, acc_ref, lag_ref, held_ref, sems = refs[count:]
+    q_ref, late_ref, term_ref, _, adj_ref, sum_ref, g_ref, acc_ref, lag_ref, held_ref, sems = refs[count:]
     copies = [pltpu.make_async_copy(refs[i], held_ref.at[i], sems.at[i]) for i in range(count)]
     for copy in copies:
         copy.start()
@@ -211,7 +211,7 @@
     )
 
 
-def last_part(place, own, other, offsets, panels, q, late, term, per):
+def last_part(place, own, other, offsets, panels, q, late, term, ready, per):
     parts, depth, seqlen = own.shape
     width, across = panels[0].shape
     groups = width // per
@@ -224,7 +224,7 @@
             grid=(1,),
             in_specs=[whole_spec(own.shape)] * 2
             + [anywhere] * len(panels)
-            + [whole_spec(q.shape), whole_spec(late.shape), whole_spec(term.shape)],
+            + [whole_spec(q.shape), whole_spec(late.shape), whole_spec(term.shape), anywhere],
             out_specs=[whole_spec(q.shape), whole_spec((seqlen, groups))],
             scratch_shapes=[
                 pltpu.VMEM((2 * parts, depth, seqlen), jnp.bfloat16),
@@ -238,7 +238,7 @@
         compiler_params=pltpu.CompilerParams(vmem_limit_bytes=VMEM),
         cost_estimate=pl.CostEstimate(flops=2 * size * seqlen, bytes_accessed=2 * size, transcendentals=0),
         name="last_tick",
-    )(place, own, other, *panels, q, late, term)
+    )(place, own, other, *panels, q, late, term, ready)
 
 
 def small_cost(width, seqlen):
@@ -340,9 +340,9 @@
     q, k, late = zip(*ready)
     toe = toeplitz(filters[0, ::-1].T.astype(jnp.float32))
     whole = both_halves(own, other, rank).reshape(-1, depth, seqlen)
+    panels[1, half] = after(panels[1, half], *ready[0], *ready[1], toe)
     circulate(2, 0)
     circulate(2, half)
-    panels[2, half] = after(panels[2, half], *ready[0], *ready[1], toe)
     for step in range(3, 5):
         for first in (0, half):
             circulate(step, first)
@@ -365,7 +365,7 @@
     every = held(0, 1, 2, 3, 4)
     adj, total = last_part(
         place, own.reshape(-1, depth, seqlen), other.reshape(-1, depth, seqlen), every, [panels[at] for at in every],
-        q[1], late[1], term, per,
+        q[1], late[1], term, grads, per,
     )
     spread = lax.all_to_all(total.reshape(lax.axis_size("fsdp"), -1, groups), "fsdp", 0, 0, tiled=True)
     grads = finish(adj, own, k[1], toe, grads, 1, per)

time: 216 us -> 215 us (level)
    unnamed x54 -> x50, local copies, waits for them, and re-layouts: 12.4 us -> 11.3 us
  transfers between devices with their start and end apart: 18 -> 18, of which waited for: 10 -> 10; matrix products, arithmetic and copies ran while one was open for 1% -> 2% of each run, Pallas kernels for 12% -> 12%
where the time goes in v3:
time: 215 us; the launch traced here: 213 us
  waiting for transfers between devices  115 us (53%)
  starting transfers between devices  42 us (20%)
  Pallas kernels  39.9 us (19%)
  local copies, waits for them, and re-layouts  13.2 us (6%)
  other arithmetic  2.51 us (1%)
    ppermute x14, waiting for transfers between devices, round_ring(): lax.ppermute(value, 'fsdp', [(i, (i + by) % peers) for i in range(peers)])  106 us
    ppermute x14, starting transfers between devices, round_ring(): lax.ppermute(value, 'fsdp', [(i, (i + by) % peers) for i in range(peers)])  25.9 us
    pallas_call x4, Pallas kernels, call(): pl.pallas_call(kernel, grid_spec=pltpu.PrefetchScalarGridSpec(num_scalar_...  16.8 us
    unnamed x50, local copies, waits for them, and re-layouts  11.3 us
    pallas_call x1, Pallas kernels, last_part(): pl.pallas_call(functools.partial(last_kernel, offsets, per), grid_spec=pl...  9.87 us
    all_to_all x1, starting transfers between devices, body(): lax.all_to_all(total.reshape(lax.axis_size('fsdp'), -1, groups), 'fsdp',...  5.83 us
    ppermute x1, waiting for transfers between devices, body(): other = lax.ppermute(out, ('pipe', 'tp'), crossed)  5.55 us
    pallas_call x1, Pallas kernels, toeplitz(): pl.pallas_call(toeplitz_kernel, grid=(groups // step,), in_specs=[pl.Bloc...  5.45 us
  transfers between devices with their start and end apart: 18, of which 10 were waited for; matrix products, arithmetic and copies ran while one was open for 2% of the time, Pallas kernels for 12%

profile of v3, /device:TPU:16, one launch (start us, length us, event | category | flops | bytes accessed | tf_op | source)
XLA Modules:
  0.0 213.5 jit_solution(2358199049333525321)
XLA Ops:
  0.7 1.8 slice_bitcast_fusion
  2.5 2.0 collective-permute-start.1
  4.5 4.0 %collective-permute-start.5 = (bf16[2048,256]{1,0:T(8,128)(2,1)S(1)}, bf16[2048,256]{1,0:T(8,128)(2,1)S(1)}, u32[]{:S(2)}, u32[]{:S(2)}) collective-permute-start(bf16[2048,256]{1,0:T(8,128)(2,1)S(1)} %get-tuple-element.24.refs_3_.refs_8_), channel_id=1, source_target_pairs={{0,14},{2,0},{4,2},{6,4},{8,6},{10,8},{12,10},{14,12},{1,15},{3,1}... | collective-permute-start | bytes 3145736 | tf_op jit(solution)/shard_map/ppermute | solution.py:313
  8.5 3.2 %collective-permute-start.12 = (bf16[2048,256]{1,0:T(8,128)(2,1)S(1)}, bf16[2048,256]{1,0:T(8,128)(2,1)}, u32[]{:S(2)}, u32[]{:S(2)}) collective-permute-start(bf16[2048,256]{1,0:T(8,128)(2,1)S(1)} %get-tuple-element.25.refs_2_.refs_7_), channel_id=1, source_target_pairs={{0,14},{2,0},{4,2},{6,4},{8,6},{10,8},{12,10},{14,12},{1,15},{3,1}... | collective-permute-start | bytes 3145736 | tf_op jit(solution)/shard_map/ppermute | solution.py:313
  18.4 5.4 %toeplitz.1.refs_7_.refs_6_.toe_ref = bf16[128,128,128]{2,1,0:T(8,128)(2,1)} custom-call(f32[128,128]{1,0:T(8,128)} %convert_bitcast_fusion.rows_ref), custom_call_target="tpu_custom_call" | custom-call | tf_op jit(solution)/shard_map/toeplitz/pallas_call | solution.py:27
  23.8 8.7 %collective-permute-done.1.refs_0_.refs_5_ = bf16[2048,256]{1,0:T(8,128)(2,1)} collective-permute-done((bf16[2048,256]{1,0:T(8,128)(2,1)S(1)}, bf16[2048,256]{1,0:T(8,128)(2,1)}, u32[]{:S(2)}, u32[]{:S(2)}) %collective-permute-start.1) | collective-permute-done | bytes 1048608 | tf_op jit(solution)/shard_map/ppermute | solution.py:313
  33.5 3.2 %collective-permute-start.6 = (bf16[2048,256]{1,0:T(8,128)(2,1)}, bf16[2048,256]{1,0:T(8,128)(2,1)}, u32[]{:S(2)}, u32[]{:S(2)}) collective-permute-start(bf16[2048,256]{1,0:T(8,128)(2,1)} %after.1.refs_5_.refs_10_), channel_id=1, source_target_pairs={{0,14},{2,0},{4,2},{6,4},{8,6},{10,8},{12,10},{14,12},{1,15},{3,1}... | collective-permute-start | bytes 3145736 | tf_op jit(solution)/shard_map/ppermute | solution.py:313
  36.7 18.2 %collective-permute-done.9.refs_1_.refs_6_ = bf16[2048,256]{1,0:T(8,128)(2,1)} collective-permute-done((bf16[2048,256]{1,0:T(8,128)(2,1)S(1)}, bf16[2048,256]{1,0:T(8,128)(2,1)}, u32[]{:S(2)}, u32[]{:S(2)}) %collective-permute-start.9) | collective-permute-done | bytes 1048608 | tf_op jit(solution)/shard_map/ppermute | solution.py:313
  55.0 3.4 %collective-permute-start.13 = (bf16[2048,256]{1,0:T(8,128)(2,1)}, bf16[2048,256]{1,0:T(8,128)(2,1)}, u32[]{:S(2)}, u32[]{:S(2)}) collective-permute-start(bf16[2048,256]{1,0:T(8,128)(2,1)} %collective-permute-done.12.refs_4_.refs_9_), channel_id=1, source_target_pairs={{0,14},{2,0},{4,2},{6,4},{8,6},{10,8},{12,10},{14,12},{1,15},{3,1}... | collective-permute-start | bytes 3145736 | tf_op jit(solution)/shard_map/ppermute | solution.py:313
  58.3 19.1 %collective-permute-done.2.refs_0_.refs_3_ = bf16[2048,256]{1,0:T(8,128)(2,1)} collective-permute-done((bf16[2048,256]{1,0:T(8,128)(2,1)}, bf16[2048,256]{1,0:T(8,128)(2,1)}, u32[]{:S(2)}, u32[]{:S(2)}) %collective-permute-start.2) | collective-permute-done | bytes 1048608 | tf_op jit(solution)/shard_map/ppermute | solution.py:313
  77.5 3.4 %collective-permute-start.7 = (bf16[2048,256]{1,0:T(8,128)(2,1)}, bf16[2048,256]{1,0:T(8,128)(2,1)}, u32[]{:S(2)}, u32[]{:S(2)}) collective-permute-start(bf16[2048,256]{1,0:T(8,128)(2,1)} %collective-permute-done.6.refs_3_.refs_12_), channel_id=1, source_target_pairs={{0,14},{2,0},{4,2},{6,4},{8,6},{10,8},{12,10},{14,12},{1,15},{3,1}... | collective-permute-start | bytes 3145736 | tf_op jit(solution)/shard_map/ppermute | solution.py:313
  80.8 1.3 copy.10
  82.1 3.1 %collective-permute-start = (bf16[2048,128]{1,0:T(8,128)(2,1)S(1)}, bf16[2048,128]{1,0:T(8,128)(2,1)}, u32[]{:S(2)}, u32[]{:S(2)}) collective-permute-start(bf16[2048,128]{1,0:T(8,128)(2,1)S(1)} %bitcast.32), channel_id=1, source_target_pairs={{0,1},{1,0},{2,3},{3,2},{4,5},{5,4},{6,7},{7,6},{8,9},{9,8},{10,11... | collective-permute-start | bytes 1572872 | tf_op jit(solution)/shard_map/ppermute | solution.py:337
  85.3 14.6 %collective-permute-done.10.refs_1_.refs_4_ = bf16[2048,256]{1,0:T(8,128)(2,1)} collective-permute-done((bf16[2048,256]{1,0:T(8,128)(2,1)}, bf16[2048,256]{1,0:T(8,128)(2,1)}, u32[]{:S(2)}, u32[]{:S(2)}) %collective-permute-start.10) | collective-permute-done | bytes 1048608 | tf_op jit(solution)/shard_map/ppermute | solution.py:313
  99.9 3.4 %collective-permute-start.14 = (bf16[2048,256]{1,0:T(8,128)(2,1)}, bf16[2048,256]{1,0:T(8,128)(2,1)S(1)}, u32[]{:S(2)}, u32[]{:S(2)}) collective-permute-start(bf16[2048,256]{1,0:T(8,128)(2,1)} %collective-permute-done.13.refs_2_.refs_11_), channel_id=1, source_target_pairs={{0,14},{2,0},{4,2},{6,4},{8,6},{10,8},{12,10},{14,12},{1,15},{3,1}... | collective-permute-start | bytes 3145736 | tf_op jit(solution)/shard_map/ppermute | solution.py:313
  103.3 19.1 %collective-permute-done.3.refs_0_.refs_1_ = bf16[2048,256]{1,0:T(8,128)(2,1)} collective-permute-done((bf16[2048,256]{1,0:T(8,128)(2,1)}, bf16[2048,256]{1,0:T(8,128)(2,1)}, u32[]{:S(2)}, u32[]{:S(2)}) %collective-permute-start.3) | collective-permute-done | bytes 1048608 | tf_op jit(solution)/shard_map/ppermute | solution.py:313
  122.4 3.4 %collective-permute-start.8 = (bf16[2048,256]{1,0:T(8,128)(2,1)}, bf16[2048,256]{1,0:T(8,128)(2,1)S(1)}, u32[]{:S(2)}, u32[]{:S(2)}) collective-permute-start(bf16[2048,256]{1,0:T(8,128)(2,1)} %collective-permute-done.7.refs_3_.refs_14_), channel_id=1, source_target_pairs={{0,14},{2,0},{4,2},{6,4},{8,6},{10,8},{12,10},{14,12},{1,15},{3,1}... | collective-permute-start | bytes 3145736 | tf_op jit(solution)/shard_map/ppermute | solution.py:313
  127.0 4.6 %partial_sums.3.refs_4_ = f32[2048,128]{1,0:T(8,128)S(1)} custom-call(s32[2]{0:T(128)S(1)} %pad_add_fusion.place_ref, bf16[8,512,128]{2,1,0:T(8,128)(2,1)S(1)} %bitcast.28, bf16[2048,256]{1,0:T(8,128)(2,1)} %collective-permute-done.1.refs_0_.refs_5_, bf16[2048,256]{1,0:T(8,128)(2,1)} %collective-permute-done.9.refs_1_.refs_6_, ...), custom_call_target="tpu_custom_call" | custom-call | flops 805306368 | bytes 6291456 | tf_op jit(solution)/shard_map/partial_sums/pallas_call | solution.py:177
  131.6 4.4 %partial_sums.4.refs_4_ = f32[2048,128]{1,0:T(8,128)S(1)} custom-call(s32[2]{0:T(128)S(1)} %pad_add_fusion.place_ref, bf16[8,512,128]{2,1,0:T(8,128)(2,1)S(1)} %bitcast.29, bf16[2048,256]{1,0:T(8,128)(2,1)} %collective-permute-done.2.refs_0_.refs_3_, bf16[2048,256]{1,0:T(8,128)(2,1)} %collective-permute-done.10.refs_1_.refs_4_, ...), custom_call_target="tpu_custom_call" | custom-call | flops 536870912 | bytes 4194304 | tf_op jit(solution)/shard_map/partial_sums/pallas_call | solution.py:177
  136.0 8.7 %collective-permute-done.11.refs_1_.refs_2_ = bf16[2048,256]{1,0:T(8,128)(2,1)S(1)} collective-permute-done((bf16[2048,256]{1,0:T(8,128)(2,1)}, bf16[2048,256]{1,0:T(8,128)(2,1)S(1)}, u32[]{:S(2)}, u32[]{:S(2)}) %collective-permute-start.11) | collective-permute-done | bytes 1048608 | tf_op jit(solution)/shard_map/ppermute | solution.py:313
  144.8 4.0 %partial_sums.5.refs_2_ = f32[2048,128]{1,0:T(8,128)S(1)} custom-call(s32[2]{0:T(128)S(1)} %pad_add_fusion.place_ref, bf16[8,512,128]{2,1,0:T(8,128)(2,1)S(1)} %bitcast.30, bf16[2048,256]{1,0:T(8,128)(2,1)} %collective-permute-done.3.refs_0_.refs_1_, bf16[2048,256]{1,0:T(8,128)(2,1)S(1)} %collective-permute-done.11.refs_1_.refs_2_, ...), custom_call_target="tpu_custom_call" | custom-call | flops 536870912 | bytes 4194304 | tf_op jit(solution)/shard_map/partial_sums/pallas_call | solution.py:177
  148.8 17.6 %collective-permute-done.4.refs_0_ = bf16[2048,256]{1,0:T(8,128)(2,1)S(1)} collective-permute-done((bf16[2048,256]{1,0:T(8,128)(2,1)}, bf16[2048,256]{1,0:T(8,128)(2,1)S(1)}, u32[]{:S(2)}, u32[]{:S(2)}) %collective-permute-start.4) | collective-permute-done | bytes 1048608 | tf_op jit(solution)/shard_map/ppermute | solution.py:313
  166.4 3.8 %first_tick.1 = (bf16[2048,128]{1,0:T(8,128)(2,1)S(1)}, bf16[2048,128]{1,0:T(8,128)(2,1)S(1)}) custom-call(s32[2]{0:T(128)S(1)} %pad_add_fusion.place_ref, bf16[8,512,128]{2,1,0:T(8,128)(2,1)S(1)} %bitcast.31, bf16[2048,256]{1,0:T(8,128)(2,1)S(1)} %collective-permute-done.4.refs_0_, bf16[2048,256]{1,0:T(8,128)(2,1)S(1)} %collective-permute-done.8.refs_1_.refs_15_, ...), custom_call_target="tpu_custom_call" | custom-call | flops 268435456 | bytes 2097152 | tf_op jit(solution)/shard_map/first_tick/pallas_call | solution.py:177
  170.2 3.6 %collective-permute-start.16 = (bf16[2048,128]{1,0:T(8,128)(2,1)S(1)}, bf16[2048,128]{1,0:T(8,128)(2,1)S(1)}, u32[]{:S(2)}, u32[]{:S(2)}) collective-permute-start(bf16[2048,128]{1,0:T(8,128)(2,1)S(1)} %get-tuple-element.18.in_ref), channel_id=1, source_target_pairs={{16,1},{17,0},{32,17},{33,16},{48,33},{49,32},{64,49},{65,48},{80,... | collective-permute-start | bytes 1572872 | tf_op jit(solution)/shard_map/ppermute | solution.py:362
  173.8 3.6 %collective-permute-start.15 = (bf16[2048,128]{1,0:T(8,128)(2,1)S(1)}, bf16[2048,128]{1,0:T(8,128)(2,1)S(1)}, u32[]{:S(2)}, u32[]{:S(2)}) collective-permute-start(bf16[2048,128]{1,0:T(8,128)(2,1)S(1)} %get-tuple-element.18.in_ref), channel_id=1, source_target_pairs={{16,0},{32,16},{48,32},{64,48},{80,64},{96,80},{112,96},{128,112},... | collective-permute-start | bytes 1572872 | tf_op jit(solution)/shard_map/ppermute | solution.py:361
  178.4 3.2 %lags.1.refs_18_ = f32[128,128]{1,0:T(8,128)S(1)} custom-call(bf16[2048,128]{1,0:T(8,128)(2,1)S(1)} %get-tuple-element.19.adj_ref, bf16[128,2048]{1,0:T(8,128)(2,1)S(1)} %copy-done.18), custom_call_target="tpu_custom_call" | custom-call | flops 268435456 | bytes 2097152 | tf_op jit(solution)/shard_map/lags/pallas_call | solution.py:250
  181.6 5.6 %collective-permute-done.16 = bf16[2048,128]{1,0:T(8,128)(2,1)S(1)} collective-permute-done((bf16[2048,128]{1,0:T(8,128)(2,1)S(1)}, bf16[2048,128]{1,0:T(8,128)(2,1)S(1)}, u32[]{:S(2)}, u32[]{:S(2)}) %collective-permute-start.16) | collective-permute-done | bytes 524320 | tf_op jit(solution)/shard_map/ppermute | solution.py:362
  187.9 9.9 %last_tick.1 = (bf16[2048,128]{1,0:T(8,128)(2,1)S(1)}, f32[128,128]{1,0:T(8,128)}) custom-call(s32[2]{0:T(128)S(1)} %pad_add_fusion.place_ref, bf16[4,512,128]{2,1,0:T(8,128)(2,1)S(1)} %bitcast.40, bf16[4,512,128]{2,1,0:T(8,128)(2,1)S(1)} %bitcast.41, bf16[2048,256]{1,0:T(8,128)(2,1)S(1)} %collective-permute-done.4.refs_0_, ...), custom_call_target="tpu_custom_call" | custom-call | flops 2147483648 | bytes 16777216 | tf_op jit(solution)/shard_map/last_tick/pallas_call | solution.py:220
  198.6 5.8 %all-to-all-start = ((f32[8,16,128]{2,1,0:T(8,128)}), f32[8,16,128]{2,1,0:T(8,128)S(1)}, u32[]{:S(2)}, u32[]{:S(2)}) async-start(f32[8,16,128]{2,1,0:T(8,128)} %bitcast.17), calls=%async_computation | async-start | bytes 131072 | tf_op jit(solution)/shard_map/all_to_all | solution.py:370
  204.5 2.2 %copy-done.1 = bf16[128,128,128]{2,1,0:T(8,128)(2,1)S(1)} copy-done((bf16[128,128,128]{2,1,0:T(8,128)(2,1)S(1)}, bf16[128,128,128]{2,1,0:T(8,128)(2,1)}, u32[]{:S(2)}) %copy-start.1) | copy-done | bytes 4194328
  207.7 2.7 %finish.1 = bf16[2,128,2048]{2,1,0:T(8,128)(2,1)} custom-call(bf16[2048,128]{1,0:T(8,128)(2,1)S(1)} %copy-done.22, bf16[2048,128]{1,0:T(8,128)(2,1)S(1)} %collective-permute-done.15.own_ref, bf16[2048,128]{1,0:T(8,128)(2,1)S(1)} %copy-done.20, bf16[128,128,128]{2,1,0:T(8,128)(2,1)S(1)} %copy-done.1, ...), custom_call_target="tpu_custom_call", output_to_operand_aliasing={{}: (4, {})} | custom-call | flops 268435456 | bytes 2097152 | tf_op jit(solution)/shard_map/finish/pallas_call | solution.py:277
  210.4 2.4 %all-to-all-done = f32[8,16,128]{2,1,0:T(8,128)S(1)} async-done(((f32[8,16,128]{2,1,0:T(8,128)}), f32[8,16,128]{2,1,0:T(8,128)S(1)}, u32[]{:S(2)}, u32[]{:S(2)}) %all-to-all-start) | async-done | bytes 65568 | tf_op jit(solution)/shard_map/all_to_all | solution.py:370
  (74 shorter events, 13.2 us)
Async XLA Ops:
  0.6 11.1 %copy-start.6 = (bf16[1,2,1,128,2048]{4,3,2,1,0:T(8,128)(2,1)S(1)}, bf16[1,2,1,128,2048]{4,3,2,1,0:T(8,128)(2,1)}, u32[]{:S(2)}) copy-start(bf16[1,2,1,128,2048]{4,3,2,1,0:T(8,128)(2,1)} %param.8) | copy-start | bytes 3145732
  0.6 11.1 %copy-start.5 = (bf16[1,2,1,128,2048]{4,3,2,1,0:T(8,128)(2,1)S(1)}, bf16[1,2,1,128,2048]{4,3,2,1,0:T(8,128)(2,1)}, u32[]{:S(2)}) copy-start(bf16[1,2,1,128,2048]{4,3,2,1,0:T(8,128)(2,1)} %param.7) | copy-start | bytes 3145732
  0.7 11.1 %copy-start.4 = (bf16[1,2,1,128,2048]{4,3,2,1,0:T(8,128)(2,1)S(1)}, bf16[1,2,1,128,2048]{4,3,2,1,0:T(8,128)(2,1)}, u32[]{:S(2)}) copy-start(bf16[1,2,1,128,2048]{4,3,2,1,0:T(8,128)(2,1)} %param.6) | copy-start | bytes 3145732
  2.5 30.0 %collective-permute-start.1 = (bf16[2048,256]{1,0:T(8,128)(2,1)S(1)}, bf16[2048,256]{1,0:T(8,128)(2,1)}, u32[]{:S(2)}, u32[]{:S(2)}) collective-permute-start(bf16[2048,256]{1,0:T(8,128)(2,1)S(1)} %get-tuple-element.25.refs_2_.refs_7_), channel_id=1, source_target_pairs={{0,2},{2,4},{4,6},{6,8},{8,10},{10,12},{12,14},{14,0},{1,3},{3,5},... | collective-permute-start | bytes 3145736 | tf_op jit(solution)/shard_map/ppermute | solution.py:313
  4.5 28.0 %collective-permute-start.5 = (bf16[2048,256]{1,0:T(8,128)(2,1)S(1)}, bf16[2048,256]{1,0:T(8,128)(2,1)S(1)}, u32[]{:S(2)}, u32[]{:S(2)}) collective-permute-start(bf16[2048,256]{1,0:T(8,128)(2,1)S(1)} %get-tuple-element.24.refs_3_.refs_8_), channel_id=1, source_target_pairs={{0,14},{2,0},{4,2},{6,4},{8,6},{10,8},{12,10},{14,12},{1,15},{3,1}... | collective-permute-start | bytes 3145736 | tf_op jit(solution)/shard_map/ppermute | solution.py:313
  8.5 46.5 %collective-permute-start.9 = (bf16[2048,256]{1,0:T(8,128)(2,1)S(1)}, bf16[2048,256]{1,0:T(8,128)(2,1)}, u32[]{:S(2)}, u32[]{:S(2)}) collective-permute-start(bf16[2048,256]{1,0:T(8,128)(2,1)S(1)} %get-tuple-element.24.refs_3_.refs_8_), channel_id=1, source_target_pairs={{0,2},{2,4},{4,6},{6,8},{8,10},{10,12},{12,14},{14,0},{1,3},{3,5},... | collective-permute-start | bytes 3145736 | tf_op jit(solution)/shard_map/ppermute | solution.py:313
  8.5 46.5 %collective-permute-start.12 = (bf16[2048,256]{1,0:T(8,128)(2,1)S(1)}, bf16[2048,256]{1,0:T(8,128)(2,1)}, u32[]{:S(2)}, u32[]{:S(2)}) collective-permute-start(bf16[2048,256]{1,0:T(8,128)(2,1)S(1)} %get-tuple-element.25.refs_2_.refs_7_), channel_id=1, source_target_pairs={{0,14},{2,0},{4,2},{6,4},{8,6},{10,8},{12,10},{14,12},{1,15},{3,1}... | collective-permute-start | bytes 3145736 | tf_op jit(solution)/shard_map/ppermute | solution.py:313
  14.6 2.9 %copy-start.23 = (bf16[1,128,128]{2,1,0:T(8,128)(2,1)S(1)}, bf16[1,128,128]{2,1,0:T(8,128)(2,1)}, u32[]{:S(2)}) copy-start(bf16[1,128,128]{2,1,0:T(8,128)(2,1)} %param.11) | copy-start | bytes 98308
  32.5 44.9 %collective-permute-start.2 = (bf16[2048,256]{1,0:T(8,128)(2,1)}, bf16[2048,256]{1,0:T(8,128)(2,1)}, u32[]{:S(2)}, u32[]{:S(2)}) collective-permute-start(bf16[2048,256]{1,0:T(8,128)(2,1)} %collective-permute-done.1.refs_0_.refs_5_), channel_id=1, source_target_pairs={{0,2},{2,4},{4,6},{6,8},{8,10},{10,12},{12,14},{14,0},{1,3},{3,5},... | collective-permute-start | bytes 3145736 | tf_op jit(solution)/shard_map/ppermute | solution.py:313
  33.5 44.0 %collective-permute-start.6 = (bf16[2048,256]{1,0:T(8,128)(2,1)}, bf16[2048,256]{1,0:T(8,128)(2,1)}, u32[]{:S(2)}, u32[]{:S(2)}) collective-permute-start(bf16[2048,256]{1,0:T(8,128)(2,1)} %after.1.refs_5_.refs_10_), channel_id=1, source_target_pairs={{0,14},{2,0},{4,2},{6,4},{8,6},{10,8},{12,10},{14,12},{1,15},{3,1}... | collective-permute-start | bytes 3145736 | tf_op jit(solution)/shard_map/ppermute | solution.py:313
  55.0 44.9 %collective-permute-start.10 = (bf16[2048,256]{1,0:T(8,128)(2,1)}, bf16[2048,256]{1,0:T(8,128)(2,1)}, u32[]{:S(2)}, u32[]{:S(2)}) collective-permute-start(bf16[2048,256]{1,0:T(8,128)(2,1)} %collective-permute-done.9.refs_1_.refs_6_), channel_id=1, source_target_pairs={{0,2},{2,4},{4,6},{6,8},{8,10},{10,12},{12,14},{14,0},{1,3},{3,5},... | collective-permute-start | bytes 3145736 | tf_op jit(solution)/shard_map/ppermute | solution.py:313
  55.0 44.9 %collective-permute-start.13 = (bf16[2048,256]{1,0:T(8,128)(2,1)}, bf16[2048,256]{1,0:T(8,128)(2,1)}, u32[]{:S(2)}, u32[]{:S(2)}) collective-permute-start(bf16[2048,256]{1,0:T(8,128)(2,1)} %collective-permute-done.12.refs_4_.refs_9_), channel_id=1, source_target_pairs={{0,14},{2,0},{4,2},{6,4},{8,6},{10,8},{12,10},{14,12},{1,15},{3,1}... | collective-permute-start | bytes 3145736 | tf_op jit(solution)/shard_map/ppermute | solution.py:313
  77.5 44.9 %collective-permute-start.3 = (bf16[2048,256]{1,0:T(8,128)(2,1)}, bf16[2048,256]{1,0:T(8,128)(2,1)}, u32[]{:S(2)}, u32[]{:S(2)}) collective-permute-start(bf16[2048,256]{1,0:T(8,128)(2,1)} %collective-permute-done.2.refs_0_.refs_3_), channel_id=1, source_target_pairs={{0,2},{2,4},{4,6},{6,8},{8,10},{10,12},{12,14},{14,0},{1,3},{3,5},... | collective-permute-start | bytes 3145736 | tf_op jit(solution)/shard_map/ppermute | solution.py:313
  77.5 44.9 %collective-permute-start.7 = (bf16[2048,256]{1,0:T(8,128)(2,1)}, bf16[2048,256]{1,0:T(8,128)(2,1)}, u32[]{:S(2)}, u32[]{:S(2)}) collective-permute-start(bf16[2048,256]{1,0:T(8,128)(2,1)} %collective-permute-done.6.refs_3_.refs_12_), channel_id=1, source_target_pairs={{0,14},{2,0},{4,2},{6,4},{8,6},{10,8},{12,10},{14,12},{1,15},{3,1}... | collective-permute-start | bytes 3145736 | tf_op jit(solution)/shard_map/ppermute | solution.py:313
  82.1 43.6 %collective-permute-start = (bf16[2048,128]{1,0:T(8,128)(2,1)S(1)}, bf16[2048,128]{1,0:T(8,128)(2,1)}, u32[]{:S(2)}, u32[]{:S(2)}) collective-permute-start(bf16[2048,128]{1,0:T(8,128)(2,1)S(1)} %bitcast.32), channel_id=1, source_target_pairs={{0,1},{1,0},{2,3},{3,2},{4,5},{5,4},{6,7},{7,6},{8,9},{9,8},{10,11... | collective-permute-start | bytes 1572872 | tf_op jit(solution)/shard_map/ppermute | solution.py:337
  85.3 41.6 %copy-start.3 = (bf16[2048,256]{1,0:T(8,128)(2,1)S(1)}, bf16[2048,256]{1,0:T(8,128)(2,1)}, u32[]{:S(2)}) copy-start(bf16[2048,256]{1,0:T(8,128)(2,1)} %after.1.refs_5_.refs_10_) | copy-start | bytes 3145732
  99.9 44.8 %collective-permute-start.11 = (bf16[2048,256]{1,0:T(8,128)(2,1)}, bf16[2048,256]{1,0:T(8,128)(2,1)S(1)}, u32[]{:S(2)}, u32[]{:S(2)}) collective-permute-start(bf16[2048,256]{1,0:T(8,128)(2,1)} %collective-permute-done.10.refs_1_.refs_4_), channel_id=1, source_target_pairs={{0,2},{2,4},{4,6},{6,8},{8,10},{10,12},{12,14},{14,0},{1,3},{3,5},... | collective-permute-start | bytes 3145736 | tf_op jit(solution)/shard_map/ppermute | solution.py:313
  99.9 44.8 %collective-permute-start.14 = (bf16[2048,256]{1,0:T(8,128)(2,1)}, bf16[2048,256]{1,0:T(8,128)(2,1)S(1)}, u32[]{:S(2)}, u32[]{:S(2)}) collective-permute-start(bf16[2048,256]{1,0:T(8,128)(2,1)} %collective-permute-done.13.refs_2_.refs_11_), channel_id=1, source_target_pairs={{0,14},{2,0},{4,2},{6,4},{8,6},{10,8},{12,10},{14,12},{1,15},{3,1}... | collective-permute-start | bytes 3145736 | tf_op jit(solution)/shard_map/ppermute | solution.py:313
  122.4 44.0 %collective-permute-start.4 = (bf16[2048,256]{1,0:T(8,128)(2,1)}, bf16[2048,256]{1,0:T(8,128)(2,1)S(1)}, u32[]{:S(2)}, u32[]{:S(2)}) collective-permute-start(bf16[2048,256]{1,0:T(8,128)(2,1)} %collective-permute-done.3.refs_0_.refs_1_), channel_id=1, source_target_pairs={{0,2},{2,4},{4,6},{6,8},{8,10},{10,12},{12,14},{14,0},{1,3},{3,5},... | collective-permute-start | bytes 3145736 | tf_op jit(solution)/shard_map/ppermute | solution.py:313
  122.4 44.0 %collective-permute-start.8 = (bf16[2048,256]{1,0:T(8,128)(2,1)}, bf16[2048,256]{1,0:T(8,128)(2,1)S(1)}, u32[]{:S(2)}, u32[]{:S(2)}) collective-permute-start(bf16[2048,256]{1,0:T(8,128)(2,1)} %collective-permute-done.7.refs_3_.refs_14_), channel_id=1, source_target_pairs={{0,14},{2,0},{4,2},{6,4},{8,6},{10,8},{12,10},{14,12},{1,15},{3,1}... | collective-permute-start | bytes 3145736 | tf_op jit(solution)/shard_map/ppermute | solution.py:313
  136.0 30.4 %copy-start = (bf16[128,128,128]{2,1,0:T(8,128)(2,1)S(1)}, bf16[128,128,128]{2,1,0:T(8,128)(2,1)}, u32[]{:S(2)}) copy-start(bf16[128,128,128]{2,1,0:T(8,128)(2,1)} %toeplitz.1.refs_7_.refs_6_.toe_ref) | copy-start | bytes 12582916
  136.0 30.4 %copy-start.14 = (bf16[2048,128]{1,0:T(8,128)(2,1)S(1)}, bf16[2048,128]{1,0:T(8,128)(2,1)}, u32[]{:S(2)}) copy-start(bf16[2048,128]{1,0:T(8,128)(2,1)} %copy-done.13) | copy-start | bytes 1572868
  136.0 30.4 %copy-start.16 = (bf16[2048,128]{1,0:T(8,128)(2,1)S(1)}, bf16[2048,128]{1,0:T(8,128)(2,1)}, u32[]{:S(2)}) copy-start(bf16[2048,128]{1,0:T(8,128)(2,1)} %copy-done.15) | copy-start | bytes 1572868
  144.8 4.0 %copy-start.8 = (bf16[2048,256]{1,0:T(8,128)(2,1)}, bf16[2048,256]{1,0:T(8,128)(2,1)S(1)}, u32[]{:S(2)}) copy-start(bf16[2048,256]{1,0:T(8,128)(2,1)S(1)} %collective-permute-done.14.refs_2_.refs_13_) | copy-start | bytes 3145732
  148.8 29.6 %copy-start.18 = (bf16[128,2048]{1,0:T(8,128)(2,1)S(1)}, bf16[128,2048]{1,0:T(8,128)(2,1)}, u32[]{:S(2)}) copy-start(bf16[128,2048]{1,0:T(8,128)(2,1)} %copy-done.17) | copy-start | bytes 1572868
  166.4 3.8 %copy-start.7 = (bf16[2048,256]{1,0:T(8,128)(2,1)}, bf16[2048,256]{1,0:T(8,128)(2,1)S(1)}, u32[]{:S(2)}) copy-start(bf16[2048,256]{1,0:T(8,128)(2,1)S(1)} %collective-permute-done.8.refs_1_.refs_15_) | copy-start | bytes 3145732
  170.2 17.7 %copy-start.10 = (bf16[2048,128]{1,0:T(8,128)(2,1)S(1)}, bf16[2048,128]{1,0:T(8,128)(2,1)}, u32[]{:S(2)}) copy-start(bf16[2048,128]{1,0:T(8,128)(2,1)} %copy-done.9) | copy-start | bytes 1572868
  170.2 17.7 %copy-start.12 = (bf16[128,2048]{1,0:T(8,128)(2,1)S(1)}, bf16[128,2048]{1,0:T(8,128)(2,1)}, u32[]{:S(2)}) copy-start(bf16[128,2048]{1,0:T(8,128)(2,1)} %copy-done.11) | copy-start | bytes 1572868
  170.2 16.9 %collective-permute-start.16 = (bf16[2048,128]{1,0:T(8,128)(2,1)S(1)}, bf16[2048,128]{1,0:T(8,128)(2,1)S(1)}, u32[]{:S(2)}, u32[]{:S(2)}) collective-permute-start(bf16[2048,128]{1,0:T(8,128)(2,1)S(1)} %get-tuple-element.18.in_ref), channel_id=1, source_target_pairs={{16,1},{17,0},{32,17},{33,16},{48,33},{49,32},{64,49},{65,48},{80,... | collective-permute-start | bytes 1572872 | tf_op jit(solution)/shard_map/ppermute | solution.py:362
  173.8 14.1 %collective-permute-start.15 = (bf16[2048,128]{1,0:T(8,128)(2,1)S(1)}, bf16[2048,128]{1,0:T(8,128)(2,1)S(1)}, u32[]{:S(2)}, u32[]{:S(2)}) collective-permute-start(bf16[2048,128]{1,0:T(8,128)(2,1)S(1)} %get-tuple-element.18.in_ref), channel_id=1, source_target_pairs={{16,0},{32,16},{48,32},{64,48},{80,64},{96,80},{112,96},{128,112},... | collective-permute-start | bytes 1572872 | tf_op jit(solution)/shard_map/ppermute | solution.py:361
  187.9 16.5 %copy-start.20 = (bf16[2048,128]{1,0:T(8,128)(2,1)S(1)}, bf16[2048,128]{1,0:T(8,128)(2,1)}, u32[]{:S(2)}) copy-start(bf16[2048,128]{1,0:T(8,128)(2,1)} %copy-done.19) | copy-start | bytes 1572868
  198.6 14.2 %all-to-all-start = ((f32[8,16,128]{2,1,0:T(8,128)}), f32[8,16,128]{2,1,0:T(8,128)S(1)}, u32[]{:S(2)}, u32[]{:S(2)}) async-start(f32[8,16,128]{2,1,0:T(8,128)} %bitcast.17), calls=%async_computation | async-start | bytes 131072 | tf_op jit(solution)/shard_map/all_to_all | solution.py:370
  (10 other events, 9.9 us)

commit v4 on v3

--- a/solution.py
+++ b/solution.py
@@ -111,20 +111,30 @@
     shape_back(adj, own_ref[...], k_ref[...], toe_ref, out_ref, per)
 
 
-def last_kernel(offsets, per, place_ref, own_ref, other_ref, *refs):
-    count = len(offsets)
-    q_ref, late_ref, term_ref, _, adj_ref, sum_ref, g_ref, acc_ref, lag_ref, held_ref, sems = refs[count:]
-    copies = [pltpu.make_async_copy(refs[i], held_ref.at[i], sems.at[i]) for i in range(count)]
+def second_kernel(offsets, per, place_ref, g_ref, *refs):
+    *given, _, out_ref, adj_ref = refs
+    first_kernel(offsets, per, place_ref, g_ref, *given, out_ref, adj_ref)
+
+
+def last_kernel(offsets, pieces, per, place_ref, own_lo, own_hi, other_lo, other_hi, *refs):
+    q_ref, late_ref, term_ref, adj_ref, sum_ref, g_ref, acc_ref, lag_ref, held_ref, sems = refs[len(pieces) :]
+    copies = [
+        pltpu.make_async_copy(refs[n], held_ref.at[i, row : row + rows, :], sems.at[n])
+        for n, (i, row, rows) in enumerate(pieces)
+    ]
     for copy in copies:
         copy.start()
-    parts = own_ref.shape[0]
-    g_ref[pl.ds(place_ref[1] * parts, parts)] = own_ref[...]
-    g_ref[pl.ds((1 - place_ref[1]) * parts, parts)] = other_ref[...]
+    parts = own_lo.shape[0]
+    for side, lo, hi in ((place_ref[1], own_lo, own_hi), (1 - place_ref[1], other_lo, other_hi)):
+        g_ref[pl.ds(side * 2 * parts, parts)] = lo[...]
+        g_ref[pl.ds(side * 2 * parts + parts, parts)] = hi[...]
     width, seqlen = acc_ref.shape
     peers, depth = g_ref.shape[0], held_ref.shape[2]
     for i, (offset, first) in enumerate(offsets):
         g = g_ref[lax.rem(place_ref[0] + (offset + peers), peers), first : first + depth, :]
-        copies[i].wait()
+        for copy, piece in zip(copies, pieces):
+            if piece[0] == i:
+                copy.wait()
         for row in range(0, width, width // 2):
             at = slice(row, row + width // 2)
             part = jnp.dot(held_ref[i, at, :], g, preferred_element_type=jnp.float32)
@@ -138,21 +148,25 @@
     sum_ref[...] = lag_ref[...].T
 
 
-def lags_kernel(per, adj_ref, late_ref, out_ref):
-    width, seqlen = adj_ref.shape
+def lags_kernel(per, adj_lo, adj_hi, late_ref, out_ref):
+    width, seqlen = adj_lo.shape
+    adj = jnp.where(pl.program_id(0) < pl.num_programs(0) // 2, adj_lo[...], adj_hi[...])
     for row in range(0, width, seqlen):
         at = slice(row, row + seqlen)
-        out_ref[row // per : (row + seqlen) // per, :] = correlate(adj_ref[at, :], late_ref[:, at], per)
-
-
-def turn_kernel(in_ref, out_ref):
-    width, seqlen = in_ref.shape
-    for row in range(0, width, seqlen):
-        out_ref[0, :, row : row + seqlen] = in_ref[row : row + seqlen, :].T
-
-
-def finish_kernel(per, adj_ref, own_ref, k_ref, toe_ref, held_ref, out_ref, back_ref):
-    shape_back(adj_ref[...], own_ref[...], k_ref[...], toe_ref, back_ref, per)
+        out_ref[row // per : (row + seqlen) // per, :] = correlate(adj[at, :], late_ref[:, at], per)
+
+
+def turn_kernel(lo_ref, hi_ref, out_ref):
+    width, seqlen = lo_ref.shape
+    for side, ref in enumerate((lo_ref, hi_ref)):
+        for row in range(0, width, seqlen):
+            to = side * width + row
+            out_ref[0, :, to : to + seqlen] = ref[row : row + seqlen, :].T
+
+
+def finish_kernel(per, adj_ref, own_lo, own_hi, k_ref, toe_ref, held_ref, out_ref, back_ref):
+    own = jnp.where(pl.program_id(0) < pl.num_programs(0) // 2, own_lo[...], own_hi[...])
+    shape_back(adj_ref[...], own, k_ref[...], toe_ref, back_ref, per)
     width, seqlen = back_ref.shape
     for row in range(0, width, seqlen):
         out_ref[0, :, row : row + seqlen] = back_ref[row : row + seqlen, :].T
@@ -201,91 +215,122 @@
     )
 
 
-def first_part(place, g, offsets, panels, acc, own, q, k, toe, per):
+def first_part(place, g, offsets, panels, acc, own, q, k, toe, arrived, per):
     seqlen = g.shape[2]
-    at = chan(seqlen)
-    return call(
-        functools.partial(first_kernel, offsets, per), place, [g], panels, [acc, own, q, k, toe],
-        [at, at, at, at, grouped(toe.shape[1:], per)], [at] * 2,
-        [jax.ShapeDtypeStruct(own.shape, jnp.bfloat16)] * 2, "first_tick",
-    )
-
-
-def last_part(place, own, other, offsets, panels, q, late, term, ready, per):
-    parts, depth, seqlen = own.shape
-    width, across = panels[0].shape
+    width = own.shape[0]
+    half = width // 2 // BLOCK
+    skip = half if arrived else 0
+    piece = jax.ShapeDtypeStruct((width // 2, seqlen), jnp.bfloat16)
+    size = sum(p.size for p in panels)
+    return pl.pallas_call(
+        functools.partial(second_kernel if arrived else first_kernel, offsets, per),
+        grid_spec=pltpu.PrefetchScalarGridSpec(
+            num_scalar_prefetch=1,
+            grid=(half,),
+            in_specs=[whole_spec(g.shape)]
+            + [pl.BlockSpec((BLOCK, p.shape[1]), lambda i, *_: (i, 0)) for p in panels]
+            + [pl.BlockSpec((BLOCK, seqlen), lambda i, *_: (i + skip, 0))] * 4
+            + [pl.BlockSpec((BLOCK // per, *toe.shape[1:]), lambda i, *_: (i + skip, 0, 0))]
+            + [pl.BlockSpec(memory_space=pl.ANY)] * len(arrived),
+            out_specs=[chan(seqlen)] * 2,
+        ),
+        out_shape=[piece] * 2,
+        compiler_params=pltpu.CompilerParams(vmem_limit_bytes=VMEM),
+        cost_estimate=pl.CostEstimate(flops=2 * size * seqlen, bytes_accessed=2 * size, transcendentals=0),
+        name="first_tick_upper" if arrived else "first_tick_lower",
+    )(place, g, *panels, acc, own, q, k, toe, *arrived)
+
+
+def last_part(place, sides, offsets, panels, q, late, term, per):
+    parts, depth, seqlen = sides[0].shape
+    width = q.shape[0]
     groups = width // per
-    size = sum(p.size for p in panels)
-    anywhere = pl.BlockSpec(memory_space=pl.ANY)
-    return pl.pallas_call(
-        functools.partial(last_kernel, offsets, per),
+    flat, pieces = [], []
+    for i, panel in enumerate(panels):
+        row = 0
+        for piece in panel:
+            flat.append(piece)
+            pieces.append((i, row, piece.shape[0]))
+            row += piece.shape[0]
+    across = flat[0].shape[1]
+    size = sum(p.size for p in flat)
+    return pl.pallas_call(
+        functools.partial(last_kernel, offsets, tuple(pieces), per),
         grid_spec=pltpu.PrefetchScalarGridSpec(
             num_scalar_prefetch=1,
             grid=(1,),
-            in_specs=[whole_spec(own.shape)] * 2
-            + [anywhere] * len(panels)
-            + [whole_spec(q.shape), whole_spec(late.shape), whole_spec(term.shape), anywhere],
+            in_specs=[whole_spec(side.shape) for side in sides]
+            + [pl.BlockSpec(memory_space=pl.ANY)] * len(flat)
+            + [whole_spec(q.shape), whole_spec(late.shape), whole_spec(term.shape)],
             out_specs=[whole_spec(q.shape), whole_spec((seqlen, groups))],
             scratch_shapes=[
-                pltpu.VMEM((2 * parts, depth, seqlen), jnp.bfloat16),
+                pltpu.VMEM((4 * parts, depth, seqlen), jnp.bfloat16),
                 pltpu.VMEM((width, seqlen), jnp.float32),
                 pltpu.VMEM((groups, seqlen), jnp.float32),
                 pltpu.VMEM((len(panels), width, across), jnp.bfloat16),
-                pltpu.SemaphoreType.DMA((len(panels),)),
+                pltpu.SemaphoreType.DMA((len(flat),)),
             ],
         ),
         out_shape=[jax.ShapeDtypeStruct(q.shape, jnp.bfloat16), jax.ShapeDtypeStruct((seqlen, groups), jnp.float32)],
         compiler_params=pltpu.CompilerParams(vmem_limit_bytes=VMEM),
         cost_estimate=pl.CostEstimate(flops=2 * size * seqlen, bytes_accessed=2 * size, transcendentals=0),
         name="last_tick",
-    )(place, own, other, *panels, q, late, term, ready)
+    )(place, *sides, *flat, q, late, term)
 
 
 def small_cost(width, seqlen):
     return pl.CostEstimate(flops=width * seqlen * seqlen * 8, bytes_accessed=8 * width * seqlen, transcendentals=0)
 
 
-def lags(adj, late, per):
-    width, seqlen = adj.shape
+def lags(adj_lo, adj_hi, late, per):
+    seqlen, width = late.shape
+    half = width // 2 // BLOCK
     return pl.pallas_call(
         functools.partial(lags_kernel, per),
         grid=(width // BLOCK,),
-        in_specs=[chan(seqlen), pl.BlockSpec((seqlen, BLOCK), lambda i: (0, i))],
-        out_specs=grouped((seqlen,), per),
+        in_specs=[
+            pl.BlockSpec((BLOCK, seqlen), lambda i: (jnp.minimum(i, half - 1), 0)),
+            pl.BlockSpec((BLOCK, seqlen), lambda i: (jnp.maximum(i - half, 0), 0)),
+            pl.BlockSpec((seqlen, BLOCK), lambda i: (0, i)),
+        ],
+        out_specs=pl.BlockSpec((BLOCK // per, seqlen), lambda i: (i, 0)),
         out_shape=jax.ShapeDtypeStruct((width // per, seqlen), jnp.float32),
         compiler_params=pltpu.CompilerParams(vmem_limit_bytes=VMEM),
         cost_estimate=small_cost(width, seqlen),
         name="lags",
-    )(adj, late)
-
-
-def turn(value, ticks):
-    width, seqlen = value.shape
+    )(adj_lo, adj_hi, late)
+
+
+def turn(lo, hi, ticks):
+    rows, seqlen = lo.shape
     return pl.pallas_call(
         turn_kernel,
         grid=(1,),
-        in_specs=[whole_spec(value.shape)],
-        out_specs=pl.BlockSpec((1, seqlen, width), lambda i: (0, 0, 0)),
-        out_shape=jax.ShapeDtypeStruct((ticks, seqlen, width), jnp.bfloat16),
+        in_specs=[whole_spec(lo.shape)] * 2,
+        out_specs=pl.BlockSpec((1, seqlen, 2 * rows), lambda i: (0, 0, 0)),
+        out_shape=jax.ShapeDtypeStruct((ticks, seqlen, 2 * rows), jnp.bfloat16),
         compiler_params=pltpu.CompilerParams(vmem_limit_bytes=VMEM),
         name="turn",
-    )(value)
-
-
-def finish(adj, own, k, toe, held, tick, per):
+    )(lo, hi)
+
+
+def finish(adj, own_lo, own_hi, k, toe, held, tick, per):
     width, seqlen = adj.shape
+    half = width // 2 // BLOCK
+    below = pl.BlockSpec((BLOCK, seqlen), lambda i: (jnp.minimum(i, half - 1), 0))
+    above = pl.BlockSpec((BLOCK, seqlen), lambda i: (jnp.maximum(i - half, 0), 0))
     return pl.pallas_call(
         functools.partial(finish_kernel, per),
         grid=(width // BLOCK,),
-        in_specs=[chan(seqlen)] * 3 + [grouped(toe.shape[1:], per), pl.BlockSpec(memory_space=pl.ANY)],
+        in_specs=[chan(seqlen), below, above, chan(seqlen)] + [grouped(toe.shape[1:], per), pl.BlockSpec(memory_space=pl.ANY)],
         out_specs=pl.BlockSpec((1, seqlen, BLOCK), lambda i: (tick, 0, i)),
         out_shape=jax.ShapeDtypeStruct(held.shape, jnp.bfloat16),
         scratch_shapes=[pltpu.VMEM((BLOCK, seqlen), jnp.bfloat16)],
-        input_output_aliases={4: 0},
+        input_output_aliases={5: 0},
         compiler_params=pltpu.CompilerParams(vmem_limit_bytes=VMEM),
         cost_estimate=small_cost(width, seqlen),
         name="finish",
-    )(adj, own, k, toe, held)
+    )(adj, own_lo, own_hi, k, toe, held)
 
 
 def after_kernel(*refs):
@@ -326,10 +371,8 @@
     panels = {(0, first): weight[0, :, first : first + half] for first in (0, half)}
 
     def circulate(step, first):
-        if step < 4 or first == 0:
-            panels[-step, first] = round_ring(panels[1 - step, first], 1)
-        if step < 4 or first == half:
-            panels[step, first] = round_ring(panels[step - 1, first], -1)
+        panels[-step, first] = round_ring(panels[1 - step, first], 1)
+        panels[step, first] = round_ring(panels[step - 1, first], -1)
 
     circulate(1, 0)
     circulate(1, half)
@@ -343,32 +386,44 @@
     panels[1, half] = after(panels[1, half], *ready[0], *ready[1], toe)
     circulate(2, 0)
     circulate(2, half)
-    for step in range(3, 5):
-        for first in (0, half):
-            circulate(step, first)
-
+    for first in (0, half):
+        circulate(3, first)
     def held(*steps):
         return [at for at in sorted(panels) if abs(at[0]) in steps]
 
     straight = [(s + 1, s) for s in range(sections - 1)]
     crossed = [((s + 1) * 2 + h, s * 2 + 1 - h) for s in range(sections - 1) for h in range(2)]
     acc = None
-    for steps in ((0, 1), (2,), (3,)):
+    for steps in ((0, 1), (2,)):
         near = held(*steps)
         acc = partial(place, whole, near, [panels[at] for at in near], acc)
-    far = held(4)
-    out, adj = first_part(place, whole, far, [panels[at] for at in far], acc, own, q[0], k[0], toe, per)
-    own = lax.ppermute(out, "pipe", straight)
-    other = lax.ppermute(out, ("pipe", "tp"), crossed)
-    term = lags(adj, late[0], per)
-    grads = turn(out, ticks)
-    every = held(0, 1, 2, 3, 4)
+    rows = width // 2
+    far = {}
+    for by, first in ((1, 0), (-1, half)):
+        source = panels[by * -3, first]
+        far[by * -4, first] = [round_ring(source[:rows], by), round_ring(after(source[rows:], acc), by)]
+    near = held(3)
+    acc = partial(place, whole, near, [panels[at] for at in near], acc)
+    ends = sorted(far)
+    out_lo, adj_lo = first_part(
+        place, whole, ends, [far[at][0] for at in ends], acc, own, q[0], k[0], toe, (), per
+    )
+    other_lo = lax.ppermute(out_lo, ("pipe", "tp"), crossed)
+    own_lo = lax.ppermute(out_lo, "pipe", straight)
+    out_hi, adj_hi = first_part(
+        place, whole, ends, [far[at][1] for at in ends], acc, own, q[0], k[0], toe, (other_lo,), per
+    )
+    other_hi = lax.ppermute(out_hi, ("pipe", "tp"), crossed)
+    own_hi = lax.ppermute(out_hi, "pipe", straight)
+    term = lags(adj_lo, adj_hi, late[0], per)
+    grads = turn(out_lo, out_hi, ticks)
+    near = held(0, 1, 2, 3)
     adj, total = last_part(
-        place, own.reshape(-1, depth, seqlen), other.reshape(-1, depth, seqlen), every, [panels[at] for at in every],
-        q[1], late[1], term, grads, per,
+        place, [x.reshape(-1, depth, seqlen) for x in (own_lo, own_hi, other_lo, other_hi)],
+        near + ends, [[panels[at]] for at in near] + [far[at] for at in ends], q[1], late[1], term, per,
     )
     spread = lax.all_to_all(total.reshape(lax.axis_size("fsdp"), -1, groups), "fsdp", 0, 0, tiled=True)
-    grads = finish(adj, own, k[1], toe, grads, 1, per)
+    grads = finish(adj, own_lo, own_hi, k[1], toe, grads, 1, per)
     summed = jnp.sum(spread, axis=0) * scale
     return (grads[None, :, None], summed[None])
 

time: 215 us -> 214 us (level)
  waiting for transfers between devices: 115 us -> 101 us
  starting transfers between devices: 42 us -> 51.6 us
  Pallas kernels: 39.9 us -> 42.9 us
  local copies, waits for them, and re-layouts: 13.2 us -> 15.9 us
    ppermute x14 -> x16, waiting for transfers between devices: 106 us -> 81.6 us  [round_ring(): lax.ppermute(value, 'fsdp', [(i, (i + by) % peers) for i in range(peers)])]
    ppermute x1, waiting for transfers between devices: 0.01 us -> 9.76 us  [body(): other = lax.ppermute(own, 'tp', [(0, 1), (1, 0)])]
    ppermute x2 -> x4, starting transfers between devices: 7.17 us -> 15.1 us  [the longest x1 5.86 us: body(): own_hi = lax.ppermute(out_hi, 'pipe', straight)]
    pallas_call x2 -> x4, Pallas kernels: 10.9 us -> 17.5 us  [the longest x1 10.2 us: last_part(): pl.pallas_call(functools.partial(last_kernel, offsets, tuple(pieces), per...]
    ppermute x14 -> x16, starting transfers between devices: 25.9 us -> 30.1 us  [round_ring(): lax.ppermute(value, 'fsdp', [(i, (i + by) % peers) for i in range(peers)])]
    pallas_call x4 -> x3, Pallas kernels: 16.8 us -> 13.2 us  [call(): pl.pallas_call(kernel, grid_spec=pltpu.PrefetchScalarGridSpec(num_scalar_...]
    slice x0 -> x2, local copies, waits for them, and re-layouts: none -> 3.51 us  [body(): source[rows:]]
    all_to_all x1, starting transfers between devices: 5.83 us -> 3.36 us  [body(): lax.all_to_all(total.reshape(lax.axis_size('fsdp'), -1, groups), 'fsdp',...]
  transfers between devices with their start and end apart: 18 -> 22, of which waited for: 10 -> 12; matrix products, arithmetic and copies ran while one was open for 2% -> 3% of each run, Pallas kernels for 12% -> 15%
where the time goes in v4:
time: 214 us
  waiting for transfers between devices  101 us (47%)
  starting transfers between devices  51.6 us (24%)
  Pallas kernels  42.9 us (20%)
  local copies, waits for them, and re-layouts  15.9 us (7%)
    ppermute x16, waiting for transfers between devices, round_ring(): lax.ppermute(value, 'fsdp', [(i, (i + by) % peers) for i in range(peers)])  81.6 us
    ppermute x16, starting transfers between devices, round_ring(): lax.ppermute(value, 'fsdp', [(i, (i + by) % peers) for i in range(peers)])  30.1 us
    pallas_call x3, Pallas kernels, call(): pl.pallas_call(kernel, grid_spec=pltpu.PrefetchScalarGridSpec(num_scalar_...  13.2 us
    unnamed x64, local copies, waits for them, and re-layouts  10.5 us
    pallas_call x1, Pallas kernels, last_part(): pl.pallas_call(functools.partial(last_kernel, offsets, tuple(pieces), per...  10.2 us
    ppermute x1, waiting for transfers between devices, body(): other = lax.ppermute(own, 'tp', [(0, 1), (1, 0)])  9.76 us
    pallas_call x2, Pallas kernels, first_part(): pl.pallas_call(functools.partial(second_kernel if arrived else first_kern...  6.32 us
    ppermute x1, starting transfers between devices, body(): own_hi = lax.ppermute(out_hi, 'pipe', straight)  5.86 us
  transfers between devices with their start and end apart: 22, of which 12 were waited for; matrix products, arithmetic and copies ran while one was open for 3% of the time, Pallas kernels for 15%

profile of v4, /device:TPU:16, one launch (start us, length us, event | category | flops | bytes accessed | tf_op | source)
XLA Modules:
  0.0 213.6 jit_solution(9996077628262899124)
XLA Ops:
  2.5 5.9 %collective-permute-start.5 = (bf16[2048,256]{1,0:T(8,128)(2,1)S(1)}, bf16[2048,256]{1,0:T(8,128)(2,1)S(1)}, u32[]{:S(2)}, u32[]{:S(2)}) collective-permute-start(bf16[2048,256]{1,0:T(8,128)(2,1)S(1)} %get-tuple-element.28.refs_3_.refs_7_), channel_id=1, source_target_pairs={{0,14},{2,0},{4,2},{6,4},{8,6},{10,8},{12,10},{14,12},{1,15},{3,1}... | collective-permute-start | bytes 3145736 | tf_op jit(solution)/shard_map/ppermute | solution.py:358
  8.4 3.2 %collective-permute-start.12 = (bf16[2048,256]{1,0:T(8,128)(2,1)S(1)}, bf16[2048,256]{1,0:T(8,128)(2,1)}, u32[]{:S(2)}, u32[]{:S(2)}) collective-permute-start(bf16[2048,256]{1,0:T(8,128)(2,1)S(1)} %get-tuple-element.29.refs_2_.refs_6_), channel_id=1, source_target_pairs={{0,14},{2,0},{4,2},{6,4},{8,6},{10,8},{12,10},{14,12},{1,15},{3,1}... | collective-permute-start | bytes 3145736 | tf_op jit(solution)/shard_map/ppermute | solution.py:358
  18.3 5.5 %toeplitz.1.refs_7_.refs_6_.toe_ref = bf16[128,128,128]{2,1,0:T(8,128)(2,1)} custom-call(f32[128,128]{1,0:T(8,128)} %convert_bitcast_fusion.rows_ref), custom_call_target="tpu_custom_call" | custom-call | tf_op jit(solution)/shard_map/toeplitz/pallas_call | solution.py:27
  23.8 8.2 %collective-permute-done.5.refs_0_ = bf16[2048,256]{1,0:T(8,128)(2,1)S(1)} collective-permute-done((bf16[2048,256]{1,0:T(8,128)(2,1)S(1)}, bf16[2048,256]{1,0:T(8,128)(2,1)S(1)}, u32[]{:S(2)}, u32[]{:S(2)}) %collective-permute-start.5) | collective-permute-done | bytes 1048608 | tf_op jit(solution)/shard_map/ppermute | solution.py:358
  33.0 3.7 %collective-permute-start.6 = (bf16[2048,256]{1,0:T(8,128)(2,1)}, bf16[2048,256]{1,0:T(8,128)(2,1)}, u32[]{:S(2)}, u32[]{:S(2)}) collective-permute-start(bf16[2048,256]{1,0:T(8,128)(2,1)} %after.3.refs_5_.refs_9_), channel_id=1, source_target_pairs={{0,14},{2,0},{4,2},{6,4},{8,6},{10,8},{12,10},{14,12},{1,15},{3,1}... | collective-permute-start | bytes 3145736 | tf_op jit(solution)/shard_map/ppermute | solution.py:358
  36.7 21.6 %collective-permute-done.9.refs_1_.refs_5_ = bf16[2048,256]{1,0:T(8,128)(2,1)} collective-permute-done((bf16[2048,256]{1,0:T(8,128)(2,1)S(1)}, bf16[2048,256]{1,0:T(8,128)(2,1)}, u32[]{:S(2)}, u32[]{:S(2)}) %collective-permute-start.9) | collective-permute-done | bytes 1048608 | tf_op jit(solution)/shard_map/ppermute | solution.py:358
  58.3 3.2 %collective-permute-start.13 = (bf16[2048,256]{1,0:T(8,128)(2,1)}, bf16[2048,256]{1,0:T(8,128)(2,1)}, u32[]{:S(2)}, u32[]{:S(2)}) collective-permute-start(bf16[2048,256]{1,0:T(8,128)(2,1)} %collective-permute-done.12.refs_4_.refs_8_), channel_id=1, source_target_pairs={{0,14},{2,0},{4,2},{6,4},{8,6},{10,8},{12,10},{14,12},{1,15},{3,1}... | collective-permute-start | bytes 3145736 | tf_op jit(solution)/shard_map/ppermute | solution.py:358
  61.6 15.5 %collective-permute-done.6.refs_3_.refs_11_ = bf16[2048,256]{1,0:T(8,128)(2,1)} collective-permute-done((bf16[2048,256]{1,0:T(8,128)(2,1)}, bf16[2048,256]{1,0:T(8,128)(2,1)}, u32[]{:S(2)}, u32[]{:S(2)}) %collective-permute-start.6) | collective-permute-done | bytes 1048608 | tf_op jit(solution)/shard_map/ppermute | solution.py:358
  77.1 3.7 %collective-permute-start.7 = (bf16[2048,256]{1,0:T(8,128)(2,1)}, bf16[2048,256]{1,0:T(8,128)(2,1)S(1)}, u32[]{:S(2)}, u32[]{:S(2)}) collective-permute-start(bf16[2048,256]{1,0:T(8,128)(2,1)} %collective-permute-done.6.refs_3_.refs_11_), channel_id=1, source_target_pairs={{0,14},{2,0},{4,2},{6,4},{8,6},{10,8},{12,10},{14,12},{1,15},{3,1}... | collective-permute-start | bytes 3145736 | tf_op jit(solution)/shard_map/ppermute | solution.py:358
  82.1 3.1 %collective-permute-start = (bf16[2048,128]{1,0:T(8,128)(2,1)S(1)}, bf16[2048,128]{1,0:T(8,128)(2,1)S(1)}, u32[]{:S(2)}, u32[]{:S(2)}) collective-permute-start(bf16[2048,128]{1,0:T(8,128)(2,1)S(1)} %bitcast.35), channel_id=1, source_target_pairs={{0,1},{1,0},{2,3},{3,2},{4,5},{5,4},{6,7},{7,6},{8,9},{9,8},{10,11... | collective-permute-start | bytes 1572872 | tf_op jit(solution)/shard_map/ppermute | solution.py:380
  85.3 9.8 %collective-permute-done = bf16[2048,128]{1,0:T(8,128)(2,1)S(1)} collective-permute-done((bf16[2048,128]{1,0:T(8,128)(2,1)S(1)}, bf16[2048,128]{1,0:T(8,128)(2,1)S(1)}, u32[]{:S(2)}, u32[]{:S(2)}) %collective-permute-start) | collective-permute-done | bytes 524320 | tf_op jit(solution)/shard_map/ppermute | solution.py:380
  95.1 8.1 %collective-permute-done.10.refs_1_.refs_3_ = bf16[2048,256]{1,0:T(8,128)(2,1)} collective-permute-done((bf16[2048,256]{1,0:T(8,128)(2,1)}, bf16[2048,256]{1,0:T(8,128)(2,1)}, u32[]{:S(2)}, u32[]{:S(2)}) %collective-permute-start.10) | collective-permute-done | bytes 1048608 | tf_op jit(solution)/shard_map/ppermute | solution.py:358
  103.3 3.2 %collective-permute-start.14 = (bf16[2048,256]{1,0:T(8,128)(2,1)}, bf16[2048,256]{1,0:T(8,128)(2,1)}, u32[]{:S(2)}, u32[]{:S(2)}) collective-permute-start(bf16[2048,256]{1,0:T(8,128)(2,1)} %collective-permute-done.13.refs_2_.refs_10_), channel_id=1, source_target_pairs={{0,14},{2,0},{4,2},{6,4},{8,6},{10,8},{12,10},{14,12},{1,15},{3,1}... | collective-permute-start | bytes 3145736 | tf_op jit(solution)/shard_map/ppermute | solution.py:358
  106.5 15.5 %collective-permute-done.7.refs_3_.refs_13_ = bf16[2048,256]{1,0:T(8,128)(2,1)S(1)} collective-permute-done((bf16[2048,256]{1,0:T(8,128)(2,1)}, bf16[2048,256]{1,0:T(8,128)(2,1)S(1)}, u32[]{:S(2)}, u32[]{:S(2)}) %collective-permute-start.7) | collective-permute-done | bytes 1048608 | tf_op jit(solution)/shard_map/ppermute | solution.py:358
  123.2 3.8 %collective-permute-start.8 = (bf16[1024,256]{1,0:T(8,128)(2,1)}, bf16[1024,256]{1,0:T(8,128)(2,1)}, u32[]{:S(2)}, u32[]{:S(2)}) collective-permute-start(bf16[1024,256]{1,0:T(8,128)(2,1)} %get-tuple-element.31), channel_id=1, source_target_pairs={{0,14},{2,0},{4,2},{6,4},{8,6},{10,8},{12,10},{14,12},{1,15},{3,1}... | collective-permute-start | bytes 1572872 | tf_op jit(solution)/shard_map/ppermute | solution.py:358
  129.4 4.6 %partial_sums.3.refs_4_ = f32[2048,128]{1,0:T(8,128)S(1)} custom-call(s32[2]{0:T(128)S(1)} %pad_add_fusion.place_ref, bf16[8,512,128]{2,1,0:T(8,128)(2,1)S(1)} %bitcast.30, bf16[2048,256]{1,0:T(8,128)(2,1)} %collective-permute-done.1.refs_0_.refs_4_, bf16[2048,256]{1,0:T(8,128)(2,1)} %collective-permute-done.9.refs_1_.refs_5_, ...), custom_call_target="tpu_custom_call" | custom-call | flops 805306368 | bytes 6291456 | tf_op jit(solution)/shard_map/partial_sums/pallas_call | solution.py:191
  134.0 4.4 %partial_sums.4.refs_4_.refs_1_ = f32[2048,128]{1,0:T(8,128)S(1)} custom-call(s32[2]{0:T(128)S(1)} %pad_add_fusion.place_ref, bf16[8,512,128]{2,1,0:T(8,128)(2,1)S(1)} %bitcast.31, bf16[2048,256]{1,0:T(8,128)(2,1)} %collective-permute-done.2.refs_0_.refs_2_, bf16[2048,256]{1,0:T(8,128)(2,1)} %collective-permute-done.10.refs_1_.refs_3_, ...), custom_call_target="tpu_custom_call" | custom-call | flops 536870912 | bytes 4194304 | tf_op jit(solution)/shard_map/partial_sums/pallas_call | solution.py:191
  139.4 3.2 %collective-permute-start.17 = (bf16[1024,256]{1,0:T(8,128)(2,1)}, bf16[1024,256]{1,0:T(8,128)(2,1)}, u32[]{:S(2)}, u32[]{:S(2)}) collective-permute-start(bf16[1024,256]{1,0:T(8,128)(2,1)} %after.5), channel_id=1, source_target_pairs={{0,14},{2,0},{4,2},{6,4},{8,6},{10,8},{12,10},{14,12},{1,15},{3,1}... | collective-permute-start | bytes 1572872 | tf_op jit(solution)/shard_map/ppermute | solution.py:358
  142.7 5.5 %collective-permute-done.11.refs_1_ = bf16[2048,256]{1,0:T(8,128)(2,1)} collective-permute-done((bf16[2048,256]{1,0:T(8,128)(2,1)}, bf16[2048,256]{1,0:T(8,128)(2,1)}, u32[]{:S(2)}, u32[]{:S(2)}) %collective-permute-start.11) | collective-permute-done | bytes 1048608 | tf_op jit(solution)/shard_map/ppermute | solution.py:358
  148.2 4.2 %partial_sums.5.refs_2_ = f32[2048,128]{1,0:T(8,128)S(1)} custom-call(s32[2]{0:T(128)S(1)} %pad_add_fusion.place_ref, bf16[8,512,128]{2,1,0:T(8,128)(2,1)S(1)} %bitcast.32, bf16[2048,256]{1,0:T(8,128)(2,1)} %collective-permute-done.3.refs_0_, bf16[2048,256]{1,0:T(8,128)(2,1)} %collective-permute-done.11.refs_1_, ...), custom_call_target="tpu_custom_call" | custom-call | flops 536870912 | bytes 4194304 | tf_op jit(solution)/shard_map/partial_sums/pallas_call | solution.py:191
  152.4 3.3 %collective-permute-done.8.refs_1_.refs_16_ = bf16[1024,256]{1,0:T(8,128)(2,1)} collective-permute-done((bf16[1024,256]{1,0:T(8,128)(2,1)}, bf16[1024,256]{1,0:T(8,128)(2,1)}, u32[]{:S(2)}, u32[]{:S(2)}) %collective-permute-start.8) | collective-permute-done | bytes 524320 | tf_op jit(solution)/shard_map/ppermute | solution.py:358
  155.7 3.7 %collective-permute-done.4.refs_0_.refs_14_ = bf16[1024,256]{1,0:T(8,128)(2,1)} collective-permute-done((bf16[1024,256]{1,0:T(8,128)(2,1)}, bf16[1024,256]{1,0:T(8,128)(2,1)}, u32[]{:S(2)}, u32[]{:S(2)}) %collective-permute-start.4) | collective-permute-done | bytes 524320 | tf_op jit(solution)/shard_map/ppermute | solution.py:358
  159.5 3.2 %first_tick_lower.1 = (bf16[1024,128]{1,0:T(8,128)(2,1)S(1)}, bf16[1024,128]{1,0:T(8,128)(2,1)S(1)}) custom-call(s32[2]{0:T(128)S(1)} %pad_add_fusion.place_ref, bf16[8,512,128]{2,1,0:T(8,128)(2,1)S(1)} %bitcast.33, bf16[1024,256]{1,0:T(8,128)(2,1)} %collective-permute-done.4.refs_0_.refs_14_, bf16[1024,256]{1,0:T(8,128)(2,1)} %collective-permute-done.8.refs_1_.refs_16_, ...), custom_call_target="tpu_custom_call" | custom-call | flops 134217728 | bytes 1048576 | tf_op jit(solution)/shard_map/first_tick_lower/pallas_call | solution.py:225
  164.9 5.1 %collective-permute-start.15 = (bf16[1024,128]{1,0:T(8,128)(2,1)S(1)}, bf16[1024,128]{1,0:T(8,128)(2,1)S(1)}, u32[]{:S(2)}, u32[]{:S(2)}) collective-permute-start(bf16[1024,128]{1,0:T(8,128)(2,1)S(1)} %get-tuple-element.20.lo_ref), channel_id=1, source_target_pairs={{16,0},{32,16},{48,32},{64,48},{80,64},{96,80},{112,96},{128,112},... | collective-permute-start | bytes 786440 | tf_op jit(solution)/shard_map/ppermute | solution.py:412
  172.3 3.1 %first_tick_upper.1 = (bf16[1024,128]{1,0:T(8,128)(2,1)S(1)}, bf16[1024,128]{1,0:T(8,128)(2,1)S(1)}) custom-call(s32[2]{0:T(128)S(1)} %pad_add_fusion.place_ref, bf16[8,512,128]{2,1,0:T(8,128)(2,1)S(1)} %bitcast.34, bf16[1024,256]{1,0:T(8,128)(2,1)S(1)} %collective-permute-done.16.refs_0_.refs_15_, ...), custom_call_target="tpu_custom_call" | custom-call | flops 134217728 | bytes 1048576 | tf_op jit(solution)/shard_map/first_tick_upper/pallas_call | solution.py:225
  175.4 5.9 %collective-permute-start.19 = (bf16[1024,128]{1,0:T(8,128)(2,1)S(1)}, bf16[1024,128]{1,0:T(8,128)(2,1)S(1)}, u32[]{:S(2)}, u32[]{:S(2)}) collective-permute-start(bf16[1024,128]{1,0:T(8,128)(2,1)S(1)} %get-tuple-element.21.hi_ref), channel_id=1, source_target_pairs={{16,0},{32,16},{48,32},{64,48},{80,64},{96,80},{112,96},{128,112},... | collective-permute-start | bytes 786440 | tf_op jit(solution)/shard_map/ppermute | solution.py:417
  183.2 3.2 %lags.1.refs_20_ = f32[128,128]{1,0:T(8,128)S(1)} custom-call(bf16[1024,128]{1,0:T(8,128)(2,1)S(1)} %get-tuple-element.22.adj_lo, bf16[1024,128]{1,0:T(8,128)(2,1)S(1)} %get-tuple-element.23.adj_hi, bf16[128,2048]{1,0:T(8,128)(2,1)S(1)} %copy-done.27), custom_call_target="tpu_custom_call" | custom-call | flops 268435456 | bytes 2097152 | tf_op jit(solution)/shard_map/lags/pallas_call | solution.py:288
  186.5 4.1 %collective-permute-done.20 = bf16[1024,128]{1,0:T(8,128)(2,1)S(1)} collective-permute-done((bf16[1024,128]{1,0:T(8,128)(2,1)S(1)}, bf16[1024,128]{1,0:T(8,128)(2,1)S(1)}, u32[]{:S(2)}, u32[]{:S(2)}) %collective-permute-start.20) | collective-permute-done | bytes 262176 | tf_op jit(solution)/shard_map/ppermute | solution.py:416
  190.6 10.2 %last_tick.1 = (bf16[2048,128]{1,0:T(8,128)(2,1)S(1)}, f32[128,128]{1,0:T(8,128)}) custom-call(s32[2]{0:T(128)S(1)} %pad_add_fusion.place_ref, bf16[2,512,128]{2,1,0:T(8,128)(2,1)S(1)} %bitcast.44, bf16[2,512,128]{2,1,0:T(8,128)(2,1)S(1)} %bitcast.46, bf16[2,512,128]{2,1,0:T(8,128)(2,1)S(1)} %bitcast.45, bf16[2,512,128]{2,1,0:T(8,128)(2,1)S(1)} %bitcast.47, ...), custom_call_target="tpu_custom_call" | custom-call | flops 2147483648 | bytes 16777216 | tf_op jit(solution)/shard_map/last_tick/pallas_call | solution.py:257
  200.8 3.4 %all-to-all-start = ((f32[8,16,128]{2,1,0:T(8,128)}), f32[8,16,128]{2,1,0:T(8,128)S(1)}, u32[]{:S(2)}, u32[]{:S(2)}) async-start(f32[8,16,128]{2,1,0:T(8,128)} %bitcast.19), calls=%async_computation | async-start | bytes 131072 | tf_op jit(solution)/shard_map/all_to_all | solution.py:425
  207.3 2.7 %finish.1 = bf16[2,128,2048]{2,1,0:T(8,128)(2,1)} custom-call(bf16[2048,128]{1,0:T(8,128)(2,1)S(1)} %get-tuple-element.24.adj_ref, bf16[1024,128]{1,0:T(8,128)(2,1)S(1)} %collective-permute-done.15.own_lo, bf16[1024,128]{1,0:T(8,128)(2,1)S(1)} %collective-permute-done.19.own_hi, bf16[2048,128]{1,0:T(8,128)(2,1)S(1)} %copy-done.29, ...), custom_call_target="tpu_custom_call", output_to_operand_aliasing={{}: (5, {})} | custom-call | flops 268435456 | bytes 2097152 | tf_op jit(solution)/shard_map/finish/pallas_call | solution.py:322
  210.0 2.9 %all-to-all-done = f32[8,16,128]{2,1,0:T(8,128)S(1)} async-done(((f32[8,16,128]{2,1,0:T(8,128)}), f32[8,16,128]{2,1,0:T(8,128)S(1)}, u32[]{:S(2)}, u32[]{:S(2)}) %all-to-all-start) | async-done | bytes 65568 | tf_op jit(solution)/shard_map/all_to_all | solution.py:425
  (101 shorter events, 25.6 us)
Async XLA Ops:
  2.5 126.9 %copy-start.6 = (bf16[2048,256]{1,0:T(8,128)(2,1)}, bf16[2048,256]{1,0:T(8,128)(2,1)S(1)}, u32[]{:S(2)}) copy-start(bf16[2048,256]{1,0:T(8,128)(2,1)S(1)} %get-tuple-element.28.refs_3_.refs_7_) | copy-start | bytes 3145732
  2.5 29.5 %collective-permute-start.5 = (bf16[2048,256]{1,0:T(8,128)(2,1)S(1)}, bf16[2048,256]{1,0:T(8,128)(2,1)S(1)}, u32[]{:S(2)}, u32[]{:S(2)}) collective-permute-start(bf16[2048,256]{1,0:T(8,128)(2,1)S(1)} %get-tuple-element.28.refs_3_.refs_7_), channel_id=1, source_target_pairs={{0,14},{2,0},{4,2},{6,4},{8,6},{10,8},{12,10},{14,12},{1,15},{3,1}... | collective-permute-start | bytes 3145736 | tf_op jit(solution)/shard_map/ppermute | solution.py:358
  8.4 28.2 %collective-permute-start.1 = (bf16[2048,256]{1,0:T(8,128)(2,1)S(1)}, bf16[2048,256]{1,0:T(8,128)(2,1)}, u32[]{:S(2)}, u32[]{:S(2)}) collective-permute-start(bf16[2048,256]{1,0:T(8,128)(2,1)S(1)} %get-tuple-element.29.refs_2_.refs_6_), channel_id=1, source_target_pairs={{0,2},{2,4},{4,6},{6,8},{8,10},{10,12},{12,14},{14,0},{1,3},{3,5},... | collective-permute-start | bytes 3145736 | tf_op jit(solution)/shard_map/ppermute | solution.py:358
  8.4 49.9 %collective-permute-start.12 = (bf16[2048,256]{1,0:T(8,128)(2,1)S(1)}, bf16[2048,256]{1,0:T(8,128)(2,1)}, u32[]{:S(2)}, u32[]{:S(2)}) collective-permute-start(bf16[2048,256]{1,0:T(8,128)(2,1)S(1)} %get-tuple-element.29.refs_2_.refs_6_), channel_id=1, source_target_pairs={{0,14},{2,0},{4,2},{6,4},{8,6},{10,8},{12,10},{14,12},{1,15},{3,1}... | collective-permute-start | bytes 3145736 | tf_op jit(solution)/shard_map/ppermute | solution.py:358
  11.7 46.6 %collective-permute-start.9 = (bf16[2048,256]{1,0:T(8,128)(2,1)S(1)}, bf16[2048,256]{1,0:T(8,128)(2,1)}, u32[]{:S(2)}, u32[]{:S(2)}) collective-permute-start(bf16[2048,256]{1,0:T(8,128)(2,1)S(1)} %get-tuple-element.28.refs_3_.refs_7_), channel_id=1, source_target_pairs={{0,2},{2,4},{4,6},{6,8},{8,10},{10,12},{12,14},{14,0},{1,3},{3,5},... | collective-permute-start | bytes 3145736 | tf_op jit(solution)/shard_map/ppermute | solution.py:358
  33.0 44.1 %collective-permute-start.6 = (bf16[2048,256]{1,0:T(8,128)(2,1)}, bf16[2048,256]{1,0:T(8,128)(2,1)}, u32[]{:S(2)}, u32[]{:S(2)}) collective-permute-start(bf16[2048,256]{1,0:T(8,128)(2,1)} %after.3.refs_5_.refs_9_), channel_id=1, source_target_pairs={{0,14},{2,0},{4,2},{6,4},{8,6},{10,8},{12,10},{14,12},{1,15},{3,1}... | collective-permute-start | bytes 3145736 | tf_op jit(solution)/shard_map/ppermute | solution.py:358
  36.7 48.5 %collective-permute-start.2 = (bf16[2048,256]{1,0:T(8,128)(2,1)}, bf16[2048,256]{1,0:T(8,128)(2,1)}, u32[]{:S(2)}, u32[]{:S(2)}) collective-permute-start(bf16[2048,256]{1,0:T(8,128)(2,1)} %collective-permute-done.1.refs_0_.refs_4_), channel_id=1, source_target_pairs={{0,2},{2,4},{4,6},{6,8},{8,10},{10,12},{12,14},{14,0},{1,3},{3,5},... | collective-permute-start | bytes 3145736 | tf_op jit(solution)/shard_map/ppermute | solution.py:358
  58.3 44.9 %collective-permute-start.10 = (bf16[2048,256]{1,0:T(8,128)(2,1)}, bf16[2048,256]{1,0:T(8,128)(2,1)}, u32[]{:S(2)}, u32[]{:S(2)}) collective-permute-start(bf16[2048,256]{1,0:T(8,128)(2,1)} %collective-permute-done.9.refs_1_.refs_5_), channel_id=1, source_target_pairs={{0,2},{2,4},{4,6},{6,8},{8,10},{10,12},{12,14},{14,0},{1,3},{3,5},... | collective-permute-start | bytes 3145736 | tf_op jit(solution)/shard_map/ppermute | solution.py:358
  58.3 44.9 %collective-permute-start.13 = (bf16[2048,256]{1,0:T(8,128)(2,1)}, bf16[2048,256]{1,0:T(8,128)(2,1)}, u32[]{:S(2)}, u32[]{:S(2)}) collective-permute-start(bf16[2048,256]{1,0:T(8,128)(2,1)} %collective-permute-done.12.refs_4_.refs_8_), channel_id=1, source_target_pairs={{0,14},{2,0},{4,2},{6,4},{8,6},{10,8},{12,10},{14,12},{1,15},{3,1}... | collective-permute-start | bytes 3145736 | tf_op jit(solution)/shard_map/ppermute | solution.py:358
  77.1 44.9 %collective-permute-start.7 = (bf16[2048,256]{1,0:T(8,128)(2,1)}, bf16[2048,256]{1,0:T(8,128)(2,1)S(1)}, u32[]{:S(2)}, u32[]{:S(2)}) collective-permute-start(bf16[2048,256]{1,0:T(8,128)(2,1)} %collective-permute-done.6.refs_3_.refs_11_), channel_id=1, source_target_pairs={{0,14},{2,0},{4,2},{6,4},{8,6},{10,8},{12,10},{14,12},{1,15},{3,1}... | collective-permute-start | bytes 3145736 | tf_op jit(solution)/shard_map/ppermute | solution.py:358
  82.1 41.1 %copy-start.13 = (bf16[1,1,128,2048]{2,3,1,0:T(8,128)(2,1)}, bf16[1,1,128,2048]{2,3,1,0:T(8,128)(2,1)S(1)}, u32[]{:S(2)}) copy-start(bf16[1,1,128,2048]{2,3,1,0:T(8,128)(2,1)S(1)} %copy.12) | copy-start | bytes 1572868
  82.1 13.0 %collective-permute-start = (bf16[2048,128]{1,0:T(8,128)(2,1)S(1)}, bf16[2048,128]{1,0:T(8,128)(2,1)S(1)}, u32[]{:S(2)}, u32[]{:S(2)}) collective-permute-start(bf16[2048,128]{1,0:T(8,128)(2,1)S(1)} %bitcast.35), channel_id=1, source_target_pairs={{0,1},{1,0},{2,3},{3,2},{4,5},{5,4},{6,7},{7,6},{8,9},{9,8},{10,11... | collective-permute-start | bytes 1572872 | tf_op jit(solution)/shard_map/ppermute | solution.py:380
  85.2 41.8 %collective-permute-start.3 = (bf16[2048,256]{1,0:T(8,128)(2,1)}, bf16[2048,256]{1,0:T(8,128)(2,1)}, u32[]{:S(2)}, u32[]{:S(2)}) collective-permute-start(bf16[2048,256]{1,0:T(8,128)(2,1)} %collective-permute-done.2.refs_0_.refs_2_), channel_id=1, source_target_pairs={{0,2},{2,4},{4,6},{6,8},{8,10},{10,12},{12,14},{14,0},{1,3},{3,5},... | collective-permute-start | bytes 3145736 | tf_op jit(solution)/shard_map/ppermute | solution.py:358
  103.3 44.9 %collective-permute-start.11 = (bf16[2048,256]{1,0:T(8,128)(2,1)}, bf16[2048,256]{1,0:T(8,128)(2,1)}, u32[]{:S(2)}, u32[]{:S(2)}) collective-permute-start(bf16[2048,256]{1,0:T(8,128)(2,1)} %collective-permute-done.10.refs_1_.refs_3_), channel_id=1, source_target_pairs={{0,2},{2,4},{4,6},{6,8},{8,10},{10,12},{12,14},{14,0},{1,3},{3,5},... | collective-permute-start | bytes 3145736 | tf_op jit(solution)/shard_map/ppermute | solution.py:358
  103.3 44.9 %collective-permute-start.14 = (bf16[2048,256]{1,0:T(8,128)(2,1)}, bf16[2048,256]{1,0:T(8,128)(2,1)}, u32[]{:S(2)}, u32[]{:S(2)}) collective-permute-start(bf16[2048,256]{1,0:T(8,128)(2,1)} %collective-permute-done.13.refs_2_.refs_10_), channel_id=1, source_target_pairs={{0,14},{2,0},{4,2},{6,4},{8,6},{10,8},{12,10},{14,12},{1,15},{3,1}... | collective-permute-start | bytes 3145736 | tf_op jit(solution)/shard_map/ppermute | solution.py:358
  123.2 32.5 %collective-permute-start.8 = (bf16[1024,256]{1,0:T(8,128)(2,1)}, bf16[1024,256]{1,0:T(8,128)(2,1)}, u32[]{:S(2)}, u32[]{:S(2)}) collective-permute-start(bf16[1024,256]{1,0:T(8,128)(2,1)} %get-tuple-element.31), channel_id=1, source_target_pairs={{0,14},{2,0},{4,2},{6,4},{8,6},{10,8},{12,10},{14,12},{1,15},{3,1}... | collective-permute-start | bytes 1572872 | tf_op jit(solution)/shard_map/ppermute | solution.py:358
  129.3 30.1 %collective-permute-start.4 = (bf16[1024,256]{1,0:T(8,128)(2,1)}, bf16[1024,256]{1,0:T(8,128)(2,1)}, u32[]{:S(2)}, u32[]{:S(2)}) collective-permute-start(bf16[1024,256]{1,0:T(8,128)(2,1)} %get-tuple-element.33), channel_id=1, source_target_pairs={{0,2},{2,4},{4,6},{6,8},{8,10},{10,12},{12,14},{14,0},{1,3},{3,5},... | collective-permute-start | bytes 1572872 | tf_op jit(solution)/shard_map/ppermute | solution.py:358
  139.4 30.6 %collective-permute-start.17 = (bf16[1024,256]{1,0:T(8,128)(2,1)}, bf16[1024,256]{1,0:T(8,128)(2,1)}, u32[]{:S(2)}, u32[]{:S(2)}) collective-permute-start(bf16[1024,256]{1,0:T(8,128)(2,1)} %after.5), channel_id=1, source_target_pairs={{0,14},{2,0},{4,2},{6,4},{8,6},{10,8},{12,10},{14,12},{1,15},{3,1}... | collective-permute-start | bytes 1572872 | tf_op jit(solution)/shard_map/ppermute | solution.py:358
  142.7 16.8 %copy-start.14 = (bf16[1,1,128,2048]{2,3,1,0:T(8,128)(2,1)S(1)}, bf16[1,1,128,2048]{2,3,1,0:T(8,128)(2,1)}, u32[]{:S(2)}) copy-start(bf16[1,1,128,2048]{2,3,1,0:T(8,128)(2,1)} %copy-done.13) | copy-start | bytes 1572868
  142.7 16.8 %copy-start.16 = (bf16[2048,128]{1,0:T(8,128)(2,1)S(1)}, bf16[2048,128]{1,0:T(8,128)(2,1)}, u32[]{:S(2)}) copy-start(bf16[2048,128]{1,0:T(8,128)(2,1)} %copy-done.15) | copy-start | bytes 1572868
  142.7 16.8 %copy-start.18 = (bf16[2048,128]{1,0:T(8,128)(2,1)S(1)}, bf16[2048,128]{1,0:T(8,128)(2,1)}, u32[]{:S(2)}) copy-start(bf16[2048,128]{1,0:T(8,128)(2,1)} %copy-done.17) | copy-start | bytes 1572868
  148.2 21.9 %collective-permute-start.16 = (bf16[1024,256]{1,0:T(8,128)(2,1)}, bf16[1024,256]{1,0:T(8,128)(2,1)S(1)}, u32[]{:S(2)}, u32[]{:S(2)}) collective-permute-start(bf16[1024,256]{1,0:T(8,128)(2,1)} %after.4), channel_id=1, source_target_pairs={{0,2},{2,4},{4,6},{6,8},{8,10},{10,12},{12,14},{14,0},{1,3},{3,5},... | collective-permute-start | bytes 1572872 | tf_op jit(solution)/shard_map/ppermute | solution.py:358
  162.7 20.5 %copy-start.27 = (bf16[128,2048]{1,0:T(8,128)(2,1)S(1)}, bf16[128,2048]{1,0:T(8,128)(2,1)}, u32[]{:S(2)}) copy-start(bf16[128,2048]{1,0:T(8,128)(2,1)} %copy-done.26) | copy-start | bytes 1572868
  162.7 27.9 %copy-start.7 = (bf16[2048,256]{1,0:T(8,128)(2,1)S(1)}, bf16[2048,256]{1,0:T(8,128)(2,1)}, u32[]{:S(2)}) copy-start(bf16[2048,256]{1,0:T(8,128)(2,1)} %copy-done.6) | copy-start | bytes 3145732
  162.7 27.9 %copy-start.10 = (bf16[2048,256]{1,0:T(8,128)(2,1)S(1)}, bf16[2048,256]{1,0:T(8,128)(2,1)}, u32[]{:S(2)}) copy-start(bf16[2048,256]{1,0:T(8,128)(2,1)} %copy-done.8) | copy-start | bytes 3145732
  162.7 27.9 %copy-start.23 = (bf16[2048,128]{1,0:T(8,128)(2,1)S(1)}, bf16[2048,128]{1,0:T(8,128)(2,1)}, u32[]{:S(2)}) copy-start(bf16[2048,128]{1,0:T(8,128)(2,1)} %copy-done.22) | copy-start | bytes 1572868
  162.7 27.9 %copy-start.25 = (bf16[128,2048]{1,0:T(8,128)(2,1)S(1)}, bf16[128,2048]{1,0:T(8,128)(2,1)}, u32[]{:S(2)}) copy-start(bf16[128,2048]{1,0:T(8,128)(2,1)} %copy-done.24) | copy-start | bytes 1572868
  162.7 9.6 %collective-permute-start.18 = (bf16[1024,128]{1,0:T(8,128)(2,1)S(1)}, bf16[1024,128]{1,0:T(8,128)(2,1)S(1)}, u32[]{:S(2)}, u32[]{:S(2)}) collective-permute-start(bf16[1024,128]{1,0:T(8,128)(2,1)S(1)} %get-tuple-element.20.lo_ref), channel_id=1, source_target_pairs={{16,1},{17,0},{32,17},{33,16},{48,33},{49,32},{64,49},{65,48},{80,... | collective-permute-start | bytes 786440 | tf_op jit(solution)/shard_map/ppermute | solution.py:411
  164.9 21.5 %collective-permute-start.15 = (bf16[1024,128]{1,0:T(8,128)(2,1)S(1)}, bf16[1024,128]{1,0:T(8,128)(2,1)S(1)}, u32[]{:S(2)}, u32[]{:S(2)}) collective-permute-start(bf16[1024,128]{1,0:T(8,128)(2,1)S(1)} %get-tuple-element.20.lo_ref), channel_id=1, source_target_pairs={{16,0},{32,16},{48,32},{64,48},{80,64},{96,80},{112,96},{128,112},... | collective-permute-start | bytes 786440 | tf_op jit(solution)/shard_map/ppermute | solution.py:412
  175.4 11.1 %collective-permute-start.19 = (bf16[1024,128]{1,0:T(8,128)(2,1)S(1)}, bf16[1024,128]{1,0:T(8,128)(2,1)S(1)}, u32[]{:S(2)}, u32[]{:S(2)}) collective-permute-start(bf16[1024,128]{1,0:T(8,128)(2,1)S(1)} %get-tuple-element.21.hi_ref), channel_id=1, source_target_pairs={{16,0},{32,16},{48,32},{64,48},{80,64},{96,80},{112,96},{128,112},... | collective-permute-start | bytes 786440 | tf_op jit(solution)/shard_map/ppermute | solution.py:417
  181.3 9.3 %collective-permute-start.20 = (bf16[1024,128]{1,0:T(8,128)(2,1)S(1)}, bf16[1024,128]{1,0:T(8,128)(2,1)S(1)}, u32[]{:S(2)}, u32[]{:S(2)}) collective-permute-start(bf16[1024,128]{1,0:T(8,128)(2,1)S(1)} %get-tuple-element.21.hi_ref), channel_id=1, source_target_pairs={{16,1},{17,0},{32,17},{33,16},{48,33},{49,32},{64,49},{65,48},{80,... | collective-permute-start | bytes 786440 | tf_op jit(solution)/shard_map/ppermute | solution.py:416
  200.8 12.2 %all-to-all-start = ((f32[8,16,128]{2,1,0:T(8,128)}), f32[8,16,128]{2,1,0:T(8,128)S(1)}, u32[]{:S(2)}, u32[]{:S(2)}) async-start(f32[8,16,128]{2,1,0:T(8,128)} %bitcast.19), calls=%async_computation | async-start | bytes 131072 | tf_op jit(solution)/shard_map/all_to_all | solution.py:425
  (21 other events, 126.2 us)
